TPU v7x, 256 devices: a whole 4x4x8 slice. The times are simulated.
256 devices in a mesh: layer: 8 (over y, core), front: 32 (over z, x).
Axes of the slice: x: 4, y: 4, z: 8, core: 2. Of those that a mesh axis runs over, the one named last changes fastest.
Arguments:
- sources_down: float32 [8, 32, 2, 32, 256], P('layer', 'front'), may hold values from -6 to 6
- sources_up: float32 [8, 32, 2, 32, 256], P('layer', 'front'), may hold values from -6 to 6
- leaf_inverse: float32 [8, 32, 2, 256, 256], P('layer', 'front'), may hold values from -0.25 to 0.25
- coupling: float32 [8, 32, 2, 512, 256], P('layer', 'front'), may hold values from -0.25 to 0.25
- sep_inverse: float32 [8, 32, 2, 256, 256], P('layer', 'front'), may hold values from -0.25 to 0.25
- inject_top: float32 [8, 32, 2, 128, 256], P('layer', 'front'), may hold values from -0.125 to 0.125
- inject_bottom: float32 [8, 32, 2, 128, 256], P('layer', 'front'), may hold values from -0.125 to 0.125
- targets: int32 [8, 32, 16, 1], P('layer', 'front'), may hold values from 0 to 31; in each aligned block of 16 rows (0 to 15, 16 to 31, ..., all dimensions but the last counted through in order) at most 2 rows name the same one
- offsets: int32 [8, 32, 16], P('layer', 'front'), may hold values from 0 to 7
Outputs:
- field_down: float32 [8, 32, 2, 32, 256], P('layer', 'front')
- field_up: float32 [8, 32, 2, 32, 256], P('layer', 'front')
Inputs may be any that keep to these rules, and one draw needn't show every extreme that they name: `targets`: the 16 blocks of one leaf name one separator at most 2 times, and in every draw some leaf names one separator exactly 2 times.
All inputs are finite; a program needn't handle non-finite values.
Results may differ from a plain program's by a relative error of at most 0.00019.
Values sent between devices are 32-bit elements; how exact they have to be, the bound alone decides.
No kernel may reach another device: no remote copies, remote signals or barrier semaphores. Data moves between devices by JAX's collectives and lax.ppermute only.
A program may use at most 64 MiB of HBM per device.

v0:
```python
import jax
import jax.numpy as jnp
from jax import lax
from jax.sharding import PartitionSpec as P

P_SIZE = 256
Q = 256
TR = 128
RB = 32
S = 32
NB = 16
QB = 8


precise = lax.Precision.HIGHEST


def passed_along(value, axis, steps):
    count = lax.axis_size(axis)
    initial, last = (max(0, -steps), min(count, count - steps))
    return lax.ppermute(value, axis, [(source, source + steps) for source in range(initial, last)])


def complex_product(pattern, first, second):
    real_part = jnp.einsum(pattern, first[0], second[0], precision=precise) - jnp.einsum(
        pattern, first[1], second[1], precision=precise
    )
    imag_part = jnp.einsum(pattern, first[0], second[1], precision=precise) + jnp.einsum(
        pattern, first[1], second[0], precision=precise
    )
    return (real_part, imag_part)


def block_ranks(target_list):
    count = target_list.shape[0]
    same = target_list[:, None] == target_list[None, :]
    earlier = jnp.arange(count)[None, :] < jnp.arange(count)[:, None]
    return jnp.sum(same & earlier, axis=1)


def to_rows(blocked, columns):
    return blocked.transpose(1, 0, 2).reshape(columns, Q)


def to_blocks(rows, columns):
    return rows.reshape(columns, QB, RB).transpose(1, 0, 2)


def front_solve(rhs, leaf_matrix, coupling_rows, sep_matrix, target_list, offset_list):
    leaves = lax.axis_size("front")
    capacity = max(2, (NB + leaves - 1) // leaves)
    columns = rhs.shape[1]
    breadth = columns * 2 * RB
    interior = complex_product("cq,pq->cp", rhs, leaf_matrix)
    coupling_blocks = coupling_rows.reshape(2, NB, RB, P_SIZE)
    update = complex_product("cp,nrp->ncr", interior, coupling_blocks)
    packed = jnp.concatenate(update, axis=2).reshape(NB, breadth)
    ranks = block_ranks(target_list)
    slot_owner = jnp.arange(leaves * capacity) // capacity
    slot_rank = jnp.arange(leaves * capacity) % capacity
    select = (target_list[None, :] == slot_owner[:, None]) & (ranks[None, :] == slot_rank[:, None])
    select_float = select.astype(jnp.float32)
    outgoing = jnp.dot(select_float, packed, precision=precise).reshape(
        leaves, capacity, columns, 2 * RB
    )
    filled = jnp.sum(select.astype(jnp.int32), axis=1)
    slot_offset = jnp.sum(jnp.where(select, offset_list[None, :], 0), axis=1) + QB * (1 - filled)
    slot_offset = slot_offset.reshape(leaves, capacity)
    arrived, arrived_offset = (
        lax.all_to_all(outgoing, "front", split_axis=0, concat_axis=0, tiled=True),
        lax.all_to_all(slot_offset, "front", split_axis=0, concat_axis=0, tiled=True),
    )
    placing = (arrived_offset.reshape(-1)[None, :] == jnp.arange(QB)[:, None]).astype(jnp.float32)
    assembled = jnp.dot(
        placing, arrived.reshape(leaves * capacity, breadth), precision=precise
    ).reshape(QB, columns, 2 * RB)
    sep_rhs = (to_rows(assembled[:, :, :RB], columns), to_rows(assembled[:, :, RB:], columns))
    solved = complex_product("cs,qs->cq", sep_rhs, sep_matrix)
    solved_packed = jnp.concatenate(
        [to_blocks(solved[0], columns), to_blocks(solved[1], columns)], axis=2
    ).reshape(QB, breadth)
    reply = jnp.einsum("qk,qx->kx", placing, solved_packed, precision=precise).reshape(
        leaves, capacity, columns, 2 * RB
    )
    returned = lax.all_to_all(reply, "front", split_axis=0, concat_axis=0, tiled=True)
    mine = jnp.einsum(
        "kn,kx->nx", select_float, returned.reshape(leaves * capacity, breadth), precision=precise
    ).reshape(NB, columns, 2 * RB)
    pushed = complex_product("ncr,nrp->cp", (mine[:, :, :RB], mine[:, :, RB:]), coupling_blocks)
    correction = complex_product("cq,pq->cp", pushed, leaf_matrix)
    return jnp.stack([interior[0] + correction[0], interior[1] + correction[1]])


def feed(sources, mapping, trace, piece_index, pieces, piece_width):
    start = jnp.clip(piece_index, 0, pieces - 1) * piece_width
    local = lax.dynamic_slice_in_dim(sources, start, piece_width, 1)
    injected = complex_product("ct,tp->cp", trace, mapping)
    return jnp.stack([local[0] + injected[0], local[1] + injected[1]])


def store(output, part, piece_index, pieces, piece_width):
    valid = (piece_index >= 0) & (piece_index < pieces)
    start = jnp.clip(piece_index, 0, pieces - 1) * piece_width
    current = lax.dynamic_slice_in_dim(output, start, piece_width, 1)
    return lax.dynamic_update_slice_in_dim(output, jnp.where(valid, part, current), start, 1)


def send_down(part):
    return passed_along(part[:, :, P_SIZE - TR :], "layer", 1)


def send_up(part):
    return passed_along(part[:, :, :TR], "layer", -1)


def body(
    sources_down,
    sources_up,
    leaf_inverse,
    coupling,
    sep_inverse,
    inject_top,
    inject_bottom,
    targets,
    offsets,
):
    depth = lax.axis_size("layer")
    depth_index = lax.axis_index("layer")
    leaf_matrix = leaf_inverse[0, 0]
    coupling_rows = coupling[0, 0]
    sep_matrix = sep_inverse[0, 0]
    top_map = inject_top[0, 0]
    bottom_map = inject_bottom[0, 0]
    down_sources = sources_down[0, 0]
    up_sources = sources_up[0, 0]
    target_list = targets[0, 0, :, 0]
    offset_list = offsets[0, 0]
    pieces = 2
    piece_width = S // pieces
    sections = pieces + depth - 1
    blank_trace = jnp.zeros((2, piece_width, TR), jnp.float32)
    blank_field = jnp.zeros((2, S, P_SIZE), jnp.float32)

    def solve_piece(rhs):
        return front_solve(rhs, leaf_matrix, coupling_rows, sep_matrix, target_list, offset_list)

    def joint_section(section, carry):
        out_down, out_up, trace_down, trace_up = carry
        piece_down = section - depth_index
        piece_up = section - (depth - 1 - depth_index)
        rhs = jnp.concatenate(
            [
                feed(down_sources, top_map, trace_down, piece_down, pieces, piece_width),
                feed(up_sources, bottom_map, trace_up, piece_up, pieces, piece_width),
            ],
            axis=1,
        )
        field = solve_piece(rhs)
        down_part = field[:, :piece_width]
        up_part = field[:, piece_width:]
        out_down = store(out_down, down_part, piece_down, pieces, piece_width)
        out_up = store(out_up, up_part, piece_up, pieces, piece_width)
        return (out_down, out_up, send_down(down_part), send_up(up_part))

    field_down, field_up, unused_down, unused_up = lax.fori_loop(
        0, sections, joint_section, (blank_field, blank_field, blank_trace, blank_trace)
    )
    return (field_down[None, None], field_up[None, None])


def solution(mesh):
    return jax.shard_map(
        body,
        mesh=mesh,
        in_specs=(
            P("layer", "front", None, None, None),
            P("layer", "front", None, None, None),
            P("layer", "front", None, None, None),
            P("layer", "front", None, None, None),
            P("layer", "front", None, None, None),
            P("layer", "front", None, None, None),
            P("layer", "front", None, None, None),
            P("layer", "front", None, None),
            P("layer", "front", None),
        ),
        out_specs=(P("layer", "front", None, None, None), P("layer", "front", None, None, None)),
        check_vma=False,
    )
```

profile of v0, /device:TPU:1, one launch (start us, length us, event | category | flops | bytes accessed | tf_op | source)
XLA Modules:
  0.0 857.1 jit_solution(15915154119581562666)
XLA Ops:
  1.5 855.0 %while.21 = (s32[]{:T(128)}, f32[2,32,256]{2,1,0:T(8,128)S(1)}, f32[2,32,256]{2,1,0:T(8,128)S(1)}, f32[2,16,128]{2,1,0:T(8,128)S(1)}, f32[2,16,128]{2,1,0:T(8,12...) while((s32[]{:T(128)}, f32[2,32,256]{2,1,0:T(8,128)S(1)}, ...), condition=%wide.region_4.5_spmd, body=%wide.region_0.4_spmd.sunk | while | flops 830776704 | bytes 44113776 | solution.py:165
  2.5 12.0 %all-to-all-start.1 = ((s32[32,1,2]{2,1,0:T(1,128)}), s32[32,1,2]{2,1,0:T(1,128)S(1)}, u32[]{:S(2)}, u32[]{:S(2)}) async-start(s32[32,1,2]{2,1,0:T(1,128)} %bitcast.384), calls=%async_computation.1 | async-start | bytes 32768 | tf_op jit(solution)/shard_map/while/body/eval_jaxpr/all_to_all | solution.py:71
  38.4 14.0 %all-to-all-done = f32[32,1,4096]{2,1,0:T(1,128)S(1)} async-done(((f32[32,1,4096]{2,1,0:T(1,128)}), f32[32,1,4096]{2,1,0:T(1,128)S(1)}, u32[]{:S(2)}, u32[]{:S(2)}) %all-to-all-start) | async-done | bytes 524320 | tf_op jit(solution)/shard_map/while/body/eval_jaxpr/all_to_all | solution.py:70
  69.2 15.0 %all-to-all-done.2 = f32[32,1,4096]{2,1,0:T(1,128)S(1)} async-done(((f32[32,1,4096]{2,1,0:T(1,128)}), f32[32,1,4096]{2,1,0:T(1,128)S(1)}, u32[]{:S(2)}, u32[]{:S(2)}) %all-to-all-start.2) | async-done | bytes 524320 | tf_op jit(solution)/shard_map/while/body/eval_jaxpr/all_to_all | solution.py:85
  123.4 9.2 %all-to-all-start = ((f32[32,1,4096]{2,1,0:T(1,128)}), f32[32,1,4096]{2,1,0:T(1,128)S(1)}, u32[]{:S(2)}, u32[]{:S(2)}) async-start(f32[32,1,4096]{2,1,0:T(1,128)} %reshape.305), calls=%async_computation | async-start | bytes 1048576 | tf_op jit(solution)/shard_map/while/body/eval_jaxpr/all_to_all | solution.py:70
  134.1 16.0 %all-to-all-done = f32[32,1,4096]{2,1,0:T(1,128)S(1)} async-done(((f32[32,1,4096]{2,1,0:T(1,128)}), f32[32,1,4096]{2,1,0:T(1,128)S(1)}, u32[]{:S(2)}, u32[]{:S(2)}) %all-to-all-start) | async-done | bytes 524320 | tf_op jit(solution)/shard_map/while/body/eval_jaxpr/all_to_all | solution.py:70
  165.1 16.7 %all-to-all-done.2 = f32[32,1,4096]{2,1,0:T(1,128)S(1)} async-done(((f32[32,1,4096]{2,1,0:T(1,128)}), f32[32,1,4096]{2,1,0:T(1,128)S(1)}, u32[]{:S(2)}, u32[]{:S(2)}) %all-to-all-start.2) | async-done | bytes 524320 | tf_op jit(solution)/shard_map/while/body/eval_jaxpr/all_to_all | solution.py:85
  219.8 9.2 %all-to-all-start = ((f32[32,1,4096]{2,1,0:T(1,128)}), f32[32,1,4096]{2,1,0:T(1,128)S(1)}, u32[]{:S(2)}, u32[]{:S(2)}) async-start(f32[32,1,4096]{2,1,0:T(1,128)} %reshape.305), calls=%async_computation | async-start | bytes 1048576 | tf_op jit(solution)/shard_map/while/body/eval_jaxpr/all_to_all | solution.py:70
  230.4 16.0 %all-to-all-done = f32[32,1,4096]{2,1,0:T(1,128)S(1)} async-done(((f32[32,1,4096]{2,1,0:T(1,128)}), f32[32,1,4096]{2,1,0:T(1,128)S(1)}, u32[]{:S(2)}, u32[]{:S(2)}) %all-to-all-start) | async-done | bytes 524320 | tf_op jit(solution)/shard_map/while/body/eval_jaxpr/all_to_all | solution.py:70
  261.4 16.7 %all-to-all-done.2 = f32[32,1,4096]{2,1,0:T(1,128)S(1)} async-done(((f32[32,1,4096]{2,1,0:T(1,128)}), f32[32,1,4096]{2,1,0:T(1,128)S(1)}, u32[]{:S(2)}, u32[]{:S(2)}) %all-to-all-start.2) | async-done | bytes 524320 | tf_op jit(solution)/shard_map/while/body/eval_jaxpr/all_to_all | solution.py:85
  315.1 9.2 %all-to-all-start = ((f32[32,1,4096]{2,1,0:T(1,128)}), f32[32,1,4096]{2,1,0:T(1,128)S(1)}, u32[]{:S(2)}, u32[]{:S(2)}) async-start(f32[32,1,4096]{2,1,0:T(1,128)} %reshape.305), calls=%async_computation | async-start | bytes 1048576 | tf_op jit(solution)/shard_map/while/body/eval_jaxpr/all_to_all | solution.py:70
  325.7 16.0 %all-to-all-done = f32[32,1,4096]{2,1,0:T(1,128)S(1)} async-done(((f32[32,1,4096]{2,1,0:T(1,128)}), f32[32,1,4096]{2,1,0:T(1,128)S(1)}, u32[]{:S(2)}, u32[]{:S(2)}) %all-to-all-start) | async-done | bytes 524320 | tf_op jit(solution)/shard_map/while/body/eval_jaxpr/all_to_all | solution.py:70
  356.7 16.7 %all-to-all-done.2 = f32[32,1,4096]{2,1,0:T(1,128)S(1)} async-done(((f32[32,1,4096]{2,1,0:T(1,128)}), f32[32,1,4096]{2,1,0:T(1,128)S(1)}, u32[]{:S(2)}, u32[]{:S(2)}) %all-to-all-start.2) | async-done | bytes 524320 | tf_op jit(solution)/shard_map/while/body/eval_jaxpr/all_to_all | solution.py:85
  408.5 9.2 %all-to-all-start = ((f32[32,1,4096]{2,1,0:T(1,128)}), f32[32,1,4096]{2,1,0:T(1,128)S(1)}, u32[]{:S(2)}, u32[]{:S(2)}) async-start(f32[32,1,4096]{2,1,0:T(1,128)} %reshape.305), calls=%async_computation | async-start | bytes 1048576 | tf_op jit(solution)/shard_map/while/body/eval_jaxpr/all_to_all | solution.py:70
  419.2 16.3 %all-to-all-done = f32[32,1,4096]{2,1,0:T(1,128)S(1)} async-done(((f32[32,1,4096]{2,1,0:T(1,128)}), f32[32,1,4096]{2,1,0:T(1,128)S(1)}, u32[]{:S(2)}, u32[]{:S(2)}) %all-to-all-start) | async-done | bytes 524320 | tf_op jit(solution)/shard_map/while/body/eval_jaxpr/all_to_all | solution.py:70
  450.8 15.8 %all-to-all-done.2 = f32[32,1,4096]{2,1,0:T(1,128)S(1)} async-done(((f32[32,1,4096]{2,1,0:T(1,128)}), f32[32,1,4096]{2,1,0:T(1,128)S(1)}, u32[]{:S(2)}, u32[]{:S(2)}) %all-to-all-start.2) | async-done | bytes 524320 | tf_op jit(solution)/shard_map/while/body/eval_jaxpr/all_to_all | solution.py:85
  512.9 16.0 %all-to-all-done = f32[32,1,4096]{2,1,0:T(1,128)S(1)} async-done(((f32[32,1,4096]{2,1,0:T(1,128)}), f32[32,1,4096]{2,1,0:T(1,128)S(1)}, u32[]{:S(2)}, u32[]{:S(2)}) %all-to-all-start) | async-done | bytes 524320 | tf_op jit(solution)/shard_map/while/body/eval_jaxpr/all_to_all | solution.py:70
  544.3 15.4 %all-to-all-done.2 = f32[32,1,4096]{2,1,0:T(1,128)S(1)} async-done(((f32[32,1,4096]{2,1,0:T(1,128)}), f32[32,1,4096]{2,1,0:T(1,128)S(1)}, u32[]{:S(2)}, u32[]{:S(2)}) %all-to-all-start.2) | async-done | bytes 524320 | tf_op jit(solution)/shard_map/while/body/eval_jaxpr/all_to_all | solution.py:85
  606.5 16.0 %all-to-all-done = f32[32,1,4096]{2,1,0:T(1,128)S(1)} async-done(((f32[32,1,4096]{2,1,0:T(1,128)}), f32[32,1,4096]{2,1,0:T(1,128)S(1)}, u32[]{:S(2)}, u32[]{:S(2)}) %all-to-all-start) | async-done | bytes 524320 | tf_op jit(solution)/shard_map/while/body/eval_jaxpr/all_to_all | solution.py:70
  637.9 15.4 %all-to-all-done.2 = f32[32,1,4096]{2,1,0:T(1,128)S(1)} async-done(((f32[32,1,4096]{2,1,0:T(1,128)}), f32[32,1,4096]{2,1,0:T(1,128)S(1)}, u32[]{:S(2)}, u32[]{:S(2)}) %all-to-all-start.2) | async-done | bytes 524320 | tf_op jit(solution)/shard_map/while/body/eval_jaxpr/all_to_all | solution.py:85
  700.0 16.0 %all-to-all-done = f32[32,1,4096]{2,1,0:T(1,128)S(1)} async-done(((f32[32,1,4096]{2,1,0:T(1,128)}), f32[32,1,4096]{2,1,0:T(1,128)S(1)}, u32[]{:S(2)}, u32[]{:S(2)}) %all-to-all-start) | async-done | bytes 524320 | tf_op jit(solution)/shard_map/while/body/eval_jaxpr/all_to_all | solution.py:70
  731.5 15.4 %all-to-all-done.2 = f32[32,1,4096]{2,1,0:T(1,128)S(1)} async-done(((f32[32,1,4096]{2,1,0:T(1,128)}), f32[32,1,4096]{2,1,0:T(1,128)S(1)}, u32[]{:S(2)}, u32[]{:S(2)}) %all-to-all-start.2) | async-done | bytes 524320 | tf_op jit(solution)/shard_map/while/body/eval_jaxpr/all_to_all | solution.py:85
  793.6 16.0 %all-to-all-done = f32[32,1,4096]{2,1,0:T(1,128)S(1)} async-done(((f32[32,1,4096]{2,1,0:T(1,128)}), f32[32,1,4096]{2,1,0:T(1,128)S(1)}, u32[]{:S(2)}, u32[]{:S(2)}) %all-to-all-start) | async-done | bytes 524320 | tf_op jit(solution)/shard_map/while/body/eval_jaxpr/all_to_all | solution.py:70
  825.0 15.4 %all-to-all-done.2 = f32[32,1,4096]{2,1,0:T(1,128)S(1)} async-done(((f32[32,1,4096]{2,1,0:T(1,128)}), f32[32,1,4096]{2,1,0:T(1,128)S(1)}, u32[]{:S(2)}, u32[]{:S(2)}) %all-to-all-start.2) | async-done | bytes 524320 | tf_op jit(solution)/shard_map/while/body/eval_jaxpr/all_to_all | solution.py:85
  (839 shorter events, 517.6 us)
Async XLA Ops:
  2.5 25.3 %all-to-all-start.1 = ((s32[32,1,2]{2,1,0:T(1,128)}), s32[32,1,2]{2,1,0:T(1,128)S(1)}, u32[]{:S(2)}, u32[]{:S(2)}) async-start(s32[32,1,2]{2,1,0:T(1,128)} %bitcast.384), calls=%async_computation.1 | async-start | bytes 32768 | tf_op jit(solution)/shard_map/while/body/eval_jaxpr/all_to_all | solution.py:71
  27.8 24.6 %all-to-all-start = ((f32[32,1,4096]{2,1,0:T(1,128)}), f32[32,1,4096]{2,1,0:T(1,128)S(1)}, u32[]{:S(2)}, u32[]{:S(2)}) async-start(f32[32,1,4096]{2,1,0:T(1,128)} %reshape.305), calls=%async_computation | async-start | bytes 1048576 | tf_op jit(solution)/shard_map/while/body/eval_jaxpr/all_to_all | solution.py:70
  63.1 21.1 %all-to-all-start.2 = ((f32[32,1,4096]{2,1,0:T(1,128)}), f32[32,1,4096]{2,1,0:T(1,128)S(1)}, u32[]{:S(2)}, u32[]{:S(2)}) async-start(f32[32,1,4096]{2,1,0:T(1,128)} %reshape.313), calls=%async_computation.2 | async-start | bytes 1048576 | tf_op jit(solution)/shard_map/while/body/eval_jaxpr/all_to_all | solution.py:85
  123.4 26.6 %all-to-all-start = ((f32[32,1,4096]{2,1,0:T(1,128)}), f32[32,1,4096]{2,1,0:T(1,128)S(1)}, u32[]{:S(2)}, u32[]{:S(2)}) async-start(f32[32,1,4096]{2,1,0:T(1,128)} %reshape.305), calls=%async_computation | async-start | bytes 1048576 | tf_op jit(solution)/shard_map/while/body/eval_jaxpr/all_to_all | solution.py:70
  160.7 21.1 %all-to-all-start.2 = ((f32[32,1,4096]{2,1,0:T(1,128)}), f32[32,1,4096]{2,1,0:T(1,128)S(1)}, u32[]{:S(2)}, u32[]{:S(2)}) async-start(f32[32,1,4096]{2,1,0:T(1,128)} %reshape.313), calls=%async_computation.2 | async-start | bytes 1048576 | tf_op jit(solution)/shard_map/while/body/eval_jaxpr/all_to_all | solution.py:85
  219.8 26.6 %all-to-all-start = ((f32[32,1,4096]{2,1,0:T(1,128)}), f32[32,1,4096]{2,1,0:T(1,128)S(1)}, u32[]{:S(2)}, u32[]{:S(2)}) async-start(f32[32,1,4096]{2,1,0:T(1,128)} %reshape.305), calls=%async_computation | async-start | bytes 1048576 | tf_op jit(solution)/shard_map/while/body/eval_jaxpr/all_to_all | solution.py:70
  257.1 21.1 %all-to-all-start.2 = ((f32[32,1,4096]{2,1,0:T(1,128)}), f32[32,1,4096]{2,1,0:T(1,128)S(1)}, u32[]{:S(2)}, u32[]{:S(2)}) async-start(f32[32,1,4096]{2,1,0:T(1,128)} %reshape.313), calls=%async_computation.2 | async-start | bytes 1048576 | tf_op jit(solution)/shard_map/while/body/eval_jaxpr/all_to_all | solution.py:85
  315.1 26.6 %all-to-all-start = ((f32[32,1,4096]{2,1,0:T(1,128)}), f32[32,1,4096]{2,1,0:T(1,128)S(1)}, u32[]{:S(2)}, u32[]{:S(2)}) async-start(f32[32,1,4096]{2,1,0:T(1,128)} %reshape.305), calls=%async_computation | async-start | bytes 1048576 | tf_op jit(solution)/shard_map/while/body/eval_jaxpr/all_to_all | solution.py:70
  352.4 21.1 %all-to-all-start.2 = ((f32[32,1,4096]{2,1,0:T(1,128)}), f32[32,1,4096]{2,1,0:T(1,128)S(1)}, u32[]{:S(2)}, u32[]{:S(2)}) async-start(f32[32,1,4096]{2,1,0:T(1,128)} %reshape.313), calls=%async_computation.2 | async-start | bytes 1048576 | tf_op jit(solution)/shard_map/while/body/eval_jaxpr/all_to_all | solution.py:85
  390.1 18.4 %all-to-all-start.1 = ((s32[32,1,2]{2,1,0:T(1,128)}), s32[32,1,2]{2,1,0:T(1,128)S(1)}, u32[]{:S(2)}, u32[]{:S(2)}) async-start(s32[32,1,2]{2,1,0:T(1,128)} %bitcast.384), calls=%async_computation.1 | async-start | bytes 32768 | tf_op jit(solution)/shard_map/while/body/eval_jaxpr/all_to_all | solution.py:71
  408.5 26.9 %all-to-all-start = ((f32[32,1,4096]{2,1,0:T(1,128)}), f32[32,1,4096]{2,1,0:T(1,128)S(1)}, u32[]{:S(2)}, u32[]{:S(2)}) async-start(f32[32,1,4096]{2,1,0:T(1,128)} %reshape.305), calls=%async_computation | async-start | bytes 1048576 | tf_op jit(solution)/shard_map/while/body/eval_jaxpr/all_to_all | solution.py:70
  446.1 20.5 %all-to-all-start.2 = ((f32[32,1,4096]{2,1,0:T(1,128)}), f32[32,1,4096]{2,1,0:T(1,128)S(1)}, u32[]{:S(2)}, u32[]{:S(2)}) async-start(f32[32,1,4096]{2,1,0:T(1,128)} %reshape.313), calls=%async_computation.2 | async-start | bytes 1048576 | tf_op jit(solution)/shard_map/while/body/eval_jaxpr/all_to_all | solution.py:85
  483.3 19.0 %all-to-all-start.1 = ((s32[32,1,2]{2,1,0:T(1,128)}), s32[32,1,2]{2,1,0:T(1,128)S(1)}, u32[]{:S(2)}, u32[]{:S(2)}) async-start(s32[32,1,2]{2,1,0:T(1,128)} %bitcast.384), calls=%async_computation.1 | async-start | bytes 32768 | tf_op jit(solution)/shard_map/while/body/eval_jaxpr/all_to_all | solution.py:71
  502.3 26.6 %all-to-all-start = ((f32[32,1,4096]{2,1,0:T(1,128)}), f32[32,1,4096]{2,1,0:T(1,128)S(1)}, u32[]{:S(2)}, u32[]{:S(2)}) async-start(f32[32,1,4096]{2,1,0:T(1,128)} %reshape.305), calls=%async_computation | async-start | bytes 1048576 | tf_op jit(solution)/shard_map/while/body/eval_jaxpr/all_to_all | solution.py:70
  539.5 20.2 %all-to-all-start.2 = ((f32[32,1,4096]{2,1,0:T(1,128)}), f32[32,1,4096]{2,1,0:T(1,128)S(1)}, u32[]{:S(2)}, u32[]{:S(2)}) async-start(f32[32,1,4096]{2,1,0:T(1,128)} %reshape.313), calls=%async_computation.2 | async-start | bytes 1048576 | tf_op jit(solution)/shard_map/while/body/eval_jaxpr/all_to_all | solution.py:85
  576.8 19.1 %all-to-all-start.1 = ((s32[32,1,2]{2,1,0:T(1,128)}), s32[32,1,2]{2,1,0:T(1,128)S(1)}, u32[]{:S(2)}, u32[]{:S(2)}) async-start(s32[32,1,2]{2,1,0:T(1,128)} %bitcast.384), calls=%async_computation.1 | async-start | bytes 32768 | tf_op jit(solution)/shard_map/while/body/eval_jaxpr/all_to_all | solution.py:71
  595.9 26.6 %all-to-all-start = ((f32[32,1,4096]{2,1,0:T(1,128)}), f32[32,1,4096]{2,1,0:T(1,128)S(1)}, u32[]{:S(2)}, u32[]{:S(2)}) async-start(f32[32,1,4096]{2,1,0:T(1,128)} %reshape.305), calls=%async_computation | async-start | bytes 1048576 | tf_op jit(solution)/shard_map/while/body/eval_jaxpr/all_to_all | solution.py:70
  633.1 20.2 %all-to-all-start.2 = ((f32[32,1,4096]{2,1,0:T(1,128)}), f32[32,1,4096]{2,1,0:T(1,128)S(1)}, u32[]{:S(2)}, u32[]{:S(2)}) async-start(f32[32,1,4096]{2,1,0:T(1,128)} %reshape.313), calls=%async_computation.2 | async-start | bytes 1048576 | tf_op jit(solution)/shard_map/while/body/eval_jaxpr/all_to_all | solution.py:85
  670.4 19.1 %all-to-all-start.1 = ((s32[32,1,2]{2,1,0:T(1,128)}), s32[32,1,2]{2,1,0:T(1,128)S(1)}, u32[]{:S(2)}, u32[]{:S(2)}) async-start(s32[32,1,2]{2,1,0:T(1,128)} %bitcast.384), calls=%async_computation.1 | async-start | bytes 32768 | tf_op jit(solution)/shard_map/while/body/eval_jaxpr/all_to_all | solution.py:71
  689.4 26.6 %all-to-all-start = ((f32[32,1,4096]{2,1,0:T(1,128)}), f32[32,1,4096]{2,1,0:T(1,128)S(1)}, u32[]{:S(2)}, u32[]{:S(2)}) async-start(f32[32,1,4096]{2,1,0:T(1,128)} %reshape.305), calls=%async_computation | async-start | bytes 1048576 | tf_op jit(solution)/shard_map/while/body/eval_jaxpr/all_to_all | solution.py:70
  726.7 20.2 %all-to-all-start.2 = ((f32[32,1,4096]{2,1,0:T(1,128)}), f32[32,1,4096]{2,1,0:T(1,128)S(1)}, u32[]{:S(2)}, u32[]{:S(2)}) async-start(f32[32,1,4096]{2,1,0:T(1,128)} %reshape.313), calls=%async_computation.2 | async-start | bytes 1048576 | tf_op jit(solution)/shard_map/while/body/eval_jaxpr/all_to_all | solution.py:85
  763.9 19.1 %all-to-all-start.1 = ((s32[32,1,2]{2,1,0:T(1,128)}), s32[32,1,2]{2,1,0:T(1,128)S(1)}, u32[]{:S(2)}, u32[]{:S(2)}) async-start(s32[32,1,2]{2,1,0:T(1,128)} %bitcast.384), calls=%async_computation.1 | async-start | bytes 32768 | tf_op jit(solution)/shard_map/while/body/eval_jaxpr/all_to_all | solution.py:71
  783.0 26.6 %all-to-all-start = ((f32[32,1,4096]{2,1,0:T(1,128)}), f32[32,1,4096]{2,1,0:T(1,128)S(1)}, u32[]{:S(2)}, u32[]{:S(2)}) async-start(f32[32,1,4096]{2,1,0:T(1,128)} %reshape.305), calls=%async_computation | async-start | bytes 1048576 | tf_op jit(solution)/shard_map/while/body/eval_jaxpr/all_to_all | solution.py:70
  820.2 20.2 %all-to-all-start.2 = ((f32[32,1,4096]{2,1,0:T(1,128)}), f32[32,1,4096]{2,1,0:T(1,128)S(1)}, u32[]{:S(2)}, u32[]{:S(2)}) async-start(f32[32,1,4096]{2,1,0:T(1,128)} %reshape.313), calls=%async_computation.2 | async-start | bytes 1048576 | tf_op jit(solution)/shard_map/while/body/eval_jaxpr/all_to_all | solution.py:85
  (72 other events, 350.5 us)
where the time goes:
time: 861 us; the launch traced here: 857 us
  waiting for transfers between devices  300 us (35%)
  starting transfers between devices  239 us (28%)
  matrix products  167 us (19%)
  local copies, waits for them, and re-layouts  99.1 us (12%)
  other arithmetic  45.3 us (5%)
    all_to_all x9, waiting for transfers between devices, front_solve(): lax.all_to_all(reply, 'front', split_axis=0, concat_axis=0, tiled=True)  143 us
    all_to_all x9, waiting for transfers between devices, front_solve(): lax.all_to_all(outgoing, 'front', split_axis=0, concat_axis=0, tiled=True)  142 us
    all_to_all x9, starting transfers between devices, front_solve(): lax.all_to_all(outgoing, 'front', split_axis=0, concat_axis=0, tiled=True)  82.9 us
    ppermute x18, starting transfers between devices, passed_along(): lax.ppermute(value, axis, [(source, source + steps) for source in range(i...  60.1 us
    all_to_all x9, starting transfers between devices, front_solve(): lax.all_to_all(slot_offset, 'front', split_axis=0, concat_axis=0, tiled=T...  53.5 us
    dot_general x63, matrix products, complex_product(): jnp.einsum(pattern, first[0], second[1], precision=precise)  45 us
    all_to_all x9, starting transfers between devices, front_solve(): lax.all_to_all(reply, 'front', split_axis=0, concat_axis=0, tiled=True)  42.9 us
    while x126, local copies, waits for them, and re-layouts  42.2 us
  transfers between devices with their start and end apart: 45, of which 27 were waited for; matrix products, arithmetic and copies ran while one was open for 15% of the time, Pallas kernels for 0%

commit v1 on v0

v1 whole, which is shorter than its diff:
```python
import functools

import jax
import jax.numpy as jnp
from jax import lax
from jax.experimental import pallas as pl
from jax.experimental.pallas import tpu as pltpu
from jax.sharding import PartitionSpec as P


P_SIZE = 256
Q = 256
TR = 128
RB = 32
S = 32
NB = 16
QB = 8
CAP = 2
HALF = 16
GROUP = 32
LANES = 128

f32 = jnp.float32
bf16 = jnp.bfloat16
VMEM_LIMIT = 48 * 1024 * 1024
smem = pl.BlockSpec(memory_space=pltpu.SMEM)
vmem = pl.BlockSpec(memory_space=pltpu.VMEM)
hbm = pl.BlockSpec(memory_space=pl.ANY)
NN = (((1,), (0,)), ((), ()))
NT = (((1,), (1,)), ((), ()))


def halves(value):
    high = value.astype(bf16)
    return high, (value - high.astype(f32)).astype(bf16)


def dot(first, second, dims=NN):
    return lax.dot_general(first, second, dims, preferred_element_type=f32)


def product(first, second, dims=NN):
    first_high, first_low = halves(first)
    second_high, second_low = halves(second)
    return (
        dot(first_high, second_high, dims)
        + dot(first_high, second_low, dims)
        + dot(first_low, second_high, dims)
    )


def narrow_product(first, second):
    first_high, first_low = halves(first)
    second_high, second_low = halves(second)
    both = dot(first_high, jnp.concatenate([second_high, second_low], axis=1))
    return both[:, :LANES] + both[:, LANES:] + dot(first_low, second_high)


def complex_pair(first, second, dims=NN):
    real = product(first[0], second[0], dims) - product(first[1], second[1], dims)
    imag = product(first[0], second[1], dims) + product(first[1], second[0], dims)
    return real, imag


def lane_ids(rows):
    return lax.broadcasted_iota(jnp.int32, (rows, LANES), 1)


def turned(value):
    lanes = lane_ids(value.shape[0])
    ahead = pltpu.roll(value, LANES - HALF, 1)
    behind = pltpu.roll(value, HALF, 1)
    return jnp.where(lanes % GROUP < HALF, -ahead, behind)


def pick(group, choices):
    return jnp.where(
        group == 0,
        choices[0],
        jnp.where(group == 1, choices[1], jnp.where(group == 2, choices[2], choices[3])),
    )


def rotations(value):
    return [value] + [pltpu.roll(value, GROUP * turn, 1) for turn in (1, 2, 3)]


def spread_group(rolled, group, source):
    return pick(group, [rolled[(place - source) % 4] for place in range(4)])


def unpack(packed):
    count = packed.shape[0]
    flat = packed.reshape(count * 8, LANES)
    group = lane_ids(count * 8) // GROUP
    rolled = rotations(flat)
    parts = [spread_group(rolled, group, k).reshape(count, 8, LANES) for k in range(4)]
    return jnp.stack(parts, axis=1).reshape(count * RB, LANES)


def unpack_both(packed):
    count = packed.shape[0]
    flat = packed.reshape(count * 8, LANES)
    return unpack(packed), unpack(turned(flat).reshape(count, 8, LANES))


def pack(spread):
    count = spread.shape[0] // RB
    parts = spread.reshape(count, 4, 8, LANES)
    group = lax.broadcasted_iota(jnp.int32, (count, 8, LANES), 2) // GROUP
    return pick(group, [parts[:, k] for k in range(4)])


def slots_kernel(targets_ref, offsets_ref, slots_ref, slot_offsets_ref, used_ref):
    leaves = slot_offsets_ref.shape[0] // CAP
    for leaf in range(leaves):
        used_ref[leaf] = 0
    for slot in range(leaves * CAP):
        slot_offsets_ref[slot] = QB
    for block in range(NB):
        target = targets_ref[block]
        rank = used_ref[target]
        used_ref[target] = rank + 1
        slot = target * CAP + rank
        slots_ref[block] = slot
        slot_offsets_ref[slot] = offsets_ref[block]


def source_kernel(
    place_ref, down_ref, up_ref, leaf_ref, coupling_ref, own_u_ref, other_u_ref, own_y_ref, other_y_ref
):
    core = place_ref[0] % 2
    own_row = pl.multiple_of(core * HALF, HALF)
    other_row = pl.multiple_of((1 - core) * HALF, HALF)
    rows, turned_rows = [], []
    for source in (down_ref, up_ref):
        for start in (own_row, other_row):
            real = source[0, pl.ds(start, HALF), :]
            imag = source[1, pl.ds(start, HALF), :]
            rows += [real, imag]
            turned_rows += [-imag, real]
    y = product(leaf_ref[0], jnp.concatenate(rows, axis=0), NT) + product(
        leaf_ref[1], jnp.concatenate(turned_rows, axis=0), NT
    )
    u = narrow_product(coupling_ref[0], y) + narrow_product(coupling_ref[1], turned(y))
    rolled = rotations(y)
    y_group = lane_ids(P_SIZE) // GROUP
    parts = u.reshape(NB, 4, 8, LANES)
    u_group = lane_ids(NB * 8) // GROUP
    for sweep in range(2):
        for side, (u_ref, y_ref) in enumerate(((own_u_ref, own_y_ref), (other_u_ref, other_y_ref))):
            source = 2 * sweep + side
            y_ref[sweep] = spread_group(rolled, y_group, source)
            choices = []
            for k in range(4):
                part = parts[:, k].reshape(NB * 8, LANES)
                turn = (k - source) % 4
                choices.append(pltpu.roll(part, GROUP * turn, 1) if turn else part)
            u_ref[sweep] = pick(u_group, choices).reshape(NB, 8, LANES)


def operator_kernel(leaf_ref, coupling_ref, top_ref, bottom_ref, forward_ref, back_ref):
    leaf = (leaf_ref[0], leaf_ref[1])
    coupling = (coupling_ref[0], coupling_ref[1])
    inject = tuple(
        jnp.concatenate([top_ref[part], bottom_ref[part]], axis=0) for part in range(2)
    )
    local = complex_pair(leaf, inject, NT)
    update = complex_pair(coupling, local)
    for sweep in range(2):
        for part in range(2):
            columns = slice(sweep * TR, sweep * TR + TR)
            place = slice(part * TR, part * TR + TR)
            forward_ref[sweep, : NB * RB, place] = update[part][:, columns]
            forward_ref[sweep, NB * RB :, place] = local[part][:, columns]
    back = complex_pair(leaf, coupling, NT)
    back_ref[0] = back[0]
    back_ref[1] = back[1]


def stage_place(place_ref, stage):
    row = place_ref[0] // 2
    core = place_ref[0] % 2
    sweep = jnp.where(row == stage, 0, 1)
    first = jnp.where(sweep == core, 0, 1)
    return sweep, first


def start_either(choice, first_ref, second_ref, target_ref, semaphore):
    @pl.when(choice == 0)
    def _():
        pltpu.make_async_copy(first_ref, target_ref, semaphore).start()

    @pl.when(choice != 0)
    def _():
        pltpu.make_async_copy(second_ref, target_ref, semaphore).start()


def wait_for(source_ref, target_ref, semaphore):
    pltpu.make_async_copy(source_ref, target_ref, semaphore).wait()


def send_blocks(choice, own_slots_ref, other_slots_ref, packed, send_ref):
    for block in range(NB):
        slot = jnp.where(choice == 0, own_slots_ref[block], other_slots_ref[block])
        send_ref[slot] = packed[block]


def first_kernel(place_ref, own_slots_ref, other_slots_ref, own_u_ref, other_u_ref, send_ref):
    sweep, first = stage_place(place_ref, 0)
    packed = jnp.where(first == 0, own_u_ref[sweep], other_u_ref[sweep])
    send_blocks(first, own_slots_ref, other_slots_ref, packed, send_ref)


def separator_kernel(
    stage,
    step,
    place_ref,
    own_offsets_ref,
    other_offsets_ref,
    arrived_ref,
    own_sep_ref,
    other_sep_ref,
    reply_ref,
    sep_ref,
    even_ref,
    odd_ref,
    solved_ref,
    semaphore,
):
    sweep, first = stage_place(place_ref, stage)
    choice = first if step == 0 else 1 - first
    start_either(choice, own_sep_ref, other_sep_ref, sep_ref, semaphore)
    slots = arrived_ref.shape[0]
    even_ref[...] = jnp.zeros_like(even_ref)
    odd_ref[...] = jnp.zeros_like(odd_ref)
    places = []
    for slot in range(slots):
        place = jnp.where(choice == 0, own_offsets_ref[slot], other_offsets_ref[slot])
        places.append(place)
        total_ref = odd_ref if slot % 2 else even_ref
        total_ref[place] = total_ref[place] + arrived_ref[slot]
    rhs, rhs_turned = unpack_both(even_ref[:QB] + odd_ref[:QB])
    wait_for(own_sep_ref, sep_ref, semaphore)
    solved = narrow_product(sep_ref[0], rhs) + narrow_product(sep_ref[1], rhs_turned)
    solved_ref[:QB] = pack(solved)
    solved_ref[QB] = jnp.zeros((8, LANES), f32)
    for slot in range(slots):
        reply_ref[slot] = solved_ref[places[slot]]


def leaf_finish(choice, own_slots_ref, other_slots_ref, returned_ref, back_ref, wait, base):
    blocks = []
    for block in range(NB):
        slot = jnp.where(choice == 0, own_slots_ref[block], other_slots_ref[block])
        blocks.append(returned_ref[slot])
    mine, mine_turned = unpack_both(jnp.stack(blocks, axis=0))
    wait()
    return base + narrow_product(back_ref[0], mine) + narrow_product(back_ref[1], mine_turned)


def leaf_begin(sweep, choice, trace, trace_turned, forward, u_refs, y_refs, slots_refs, send_ref, base_ref):
    driven = narrow_product(forward, jnp.concatenate([trace, trace_turned], axis=0))
    packed = pack(driven[: NB * RB]) + jnp.where(choice == 0, u_refs[0][sweep], u_refs[1][sweep])
    send_blocks(choice, slots_refs[0], slots_refs[1], packed, send_ref)
    base_ref[...] = driven[NB * RB :] + jnp.where(choice == 0, y_refs[0][sweep], y_refs[1][sweep])


def middle_kernel(
    stage,
    place_ref,
    own_slots_ref,
    other_slots_ref,
    returned_ref,
    base_refs,
    own_u_ref,
    other_u_ref,
    own_y_ref,
    other_y_ref,
    own_back_ref,
    other_back_ref,
    own_forward_ref,
    other_forward_ref,
    field_ref,
    send_ref,
    next_base_ref,
    back_ref,
    forward_ref,
    semaphores,
):
    sweep, first = stage_place(place_ref, stage)
    second = 1 - first
    start_either(first, own_back_ref, other_back_ref, back_ref, semaphores.at[0])
    start_either(
        second, own_forward_ref.at[sweep], other_forward_ref.at[sweep], forward_ref, semaphores.at[1]
    )
    if len(base_refs) == 1:
        base = base_refs[0][...]
    else:
        base = jnp.where(first == 0, own_y_ref[sweep], other_y_ref[sweep])
    field_ref[...] = leaf_finish(
        first,
        own_slots_ref,
        other_slots_ref,
        returned_ref,
        back_ref,
        lambda: wait_for(own_back_ref, back_ref, semaphores.at[0]),
        base,
    )
    trace = field_ref[pl.ds(pl.multiple_of((1 - sweep) * TR, TR), TR), :]
    wait_for(own_forward_ref.at[0], forward_ref, semaphores.at[1])
    leaf_begin(
        sweep,
        second,
        trace,
        turned(trace),
        forward_ref[...],
        (own_u_ref, other_u_ref),
        (own_y_ref, other_y_ref),
        (own_slots_ref, other_slots_ref),
        send_ref,
        next_base_ref,
    )


def last_kernel(
    stage,
    place_ref,
    own_slots_ref,
    other_slots_ref,
    returned_ref,
    base_ref,
    own_back_ref,
    other_back_ref,
    field_ref,
    trace_ref,
    back_ref,
    semaphore,
):
    sweep, first = stage_place(place_ref, stage)
    second = 1 - first
    start_either(second, own_back_ref, other_back_ref, back_ref, semaphore)
    field_ref[...] = leaf_finish(
        second,
        own_slots_ref,
        other_slots_ref,
        returned_ref,
        back_ref,
        lambda: wait_for(own_back_ref, back_ref, semaphore),
        base_ref[...],
    )
    trace_ref[...] = pack(field_ref[pl.ds(pl.multiple_of((1 - sweep) * TR, TR), TR), :])


def enter_kernel(
    stage,
    place_ref,
    own_slots_ref,
    other_slots_ref,
    trace_ref,
    own_u_ref,
    other_u_ref,
    own_y_ref,
    other_y_ref,
    own_forward_ref,
    other_forward_ref,
    send_ref,
    next_base_ref,
    forward_ref,
    semaphore,
):
    sweep, first = stage_place(place_ref, stage)
    start_either(
        first, own_forward_ref.at[sweep], other_forward_ref.at[sweep], forward_ref, semaphore
    )
    trace, trace_turned = unpack_both(trace_ref[...])
    wait_for(own_forward_ref.at[0], forward_ref, semaphore)
    leaf_begin(
        sweep,
        first,
        trace,
        trace_turned,
        forward_ref[...],
        (own_u_ref, other_u_ref),
        (own_y_ref, other_y_ref),
        (own_slots_ref, other_slots_ref),
        send_ref,
        next_base_ref,
    )


def collect_kernel(place_ref, field_refs, own_ref, other_ref, parts_ref, semaphores):
    row = place_ref[0] // 2
    core = place_ref[0] % 2
    for sweep in range(2):
        for position in range(2):
            layer = position if sweep == 0 else 1 - position
            side = jnp.where(core == layer, 0, 1)
            for stage in range(4):
                active = row == stage if sweep == 0 else row == 3 - stage

                @pl.when(active)
                def _():
                    pltpu.make_async_copy(
                        field_refs[2 * stage + position],
                        parts_ref.at[2 * sweep + side],
                        semaphores.at[2 * sweep + position],
                    ).start()

    for index in range(4):
        wait_for(field_refs[0], parts_ref.at[0], semaphores.at[index])
    group = lane_ids(P_SIZE) // GROUP
    joined = pick(group, [parts_ref[index] for index in range(4)])
    rows = joined.T.reshape(2, 2, 2, HALF, P_SIZE)
    own_ref[...] = rows[:, 0]
    other_ref[...] = rows[:, 1]


def output_kernel(place_ref, own_ref, other_ref, down_ref, up_ref):
    core = place_ref[0] % 2
    for sweep, field_ref in enumerate((down_ref, up_ref)):
        for part in range(2):
            field_ref[part, pl.ds(pl.multiple_of(core * HALF, HALF), HALF), :] = own_ref[sweep, part]
            field_ref[part, pl.ds(pl.multiple_of((1 - core) * HALF, HALF), HALF), :] = other_ref[
                sweep, part
            ]


def call(kernel, outs, in_specs, out_specs, scratch=(), cost=None):
    return pl.pallas_call(
        kernel,
        out_shape=outs,
        in_specs=in_specs,
        out_specs=out_specs,
        scratch_shapes=list(scratch),
        compiler_params=pltpu.CompilerParams(vmem_limit_bytes=VMEM_LIMIT),
        cost_estimate=cost,
    )


def shape(*dims, dtype=f32):
    return jax.ShapeDtypeStruct(dims, dtype)


def cost_of(flops, size):
    return pl.CostEstimate(flops=flops, bytes_accessed=size, transcendentals=0)


def across_cores(value):
    layers = lax.axis_size("layer")
    return lax.ppermute(value, "layer", [(index, index ^ 1) for index in range(layers)])


def exchange(value):
    return lax.all_to_all(value, "front", split_axis=0, concat_axis=0, tiled=True)


def to_next_stage(value, stage):
    moves = [(stage, stage + 1), (3 - stage, 2 - stage)]
    pairs = [(2 * a + core, 2 * b + core) for a, b in moves for core in range(2)]
    return lax.ppermute(value, "layer", pairs)


def body(
    sources_down,
    sources_up,
    leaf_inverse,
    coupling,
    sep_inverse,
    inject_top,
    inject_bottom,
    targets,
    offsets,
):
    leaves = lax.axis_size("front")
    slots = leaves * CAP
    place = lax.axis_index("layer").reshape(1).astype(jnp.int32)
    leaf = leaf_inverse[0, 0]
    rows = coupling[0, 0]
    sep = sep_inverse[0, 0]

    own_slots, slot_offsets = call(
        slots_kernel,
        (shape(NB, dtype=jnp.int32), shape(slots, dtype=jnp.int32)),
        [smem, smem],
        (smem, smem),
        [pltpu.SMEM((leaves,), jnp.int32)],
    )(targets[0, 0, :, 0], offsets[0, 0])
    own_offsets = exchange(slot_offsets.reshape(leaves, CAP)).reshape(slots)
    other_slots = across_cores(own_slots)
    other_offsets = across_cores(own_offsets)

    u_shape = shape(2, NB, 8, LANES)
    y_shape = shape(2, P_SIZE, LANES)
    own_u, to_other_u, own_y, to_other_y = call(
        source_kernel,
        (u_shape, u_shape, y_shape, y_shape),
        [smem] + [vmem] * 4,
        (vmem,) * 4,
        cost=cost_of(600_000_000, 2_500_000),
    )(place, sources_down[0, 0], sources_up[0, 0], leaf, rows)
    other_u = across_cores(to_other_u)
    other_y = across_cores(to_other_y)

    own_forward, own_back = call(
        operator_kernel,
        (shape(2, NB * RB + P_SIZE, 2 * TR), shape(2, P_SIZE, NB * RB)),
        [vmem] * 4,
        (vmem,) * 2,
        cost=cost_of(4_000_000_000, 5_000_000),
    )(leaf, rows, inject_top[0, 0], inject_bottom[0, 0])
    other_forward = across_cores(own_forward)
    other_back = across_cores(own_back)
    other_sep = across_cores(sep)

    slot_shape = shape(slots, 8, LANES)
    field_shape = shape(P_SIZE, LANES)
    back_scratch = pltpu.VMEM((2, P_SIZE, NB * RB), f32)
    forward_scratch = pltpu.VMEM((NB * RB + P_SIZE, 2 * TR), f32)

    def separator(stage, step, arrived):
        return call(
            functools.partial(separator_kernel, stage, step),
            slot_shape,
            [smem] * 3 + [vmem] + [hbm] * 2,
            vmem,
            [
                pltpu.VMEM((2, Q, Q), f32),
                pltpu.VMEM((QB + 1, 8, LANES), f32),
                pltpu.VMEM((QB + 1, 8, LANES), f32),
                pltpu.VMEM((QB + 1, 8, LANES), f32),
                pltpu.SemaphoreType.DMA,
            ],
            cost_of(100_000_000, 1_100_000),
        )(place, own_offsets, other_offsets, arrived, sep, other_sep)

    fields = []
    base = None
    trace = None
    for stage in range(4):
        if stage == 0:
            send = call(first_kernel, slot_shape, [smem] * 3 + [vmem] * 2, vmem)(
                place, own_slots, other_slots, own_u, other_u
            )
        else:
            send, base = call(
                functools.partial(enter_kernel, stage),
                (slot_shape, field_shape),
                [smem] * 3 + [vmem] * 5 + [hbm] * 2,
                (vmem, vmem),
                [forward_scratch, pltpu.SemaphoreType.DMA],
                cost_of(100_000_000, 2_000_000),
            )(
                place,
                own_slots,
                other_slots,
                trace,
                own_u,
                other_u,
                own_y,
                other_y,
                own_forward,
                other_forward,
            )
        returned = exchange(separator(stage, 0, exchange(send)))
        bases = [] if base is None else [base]

        def middle(*refs, stage=stage, count=len(bases)):
            head, rest = refs[:4], refs[4:]
            middle_kernel(stage, *head, rest[:count], *rest[count:])

        field, send, base = call(
            middle,
            (field_shape, slot_shape, field_shape),
            [smem] * 3 + [vmem] * (1 + len(bases)) + [vmem] * 4 + [hbm] * 4,
            (vmem,) * 3,
            [back_scratch, forward_scratch, pltpu.SemaphoreType.DMA((2,))],
            cost_of(300_000_000, 3_000_000),
        )(
            place,
            own_slots,
            other_slots,
            returned,
            *bases,
            own_u,
            other_u,
            own_y,
            other_y,
            own_back,
            other_back,
            own_forward,
            other_forward,
        )
        fields.append(field)
        returned = exchange(separator(stage, 1, exchange(send)))
        field, trace = call(
            functools.partial(last_kernel, stage),
            (field_shape, shape(TR // RB, 8, LANES)),
            [smem] * 3 + [vmem] * 2 + [hbm] * 2,
            (vmem, vmem),
            [back_scratch, pltpu.SemaphoreType.DMA],
            cost_of(200_000_000, 2_000_000),
        )(place, own_slots, other_slots, returned, base, own_back, other_back)
        fields.append(field)
        if stage < 3:
            trace = to_next_stage(trace, stage)

    half_shape = shape(2, 2, HALF, P_SIZE)

    def collect(place_ref, *refs):
        collect_kernel(place_ref, refs[:8], *refs[8:])

    own, to_other = call(
        collect,
        (half_shape, half_shape),
        [smem] + [hbm] * 8,
        (vmem, vmem),
        [pltpu.VMEM((4, P_SIZE, LANES), f32), pltpu.SemaphoreType.DMA((4,))],
    )(place, *fields)
    down, up = call(
        output_kernel,
        (shape(2, S, P_SIZE), shape(2, S, P_SIZE)),
        [smem, vmem, vmem],
        (vmem, vmem),
    )(place, own, across_cores(to_other))
    return down[None, None], up[None, None]


def solution(mesh):
    whole = P("layer", "front", None, None, None)
    return jax.shard_map(
        body,
        mesh=mesh,
        in_specs=(whole,) * 7 + (P("layer", "front", None, None), P("layer", "front", None)),
        out_specs=(whole, whole),
        check_vma=False,
    )
```

time: 861 us -> 361 us (0.42)
  waiting for transfers between devices: 300 us -> 27.8 us
  blocking collectives: 0 us -> 198 us
  starting transfers between devices: 239 us -> 60.9 us
  matrix products: 167 us -> 0 us
  local copies, waits for them, and re-layouts: 99.1 us -> 15.1 us
  Pallas kernels: 0 us -> 53.8 us
  other arithmetic: 45.3 us -> 2.01 us
    all_to_all x27 -> x3, waiting for transfers between devices: 285 us -> 14.8 us  [exchange(): lax.all_to_all(value, 'front', split_axis=0, concat_axis=0, tiled=True)]
    all_to_all x0 -> x14, blocking collectives: none -> 198 us  [exchange(): lax.all_to_all(value, 'front', split_axis=0, concat_axis=0, tiled=True)]
    dot_general x288 -> x0, matrix products: 167 us -> none  [the longest x63 45 us: complex_product(): jnp.einsum(pattern, first[0], second[1], precision=precise)]
    all_to_all x27 -> x3, starting transfers between devices: 179 us -> 19.1 us  [exchange(): lax.all_to_all(value, 'front', split_axis=0, concat_axis=0, tiled=True)]
    pallas_call x0 -> x25, Pallas kernels: none -> 53.8 us  [the longest x8 17.5 us: separator(): call(functools.partial(separator_kernel, stage, step), slot_shape, [smem]...]
    while x126 -> x0, local copies, waits for them, and re-layouts: 42.2 us -> none
    all_to_all x27 -> x1, other arithmetic: 40.3 us -> 2.01 us  [exchange(): lax.all_to_all(value, 'front', split_axis=0, concat_axis=0, tiled=True)]
    dot_general x54 -> x0, local copies, waits for them, and re-layouts: 18.6 us -> none  [the longest x18 6.43 us: front_solve(): jnp.dot(select_float, packed, precision=precise)]
  transfers between devices with their start and end apart: 45 -> 14, of which waited for: 27 -> 9; matrix products, arithmetic and copies ran while one was open for 15% -> 1% of each run, Pallas kernels for 0% -> 2%
where the time goes in v1:
time: 361 us; the launch traced here: 359 us
  blocking collectives  198 us (55%)
  starting transfers between devices  60.9 us (17%)
  Pallas kernels  53.8 us (15%)
  waiting for transfers between devices  27.8 us (8%)
  local copies, waits for them, and re-layouts  15.1 us (4%)
    all_to_all x14, blocking collectives, exchange(): lax.all_to_all(value, 'front', split_axis=0, concat_axis=0, tiled=True)  198 us
    ppermute x8, starting transfers between devices, across_cores(): lax.ppermute(value, 'layer', [(index, index ^ 1) for index in range(layer...  36.7 us
    all_to_all x3, starting transfers between devices, exchange(): lax.all_to_all(value, 'front', split_axis=0, concat_axis=0, tiled=True)  19.1 us
    pallas_call x8, Pallas kernels, separator(): call(functools.partial(separator_kernel, stage, step), slot_shape, [smem]...  17.5 us
    all_to_all x3, waiting for transfers between devices, exchange(): lax.all_to_all(value, 'front', split_axis=0, concat_axis=0, tiled=True)  14.8 us
    unnamed x40, local copies, waits for them, and re-layouts  13.1 us
    pallas_call x4, Pallas kernels, body(): call(middle, (field_shape, slot_shape, field_shape), [smem] * 3 + [vmem]...  12.4 us
    pallas_call x4, Pallas kernels, body(): call(functools.partial(last_kernel, stage), (field_shape, shape(TR // RB,...  10.1 us
  transfers between devices with their start and end apart: 14, of which 9 were waited for; matrix products, arithmetic and copies ran while one was open for 1% of the time, Pallas kernels for 2%

profile of v1, /device:TPU:1, one launch (start us, length us, event | category | flops | bytes accessed | tf_op | source)
XLA Modules:
  0.0 359.1 jit_solution(13125390301155710344)
XLA Ops:
  4.8 3.3 shard_map.108
  8.2 3.2 collective-permute-start.6
  20.6 9.4 %all-to-all-start = ((s32[32,1,2]{2,1,0:T(1,128)}), s32[32,1,2]{2,1,0:T(1,128)}, u32[]{:S(2)}, u32[]{:S(2)}) async-start(s32[32,1,2]{2,1,0:T(1,128)} %bitcast.23), calls=%async_computation | async-start | bytes 32768 | tf_op jit(solution)/shard_map/all_to_all | solution.py:455
  33.4 5.1 %all-to-all-done = s32[32,1,2]{2,1,0:T(1,128)} async-done(((s32[32,1,2]{2,1,0:T(1,128)}), s32[32,1,2]{2,1,0:T(1,128)}, u32[]{:S(2)}, u32[]{:S(2)}) %all-to-all-start) | async-done | bytes 288 | tf_op jit(solution)/shard_map/all_to_all | solution.py:455
  38.5 4.6 %all-to-all-start.1 = ((f32[64,8,128]{2,1,0:T(8,128)}), f32[64,8,128]{2,1,0:T(8,128)}, u32[]{:S(2)}, u32[]{:S(2)}) async-start(f32[64,8,128]{2,1,0:T(8,128)} %copy-done.8), calls=%async_computation.1 | async-start | bytes 524288 | tf_op jit(solution)/shard_map/all_to_all | solution.py:455
  49.1 4.5 %all-to-all-done.1.arrived_ref = f32[64,8,128]{2,1,0:T(8,128)} async-done(((f32[64,8,128]{2,1,0:T(8,128)}), f32[64,8,128]{2,1,0:T(8,128)}, u32[]{:S(2)}, u32[]{:S(2)}) %all-to-all-start.1) | async-done | bytes 262176 | tf_op jit(solution)/shard_map/all_to_all | solution.py:455
  56.9 5.1 %all-to-all-start.2 = ((f32[64,8,128]{2,1,0:T(8,128)}), f32[64,8,128]{2,1,0:T(8,128)}, u32[]{:S(2)}, u32[]{:S(2)}) async-start(f32[64,8,128]{2,1,0:T(8,128)} %copy-done.7), calls=%async_computation.2 | async-start | bytes 524288 | tf_op jit(solution)/shard_map/all_to_all | solution.py:455
  67.2 5.2 %all-to-all-done.2.refs_3_ = f32[64,8,128]{2,1,0:T(8,128)} async-done(((f32[64,8,128]{2,1,0:T(8,128)}), f32[64,8,128]{2,1,0:T(8,128)}, u32[]{:S(2)}, u32[]{:S(2)}) %all-to-all-start.2) | async-done | bytes 262176 | tf_op jit(solution)/shard_map/all_to_all | solution.py:455
  77.7 14.5 %all_to_all.89.arrived_ref = f32[64,8,128]{2,1,0:T(8,128)S(1)} all-to-all(f32[64,8,128]{2,1,0:T(8,128)S(1)} %get-tuple-element.48), channel_id=1, replica_groups=mesh['layer'=8,'front'=32] {'front'}, dimensions={0} | all-to-all | bytes 524288 | tf_op jit(solution)/shard_map/all_to_all | solution.py:455
  94.4 14.1 %all_to_all.90.returned_ref = f32[64,8,128]{2,1,0:T(8,128)S(1)} all-to-all(f32[64,8,128]{2,1,0:T(8,128)S(1)} %shard_map.110), channel_id=1, replica_groups=mesh['layer'=8,'front'=32] {'front'}, dimensions={0} | all-to-all | bytes 524288 | tf_op jit(solution)/shard_map/all_to_all | solution.py:455
  116.5 13.9 %all_to_all.91.arrived_ref = f32[64,8,128]{2,1,0:T(8,128)S(1)} all-to-all(f32[64,8,128]{2,1,0:T(8,128)S(1)} %get-tuple-element.52), channel_id=1, replica_groups=mesh['layer'=8,'front'=32] {'front'}, dimensions={0} | all-to-all | bytes 524288 | tf_op jit(solution)/shard_map/all_to_all | solution.py:455
  132.5 13.8 %all_to_all.92.refs_3_ = f32[64,8,128]{2,1,0:T(8,128)S(1)} all-to-all(f32[64,8,128]{2,1,0:T(8,128)S(1)} %shard_map.113), channel_id=1, replica_groups=mesh['layer'=8,'front'=32] {'front'}, dimensions={0} | all-to-all | bytes 524288 | tf_op jit(solution)/shard_map/all_to_all | solution.py:455
  149.4 13.8 %all_to_all.93.arrived_ref = f32[64,8,128]{2,1,0:T(8,128)S(1)} all-to-all(f32[64,8,128]{2,1,0:T(8,128)S(1)} %get-tuple-element.55), channel_id=1, replica_groups=mesh['layer'=8,'front'=32] {'front'}, dimensions={0} | all-to-all | bytes 524288 | tf_op jit(solution)/shard_map/all_to_all | solution.py:455
  165.3 13.9 %all_to_all.94.returned_ref = f32[64,8,128]{2,1,0:T(8,128)S(1)} all-to-all(f32[64,8,128]{2,1,0:T(8,128)S(1)} %shard_map.115), channel_id=1, replica_groups=mesh['layer'=8,'front'=32] {'front'}, dimensions={0} | all-to-all | bytes 524288 | tf_op jit(solution)/shard_map/all_to_all | solution.py:455
  183.8 13.8 %all_to_all.95.arrived_ref = f32[64,8,128]{2,1,0:T(8,128)S(1)} all-to-all(f32[64,8,128]{2,1,0:T(8,128)S(1)} %get-tuple-element.59), channel_id=1, replica_groups=mesh['layer'=8,'front'=32] {'front'}, dimensions={0} | all-to-all | bytes 524288 | tf_op jit(solution)/shard_map/all_to_all | solution.py:455
  199.7 14.1 %all_to_all.96.refs_3_ = f32[64,8,128]{2,1,0:T(8,128)S(1)} all-to-all(f32[64,8,128]{2,1,0:T(8,128)S(1)} %shard_map.118), channel_id=1, replica_groups=mesh['layer'=8,'front'=32] {'front'}, dimensions={0} | all-to-all | bytes 524288 | tf_op jit(solution)/shard_map/all_to_all | solution.py:455
  216.9 14.3 %all_to_all.97.arrived_ref = f32[64,8,128]{2,1,0:T(8,128)S(1)} all-to-all(f32[64,8,128]{2,1,0:T(8,128)S(1)} %get-tuple-element.62), channel_id=1, replica_groups=mesh['layer'=8,'front'=32] {'front'}, dimensions={0} | all-to-all | bytes 524288 | tf_op jit(solution)/shard_map/all_to_all | solution.py:455
  233.4 16.1 %all_to_all.98.returned_ref = f32[64,8,128]{2,1,0:T(8,128)S(1)} all-to-all(f32[64,8,128]{2,1,0:T(8,128)S(1)} %shard_map.120), channel_id=1, replica_groups=mesh['layer'=8,'front'=32] {'front'}, dimensions={0} | all-to-all | bytes 524288 | tf_op jit(solution)/shard_map/all_to_all | solution.py:455
  253.2 8.3 %collective-permute-done.9.trace_ref = f32[4,8,128]{2,1,0:T(8,128)S(1)} collective-permute-done((f32[4,8,128]{2,1,0:T(8,128)S(1)}, f32[4,8,128]{2,1,0:T(8,128)S(1)}, u32[]{:S(2)}, u32[]{:S(2)}) %collective-permute-start.9) | collective-permute-done | bytes 16416 | tf_op jit(solution)/shard_map/ppermute | solution.py:461
  263.0 15.0 %all_to_all.99.arrived_ref = f32[64,8,128]{2,1,0:T(8,128)S(1)} all-to-all(f32[64,8,128]{2,1,0:T(8,128)S(1)} %get-tuple-element.66), channel_id=1, replica_groups=mesh['layer'=8,'front'=32] {'front'}, dimensions={0} | all-to-all | bytes 524288 | tf_op jit(solution)/shard_map/all_to_all | solution.py:455
  280.1 13.8 %all_to_all.100.refs_3_ = f32[64,8,128]{2,1,0:T(8,128)S(1)} all-to-all(f32[64,8,128]{2,1,0:T(8,128)S(1)} %shard_map.123), channel_id=1, replica_groups=mesh['layer'=8,'front'=32] {'front'}, dimensions={0} | all-to-all | bytes 524288 | tf_op jit(solution)/shard_map/all_to_all | solution.py:455
  296.9 13.8 %all_to_all.101.arrived_ref = f32[64,8,128]{2,1,0:T(8,128)S(1)} all-to-all(f32[64,8,128]{2,1,0:T(8,128)S(1)} %get-tuple-element.69), channel_id=1, replica_groups=mesh['layer'=8,'front'=32] {'front'}, dimensions={0} | all-to-all | bytes 524288 | tf_op jit(solution)/shard_map/all_to_all | solution.py:455
  312.9 13.8 %all_to_all.102.returned_ref = f32[64,8,128]{2,1,0:T(8,128)S(1)} all-to-all(f32[64,8,128]{2,1,0:T(8,128)S(1)} %shard_map.125), channel_id=1, replica_groups=mesh['layer'=8,'front'=32] {'front'}, dimensions={0} | all-to-all | bytes 524288 | tf_op jit(solution)/shard_map/all_to_all | solution.py:455
  330.5 27.0 %collective-permute-start.10 = (f32[2,2,16,256]{3,2,1,0:T(8,128)S(1)}, f32[2,2,16,256]{3,2,1,0:T(8,128)S(1)}, u32[]{:S(2)}, u32[]{:S(2)}) collective-permute-start(f32[2,2,16,256]{3,2,1,0:T(8,128)S(1)} %get-tuple-element.73), channel_id=1, source_target_pairs={{0,32},{32,0},{64,96},{96,64},{128,160},{160,128},{192,224},{224,1... | collective-permute-start | bytes 196616 | tf_op jit(solution)/shard_map/ppermute | solution.py:451
  (87 shorter events, 83.9 us)
Async XLA Ops:
  0.6 1.2 copy-start.9
  1.9 1.0 copy-start.11
  8.2 10.5 %copy-start.18 = (s32[1,1,16,1]{2,3,1,0:T(1,128)S(1)}, s32[1,1,16,1]{2,3,1,0:T(1,128)}, u32[]{:S(2)}) copy-start(s32[1,1,16,1]{2,3,1,0:T(1,128)} %param.16) | copy-start | bytes 196
  8.2 10.5 %copy-start.19 = (s32[1,1,16]{2,1,0:T(1,128)S(1)}, s32[1,1,16]{2,1,0:T(1,128)}, u32[]{:S(2)}) copy-start(s32[1,1,16]{2,1,0:T(1,128)} %param.17) | copy-start | bytes 196
  8.2 64.3 %collective-permute-start.6 = (f32[2,768,256]{2,1,0:T(8,128)S(1)}, f32[2,768,256]{2,1,0:T(8,128)S(1)}, u32[]{:S(2)}, u32[]{:S(2)}) collective-permute-start(f32[2,768,256]{2,1,0:T(8,128)S(1)} %get-tuple-element.46.refs_10_.own_forward_ref.refs_11_), channel_id=1, source_target_pairs={{0,32},{32,0},{64,96},{96,64},{128,160},{160,128},{192,224},{224,1... | collective-permute-start | bytes 4718600 | tf_op jit(solution)/shard_map/ppermute | solution.py:451
  11.4 1.2 copy-start.10
  18.1 13.6 %collective-permute-start.2 = (f32[2,16,8,128]{3,2,1,0:T(8,128)}, f32[2,16,8,128]{3,2,1,0:T(8,128)}, u32[]{:S(2)}, u32[]{:S(2)}) collective-permute-start(f32[2,16,8,128]{3,2,1,0:T(8,128)} %get-tuple-element.42), channel_id=1, source_target_pairs={{0,32},{32,0},{64,96},{96,64},{128,160},{160,128},{192,224},{224,1... | collective-permute-start | bytes 393224 | tf_op jit(solution)/shard_map/ppermute | solution.py:451
  18.1 49.1 %collective-permute-start.5 = (f32[2,256,512]{2,1,0:T(8,128)}, f32[2,256,512]{2,1,0:T(8,128)}, u32[]{:S(2)}, u32[]{:S(2)}) collective-permute-start(f32[2,256,512]{2,1,0:T(8,128)} %get-tuple-element.45.refs_8_.own_back_ref.refs_9_), channel_id=1, source_target_pairs={{0,32},{32,0},{64,96},{96,64},{128,160},{160,128},{192,224},{224,1... | collective-permute-start | bytes 3145736 | tf_op jit(solution)/shard_map/ppermute | solution.py:451
  18.6 30.6 %collective-permute-start.3 = (f32[2,256,256]{2,1,0:T(8,128)}, f32[2,256,256]{2,1,0:T(8,128)}, u32[]{:S(2)}, u32[]{:S(2)}) collective-permute-start(f32[2,256,256]{2,1,0:T(8,128)} %bitcast.8.own_sep_ref), channel_id=1, source_target_pairs={{0,32},{32,0},{64,96},{96,64},{128,160},{160,128},{192,224},{224,1... | collective-permute-start | bytes 1572872 | tf_op jit(solution)/shard_map/ppermute | solution.py:451
  20.6 17.9 %all-to-all-start = ((s32[32,1,2]{2,1,0:T(1,128)}), s32[32,1,2]{2,1,0:T(1,128)}, u32[]{:S(2)}, u32[]{:S(2)}) async-start(s32[32,1,2]{2,1,0:T(1,128)} %bitcast.23), calls=%async_computation | async-start | bytes 32768 | tf_op jit(solution)/shard_map/all_to_all | solution.py:455
  30.0 1.7 collective-permute-start
  38.5 15.1 %all-to-all-start.1 = ((f32[64,8,128]{2,1,0:T(8,128)}), f32[64,8,128]{2,1,0:T(8,128)}, u32[]{:S(2)}, u32[]{:S(2)}) async-start(f32[64,8,128]{2,1,0:T(8,128)} %copy-done.8), calls=%async_computation.1 | async-start | bytes 524288 | tf_op jit(solution)/shard_map/all_to_all | solution.py:455
  46.5 2.7 collective-permute-start.1
  56.9 15.5 %all-to-all-start.2 = ((f32[64,8,128]{2,1,0:T(8,128)}), f32[64,8,128]{2,1,0:T(8,128)}, u32[]{:S(2)}, u32[]{:S(2)}) async-start(f32[64,8,128]{2,1,0:T(8,128)} %copy-done.7), calls=%async_computation.2 | async-start | bytes 524288 | tf_op jit(solution)/shard_map/all_to_all | solution.py:455
  62.0 4.5 %collective-permute-start.4 = (f32[2,256,128]{2,1,0:T(8,128)}, f32[2,256,128]{2,1,0:T(8,128)S(1)}, u32[]{:S(2)}, u32[]{:S(2)}) collective-permute-start(f32[2,256,128]{2,1,0:T(8,128)} %copy-done.15), channel_id=1, source_target_pairs={{0,32},{32,0},{64,96},{96,64},{128,160},{160,128},{192,224},{224,1... | collective-permute-start | bytes 786440 | tf_op jit(solution)/shard_map/ppermute | solution.py:451
  72.4 1.2 copy-start
  94.4 20.6 %copy-start.1 = (f32[2,768,256]{2,1,0:T(8,128)S(1)}, f32[2,768,256]{2,1,0:T(8,128)}, u32[]{:S(2)}) copy-start(f32[2,768,256]{2,1,0:T(8,128)} %copy-done) | copy-start | bytes 4718596
  94.4 20.6 %copy-start.6 = (f32[2,256,128]{2,1,0:T(8,128)S(1)}, f32[2,256,128]{2,1,0:T(8,128)}, u32[]{:S(2)}) copy-start(f32[2,256,128]{2,1,0:T(8,128)} %copy-done.4) | copy-start | bytes 786436
  110.9 4.1 %collective-permute-start.7 = (f32[4,8,128]{2,1,0:T(8,128)S(1)}, f32[4,8,128]{2,1,0:T(8,128)S(1)}, u32[]{:S(2)}, u32[]{:S(2)}) collective-permute-start(f32[4,8,128]{2,1,0:T(8,128)S(1)} %get-tuple-element.51), channel_id=1, source_target_pairs={{0,64},{32,96},{192,128},{224,160},{1,65},{33,97},{193,129},{225,1... | collective-permute-start | bytes 49160 | tf_op jit(solution)/shard_map/ppermute | solution.py:461
  165.3 17.0 %copy-start.2 = (f32[2,768,256]{2,1,0:T(8,128)S(1)}, f32[2,768,256]{2,1,0:T(8,128)}, u32[]{:S(2)}) copy-start(f32[2,768,256]{2,1,0:T(8,128)} %copy-done) | copy-start | bytes 4718596
  181.6 0.7 collective-permute-start.8
  233.3 28.1 %copy-start.3 = (f32[2,768,256]{2,1,0:T(8,128)S(1)}, f32[2,768,256]{2,1,0:T(8,128)}, u32[]{:S(2)}) copy-start(f32[2,768,256]{2,1,0:T(8,128)} %copy-done) | copy-start | bytes 4718596
  251.9 9.6 %collective-permute-start.9 = (f32[4,8,128]{2,1,0:T(8,128)S(1)}, f32[4,8,128]{2,1,0:T(8,128)S(1)}, u32[]{:S(2)}, u32[]{:S(2)}) collective-permute-start(f32[4,8,128]{2,1,0:T(8,128)S(1)} %get-tuple-element.65), channel_id=1, source_target_pairs={{128,192},{160,224},{64,0},{96,32},{129,193},{161,225},{65,1},{97,... | collective-permute-start | bytes 49160 | tf_op jit(solution)/shard_map/ppermute | solution.py:461
  330.5 27.9 %collective-permute-start.10 = (f32[2,2,16,256]{3,2,1,0:T(8,128)S(1)}, f32[2,2,16,256]{3,2,1,0:T(8,128)S(1)}, u32[]{:S(2)}, u32[]{:S(2)}) collective-permute-start(f32[2,2,16,256]{3,2,1,0:T(8,128)S(1)} %get-tuple-element.73), channel_id=1, source_target_pairs={{0,32},{32,0},{64,96},{96,64},{128,160},{160,128},{192,224},{224,1... | collective-permute-start | bytes 196616 | tf_op jit(solution)/shard_map/ppermute | solution.py:451
  (10 other events, 8.4 us)

commit v2 on v1

--- a/solution.py
+++ b/solution.py
@@ -23,6 +23,7 @@
 f32 = jnp.float32
 bf16 = jnp.bfloat16
 VMEM_LIMIT = 48 * 1024 * 1024
+ALMOST_ALL_VMEM = 60 * 1024 * 1024
 smem = pl.BlockSpec(memory_space=pltpu.SMEM)
 vmem = pl.BlockSpec(memory_space=pltpu.VMEM)
 hbm = pl.BlockSpec(memory_space=pl.ANY)
@@ -111,27 +112,40 @@
     return pick(group, [parts[:, k] for k in range(4)])
 
 
-def slots_kernel(targets_ref, offsets_ref, slots_ref, slot_offsets_ref, used_ref):
-    leaves = slot_offsets_ref.shape[0] // CAP
-    for leaf in range(leaves):
-        used_ref[leaf] = 0
-    for slot in range(leaves * CAP):
-        slot_offsets_ref[slot] = QB
-    for block in range(NB):
-        target = targets_ref[block]
-        rank = used_ref[target]
-        used_ref[target] = rank + 1
-        slot = target * CAP + rank
-        slots_ref[block] = slot
-        slot_offsets_ref[slot] = offsets_ref[block]
-
-
 def source_kernel(
-    place_ref, down_ref, up_ref, leaf_ref, coupling_ref, own_u_ref, other_u_ref, own_y_ref, other_y_ref
+    place_ref,
+    down_hbm,
+    up_hbm,
+    leaf_hbm,
+    coupling_hbm,
+    own_u_ref,
+    other_u_ref,
+    own_y_ref,
+    other_y_ref,
+    down_ref,
+    up_ref,
+    leaf_ref,
+    coupling_ref,
+    semaphores,
 ):
+    copies = [
+        pltpu.make_async_copy(source, target, semaphores.at[index])
+        for index, (source, target) in enumerate(
+            (
+                (down_hbm, down_ref),
+                (up_hbm, up_ref),
+                (leaf_hbm, leaf_ref),
+                (coupling_hbm, coupling_ref),
+            )
+        )
+    ]
+    for copy in copies:
+        copy.start()
     core = place_ref[0] % 2
     own_row = pl.multiple_of(core * HALF, HALF)
     other_row = pl.multiple_of((1 - core) * HALF, HALF)
+    copies[0].wait()
+    copies[1].wait()
     rows, turned_rows = [], []
     for source in (down_ref, up_ref):
         for start in (own_row, other_row):
@@ -139,33 +153,65 @@
             imag = source[1, pl.ds(start, HALF), :]
             rows += [real, imag]
             turned_rows += [-imag, real]
+    copies[2].wait()
     y = product(leaf_ref[0], jnp.concatenate(rows, axis=0), NT) + product(
         leaf_ref[1], jnp.concatenate(turned_rows, axis=0), NT
     )
-    u = narrow_product(coupling_ref[0], y) + narrow_product(coupling_ref[1], turned(y))
     rolled = rotations(y)
     y_group = lane_ids(P_SIZE) // GROUP
+    for sweep in range(2):
+        for side, y_ref in enumerate((own_y_ref, other_y_ref)):
+            y_ref[sweep] = spread_group(rolled, y_group, 2 * sweep + side)
+    copies[3].wait()
+    u = narrow_product(coupling_ref[0], y) + narrow_product(coupling_ref[1], turned(y))
     parts = u.reshape(NB, 4, 8, LANES)
     u_group = lane_ids(NB * 8) // GROUP
     for sweep in range(2):
-        for side, (u_ref, y_ref) in enumerate(((own_u_ref, own_y_ref), (other_u_ref, other_y_ref))):
-            source = 2 * sweep + side
-            y_ref[sweep] = spread_group(rolled, y_group, source)
+        for side, u_ref in enumerate((own_u_ref, other_u_ref)):
             choices = []
             for k in range(4):
                 part = parts[:, k].reshape(NB * 8, LANES)
-                turn = (k - source) % 4
+                turn = (k - 2 * sweep - side) % 4
                 choices.append(pltpu.roll(part, GROUP * turn, 1) if turn else part)
             u_ref[sweep] = pick(u_group, choices).reshape(NB, 8, LANES)
 
 
-def operator_kernel(leaf_ref, coupling_ref, top_ref, bottom_ref, forward_ref, back_ref):
+def operator_kernel(
+    after_ref,
+    leaf_hbm,
+    coupling_hbm,
+    top_hbm,
+    bottom_hbm,
+    forward_ref,
+    back_ref,
+    leaf_ref,
+    coupling_ref,
+    top_ref,
+    bottom_ref,
+    semaphores,
+):
+    copies = [
+        pltpu.make_async_copy(source, target, semaphores.at[index])
+        for index, (source, target) in enumerate(
+            (
+                (leaf_hbm, leaf_ref),
+                (top_hbm, top_ref),
+                (bottom_hbm, bottom_ref),
+                (coupling_hbm, coupling_ref),
+            )
+        )
+    ]
+    for copy in copies:
+        copy.start()
+    for copy in copies[:3]:
+        copy.wait()
     leaf = (leaf_ref[0], leaf_ref[1])
-    coupling = (coupling_ref[0], coupling_ref[1])
     inject = tuple(
         jnp.concatenate([top_ref[part], bottom_ref[part]], axis=0) for part in range(2)
     )
     local = complex_pair(leaf, inject, NT)
+    copies[3].wait()
+    coupling = (coupling_ref[0], coupling_ref[1])
     update = complex_pair(coupling, local)
     for sweep in range(2):
         for part in range(2):
@@ -206,18 +252,76 @@
         send_ref[slot] = packed[block]
 
 
-def first_kernel(place_ref, own_slots_ref, other_slots_ref, own_u_ref, other_u_ref, send_ref):
+def first_kernel(
+    place_ref,
+    own_targets_ref,
+    other_targets_ref,
+    own_offsets_ref,
+    other_offsets_ref,
+    own_u_ref,
+    other_u_ref,
+    own_slots_ref,
+    other_slots_ref,
+    send_ref,
+):
+    leaves = send_ref.shape[0]
     sweep, first = stage_place(place_ref, 0)
+    lanes = lane_ids(leaves)
+    rows = lax.broadcasted_iota(jnp.int32, (leaves, LANES), 0)
+    notes = jnp.full((leaves, LANES), QB, jnp.int32)
+    all_slots = []
+    for side, (targets_ref, offsets_ref, slots_ref) in enumerate(
+        (
+            (own_targets_ref, own_offsets_ref, own_slots_ref),
+            (other_targets_ref, other_offsets_ref, other_slots_ref),
+        )
+    ):
+        targets = [targets_ref[block] for block in range(NB)]
+        slots = []
+        for block in range(NB):
+            rank = jnp.int32(0)
+            for earlier in range(block):
+                rank = rank + jnp.where(targets[earlier] == targets[block], 1, 0)
+            slot = targets[block] * CAP + rank
+            slots_ref[block] = slot
+            slots.append(slot)
+            here = (rows == targets[block]) & (lanes == CAP * side + rank)
+            notes = jnp.where(here, offsets_ref[block], notes)
+        all_slots.append(slots)
+    send_ref[:, CAP * 8 :, :] = jnp.broadcast_to(
+        notes.astype(f32)[:, None, :], (leaves, 8, LANES)
+    )
     packed = jnp.where(first == 0, own_u_ref[sweep], other_u_ref[sweep])
-    send_blocks(first, own_slots_ref, other_slots_ref, packed, send_ref)
+    for block in range(NB):
+        slot = jnp.where(first == 0, all_slots[0][block], all_slots[1][block])
+        row = pl.multiple_of((slot % CAP) * 8, 8)
+        send_ref[slot // CAP, pl.ds(row, 8), :] = packed[block]
+
+
+def separator_solve(choice, offsets_ref, arrived, reply_ref, sep, even_ref, odd_ref, solved_ref):
+    leaves = reply_ref.shape[0] // CAP
+    even_ref[...] = jnp.zeros_like(even_ref)
+    odd_ref[...] = jnp.zeros_like(odd_ref)
+    places = []
+    for leaf in range(leaves):
+        for rank, total_ref in enumerate((even_ref, odd_ref)):
+            place = offsets_ref[CAP * choice + rank, leaf]
+            places.append(place)
+            total_ref[place] = total_ref[place] + arrived(leaf, rank)
+    rhs, rhs_turned = unpack_both(even_ref[:QB] + odd_ref[:QB])
+    sep_ref = sep()
+    solved = narrow_product(sep_ref[0], rhs) + narrow_product(sep_ref[1], rhs_turned)
+    solved_ref[:QB] = pack(solved)
+    solved_ref[QB] = jnp.zeros((8, LANES), f32)
+    for slot, place in enumerate(places):
+        reply_ref[slot] = solved_ref[place]
 
 
 def separator_kernel(
     stage,
     step,
     place_ref,
-    own_offsets_ref,
-    other_offsets_ref,
+    offsets_ref,
     arrived_ref,
     own_sep_ref,
     other_sep_ref,
@@ -231,22 +335,61 @@
     sweep, first = stage_place(place_ref, stage)
     choice = first if step == 0 else 1 - first
     start_either(choice, own_sep_ref, other_sep_ref, sep_ref, semaphore)
-    slots = arrived_ref.shape[0]
-    even_ref[...] = jnp.zeros_like(even_ref)
-    odd_ref[...] = jnp.zeros_like(odd_ref)
-    places = []
-    for slot in range(slots):
-        place = jnp.where(choice == 0, own_offsets_ref[slot], other_offsets_ref[slot])
-        places.append(place)
-        total_ref = odd_ref if slot % 2 else even_ref
-        total_ref[place] = total_ref[place] + arrived_ref[slot]
-    rhs, rhs_turned = unpack_both(even_ref[:QB] + odd_ref[:QB])
-    wait_for(own_sep_ref, sep_ref, semaphore)
-    solved = narrow_product(sep_ref[0], rhs) + narrow_product(sep_ref[1], rhs_turned)
-    solved_ref[:QB] = pack(solved)
-    solved_ref[QB] = jnp.zeros((8, LANES), f32)
-    for slot in range(slots):
-        reply_ref[slot] = solved_ref[places[slot]]
+
+    def sep():
+        wait_for(own_sep_ref, sep_ref, semaphore)
+        return sep_ref
+
+    separator_solve(
+        choice,
+        offsets_ref,
+        lambda leaf, rank: arrived_ref[CAP * leaf + rank],
+        reply_ref,
+        sep,
+        even_ref,
+        odd_ref,
+        solved_ref,
+    )
+
+
+def first_separator_kernel(
+    place_ref,
+    arrived_ref,
+    own_sep_ref,
+    other_sep_ref,
+    offsets_ref,
+    reply_ref,
+    sep_ref,
+    even_ref,
+    odd_ref,
+    solved_ref,
+    notes_ref,
+    semaphores,
+):
+    sweep, first = stage_place(place_ref, 0)
+    start_either(first, own_sep_ref, other_sep_ref, sep_ref, semaphores.at[0])
+    leaves = arrived_ref.shape[0]
+    notes = arrived_ref[:, CAP * 8, :]
+    whole = jnp.concatenate([notes, jnp.zeros((LANES - leaves, LANES), f32)], axis=0)
+    notes_ref[...] = whole.T[:8].astype(jnp.int32)
+    copy = pltpu.make_async_copy(notes_ref, offsets_ref, semaphores.at[1])
+    copy.start()
+    copy.wait()
+
+    def sep():
+        wait_for(own_sep_ref, sep_ref, semaphores.at[0])
+        return sep_ref
+
+    separator_solve(
+        first,
+        offsets_ref,
+        lambda leaf, rank: arrived_ref[leaf, 8 * rank : 8 * rank + 8, :],
+        reply_ref,
+        sep,
+        even_ref,
+        odd_ref,
+        solved_ref,
+    )
 
 
 def leaf_finish(choice, own_slots_ref, other_slots_ref, returned_ref, back_ref, wait, base):
@@ -426,14 +569,14 @@
             ]
 
 
-def call(kernel, outs, in_specs, out_specs, scratch=(), cost=None):
+def call(kernel, outs, in_specs, out_specs, scratch=(), cost=None, limit=VMEM_LIMIT):
     return pl.pallas_call(
         kernel,
         out_shape=outs,
         in_specs=in_specs,
         out_specs=out_specs,
         scratch_shapes=list(scratch),
-        compiler_params=pltpu.CompilerParams(vmem_limit_bytes=VMEM_LIMIT),
+        compiler_params=pltpu.CompilerParams(vmem_limit_bytes=limit),
         cost_estimate=cost,
     )
 
@@ -478,71 +621,96 @@
     leaf = leaf_inverse[0, 0]
     rows = coupling[0, 0]
     sep = sep_inverse[0, 0]
-
-    own_slots, slot_offsets = call(
-        slots_kernel,
-        (shape(NB, dtype=jnp.int32), shape(slots, dtype=jnp.int32)),
-        [smem, smem],
-        (smem, smem),
-        [pltpu.SMEM((leaves,), jnp.int32)],
-    )(targets[0, 0, :, 0], offsets[0, 0])
-    own_offsets = exchange(slot_offsets.reshape(leaves, CAP)).reshape(slots)
-    other_slots = across_cores(own_slots)
-    other_offsets = across_cores(own_offsets)
-
+    own_targets = targets[0, 0, :, 0]
+    other_targets = across_cores(own_targets)
+    other_offsets = across_cores(offsets[0, 0])
+    other_sep = across_cores(sep)
+
+    source_scratch = pltpu.VMEM((2, S, P_SIZE), f32)
+    leaf_scratch = pltpu.VMEM((2, P_SIZE, P_SIZE), f32)
+    rows_scratch = pltpu.VMEM((2, NB * RB, P_SIZE), f32)
+    inject_scratch = pltpu.VMEM((2, TR, P_SIZE), f32)
     u_shape = shape(2, NB, 8, LANES)
     y_shape = shape(2, P_SIZE, LANES)
     own_u, to_other_u, own_y, to_other_y = call(
         source_kernel,
         (u_shape, u_shape, y_shape, y_shape),
-        [smem] + [vmem] * 4,
+        [smem] + [hbm] * 4,
         (vmem,) * 4,
-        cost=cost_of(600_000_000, 2_500_000),
+        [
+            source_scratch,
+            source_scratch,
+            leaf_scratch,
+            rows_scratch,
+            pltpu.SemaphoreType.DMA((4,)),
+        ],
+        cost_of(600_000_000, 2_500_000),
+        ALMOST_ALL_VMEM,
     )(place, sources_down[0, 0], sources_up[0, 0], leaf, rows)
     other_u = across_cores(to_other_u)
-    other_y = across_cores(to_other_y)
 
     own_forward, own_back = call(
         operator_kernel,
         (shape(2, NB * RB + P_SIZE, 2 * TR), shape(2, P_SIZE, NB * RB)),
-        [vmem] * 4,
+        [hbm] * 5,
         (vmem,) * 2,
-        cost=cost_of(4_000_000_000, 5_000_000),
-    )(leaf, rows, inject_top[0, 0], inject_bottom[0, 0])
+        [
+            leaf_scratch,
+            rows_scratch,
+            inject_scratch,
+            inject_scratch,
+            pltpu.SemaphoreType.DMA((4,)),
+        ],
+        cost_of(4_000_000_000, 5_000_000),
+        ALMOST_ALL_VMEM,
+    )(to_other_u, leaf, rows, inject_top[0, 0], inject_bottom[0, 0])
+    other_y = across_cores(to_other_y)
+    other_back = across_cores(own_back)
     other_forward = across_cores(own_forward)
-    other_back = across_cores(own_back)
-    other_sep = across_cores(sep)
 
     slot_shape = shape(slots, 8, LANES)
     field_shape = shape(P_SIZE, LANES)
+    slots_shape = shape(NB, dtype=jnp.int32)
     back_scratch = pltpu.VMEM((2, P_SIZE, NB * RB), f32)
     forward_scratch = pltpu.VMEM((NB * RB + P_SIZE, 2 * TR), f32)
+    separator_scratch = [
+        pltpu.VMEM((2, Q, Q), f32),
+        pltpu.VMEM((QB + 1, 8, LANES), f32),
+        pltpu.VMEM((QB + 1, 8, LANES), f32),
+        pltpu.VMEM((QB + 1, 8, LANES), f32),
+    ]
+
+    own_slots, other_slots, send = call(
+        first_kernel,
+        (slots_shape, slots_shape, shape(leaves, (CAP + 1) * 8, LANES)),
+        [smem] * 5 + [vmem] * 2,
+        (smem, smem, vmem),
+    )(place, own_targets, other_targets, offsets[0, 0], other_offsets, own_u, other_u)
+    places, reply = call(
+        first_separator_kernel,
+        (shape(8, LANES, dtype=jnp.int32), slot_shape),
+        [smem, vmem, hbm, hbm],
+        (smem, vmem),
+        separator_scratch
+        + [pltpu.VMEM((8, LANES), jnp.int32), pltpu.SemaphoreType.DMA((2,))],
+        cost_of(100_000_000, 1_100_000),
+    )(place, exchange(send), sep, other_sep)
 
     def separator(stage, step, arrived):
         return call(
             functools.partial(separator_kernel, stage, step),
             slot_shape,
-            [smem] * 3 + [vmem] + [hbm] * 2,
+            [smem] * 2 + [vmem] + [hbm] * 2,
             vmem,
-            [
-                pltpu.VMEM((2, Q, Q), f32),
-                pltpu.VMEM((QB + 1, 8, LANES), f32),
-                pltpu.VMEM((QB + 1, 8, LANES), f32),
-                pltpu.VMEM((QB + 1, 8, LANES), f32),
-                pltpu.SemaphoreType.DMA,
-            ],
+            separator_scratch + [pltpu.SemaphoreType.DMA],
             cost_of(100_000_000, 1_100_000),
-        )(place, own_offsets, other_offsets, arrived, sep, other_sep)
+        )(place, places, arrived, sep, other_sep)
 
     fields = []
     base = None
     trace = None
     for stage in range(4):
-        if stage == 0:
-            send = call(first_kernel, slot_shape, [smem] * 3 + [vmem] * 2, vmem)(
-                place, own_slots, other_slots, own_u, other_u
-            )
-        else:
+        if stage > 0:
             send, base = call(
                 functools.partial(enter_kernel, stage),
                 (slot_shape, field_shape),
@@ -562,7 +730,8 @@
                 own_forward,
                 other_forward,
             )
-        returned = exchange(separator(stage, 0, exchange(send)))
+            reply = separator(stage, 0, exchange(send))
+        returned = exchange(reply)
         bases = [] if base is None else [base]
 
         def middle(*refs, stage=stage, count=len(bases)):

time: 361 us -> 340 us (0.942)
  starting transfers between devices: 60.9 us -> 50.9 us
  Pallas kernels: 53.8 us -> 47.5 us
  waiting for transfers between devices: 27.8 us -> 33 us
  local copies, waits for them, and re-layouts: 15.1 us -> 9.98 us
    pallas_call x8 -> x7, Pallas kernels: 17.5 us -> 9.82 us  [separator(): call(functools.partial(separator_kernel, stage, step), slot_shape, [smem]...]
    ppermute x8, starting transfers between devices: 36.7 us -> 30.5 us  [across_cores(): lax.ppermute(value, 'layer', [(index, index ^ 1) for index in range(layer...]
    all_to_all x3 -> x2, starting transfers between devices: 19.1 us -> 14.5 us  [exchange(): lax.all_to_all(value, 'front', split_axis=0, concat_axis=0, tiled=True)]
    ppermute x8, waiting for transfers between devices: 3.92 us -> 8.03 us  [across_cores(): lax.ppermute(value, 'layer', [(index, index ^ 1) for index in range(layer...]
    unnamed x40 -> x50, local copies, waits for them, and re-layouts: 13.1 us -> 9.98 us
    all_to_all x3 -> x2, waiting for transfers between devices: 14.8 us -> 15.5 us  [exchange(): lax.all_to_all(value, 'front', split_axis=0, concat_axis=0, tiled=True)]
  transfers between devices with their start and end apart: 14 -> 13, of which waited for: 9 -> 9; matrix products, arithmetic and copies ran while one was open for 1% -> 0% of each run, Pallas kernels for 2% -> 1%
where the time goes in v2:
time: 340 us; the launch traced here: 339 us
  blocking collectives  196 us (58%)
  starting transfers between devices  50.9 us (15%)
  Pallas kernels  47.5 us (14%)
  waiting for transfers between devices  33 us (10%)
  local copies, waits for them, and re-layouts  9.98 us (3%)
    all_to_all x14, blocking collectives, exchange(): lax.all_to_all(value, 'front', split_axis=0, concat_axis=0, tiled=True)  196 us
    ppermute x8, starting transfers between devices, across_cores(): lax.ppermute(value, 'layer', [(index, index ^ 1) for index in range(layer...  30.5 us
    all_to_all x2, waiting for transfers between devices, exchange(): lax.all_to_all(value, 'front', split_axis=0, concat_axis=0, tiled=True)  15.5 us
    all_to_all x2, starting transfers between devices, exchange(): lax.all_to_all(value, 'front', split_axis=0, concat_axis=0, tiled=True)  14.5 us
    pallas_call x4, Pallas kernels, body(): call(middle, (field_shape, slot_shape, field_shape), [smem] * 3 + [vmem]...  10.4 us
    unnamed x50, local copies, waits for them, and re-layouts  9.98 us
    pallas_call x7, Pallas kernels, separator(): call(functools.partial(separator_kernel, stage, step), slot_shape, [smem]...  9.82 us
    ppermute x3, waiting for transfers between devices, to_next_stage(): return lax.ppermute(value, 'layer', pairs)  9.49 us
  transfers between devices with their start and end apart: 13, of which 9 were waited for; matrix products, arithmetic and copies ran while one was open for 0% of the time, Pallas kernels for 1%

profile of v2, /device:TPU:1, one launch (start us, length us, event | category | flops | bytes accessed | tf_op | source)
XLA Modules:
  0.0 338.6 jit_solution(6761098157929999126)
XLA Ops:
  0.6 3.4 %shard_map.104 = (f32[2,16,8,128]{3,2,1,0:T(8,128)}, f32[2,16,8,128]{3,2,1,0:T(8,128)}, f32[2,256,128]{2,1,0:T(8,128)}, f32[2,256,128]{2,1,0:T(8,128)}) custom-call(s32[1]{0:T(128)} %bitcast.place_ref.refs_0_, f32[2,32,256]{2,1,0:T(8,128)} %bitcast.31, f32[2,32,256]{2,1,0:T(8,128)} %bitcast.32, f32[2,256,256]{2,1,0:T(8,128)} %bitcast.27, f32[2,512,256]{2,1,0:T(8,128)} %bitcast.25), custom_call_target="tpu_custom_call" | custom-call | flops 600000000 | bytes 2500000 | tf_op jit(solution)/shard_map/pallas_call | solution.py:635
  4.1 5.2 %shard_map.107 = (f32[2,768,256]{2,1,0:T(8,128)}, f32[2,256,512]{2,1,0:T(8,128)}) custom-call(f32[2,16,8,128]{3,2,1,0:T(8,128)} %get-tuple-element.43.after_ref, f32[2,256,256]{2,1,0:T(8,128)} %bitcast.28, f32[2,512,256]{2,1,0:T(8,128)} %bitcast.26, f32[2,128,256]{2,1,0:T(8,128)} %bitcast.29, f32[2,128,256]{2,1,0:T(8,128)} %bitcast.30), custom_call_target="tpu_custom_call" | custom-call | flops 4000000000 | bytes 5000000 | tf_op jit(solution)/shard_map/pallas_call | solution.py:652
  9.3 3.3 collective-permute-start.6
  18.8 9.4 %all-to-all-start = ((f32[32,24,128]{2,1,0:T(8,128)}), f32[32,24,128]{2,1,0:T(8,128)}, u32[]{:S(2)}, u32[]{:S(2)}) async-start(f32[32,24,128]{2,1,0:T(8,128)} %copy-done.20), calls=%async_computation | async-start | bytes 786432 | tf_op jit(solution)/shard_map/all_to_all | solution.py:598
  33.0 9.2 %all-to-all-done.arrived_ref = f32[32,24,128]{2,1,0:T(8,128)} async-done(((f32[32,24,128]{2,1,0:T(8,128)}), f32[32,24,128]{2,1,0:T(8,128)}, u32[]{:S(2)}, u32[]{:S(2)}) %all-to-all-start) | async-done | bytes 393248 | tf_op jit(solution)/shard_map/all_to_all | solution.py:598
  47.8 5.0 %all-to-all-start.1 = ((f32[64,8,128]{2,1,0:T(8,128)}), f32[64,8,128]{2,1,0:T(8,128)}, u32[]{:S(2)}, u32[]{:S(2)}) async-start(f32[64,8,128]{2,1,0:T(8,128)} %copy-done.21), calls=%async_computation.1 | async-start | bytes 524288 | tf_op jit(solution)/shard_map/all_to_all | solution.py:598
  56.9 6.3 %all-to-all-done.1.refs_3_ = f32[64,8,128]{2,1,0:T(8,128)} async-done(((f32[64,8,128]{2,1,0:T(8,128)}), f32[64,8,128]{2,1,0:T(8,128)}, u32[]{:S(2)}, u32[]{:S(2)}) %all-to-all-start.1) | async-done | bytes 262176 | tf_op jit(solution)/shard_map/all_to_all | solution.py:598
  70.7 15.0 %all_to_all.80.arrived_ref = f32[64,8,128]{2,1,0:T(8,128)S(1)} all-to-all(f32[64,8,128]{2,1,0:T(8,128)S(1)} %get-tuple-element.54), channel_id=1, replica_groups=mesh['layer'=8,'front'=32] {'front'}, dimensions={0} | all-to-all | bytes 524288 | tf_op jit(solution)/shard_map/all_to_all | solution.py:598
  87.1 14.2 %all_to_all.81.returned_ref = f32[64,8,128]{2,1,0:T(8,128)S(1)} all-to-all(f32[64,8,128]{2,1,0:T(8,128)S(1)} %shard_map.109), channel_id=1, replica_groups=mesh['layer'=8,'front'=32] {'front'}, dimensions={0} | all-to-all | bytes 524288 | tf_op jit(solution)/shard_map/all_to_all | solution.py:598
  102.8 3.9 %collective-permute-start.7 = (f32[4,8,128]{2,1,0:T(8,128)S(1)}, f32[4,8,128]{2,1,0:T(8,128)S(1)}, u32[]{:S(2)}, u32[]{:S(2)}) collective-permute-start(f32[4,8,128]{2,1,0:T(8,128)S(1)} %get-tuple-element.57), channel_id=1, source_target_pairs={{0,64},{32,96},{192,128},{224,160},{1,65},{33,97},{193,129},{225,1... | collective-permute-start | bytes 49160 | tf_op jit(solution)/shard_map/ppermute | solution.py:604
  108.8 13.8 %all_to_all.82.arrived_ref = f32[64,8,128]{2,1,0:T(8,128)S(1)} all-to-all(f32[64,8,128]{2,1,0:T(8,128)S(1)} %get-tuple-element.58), channel_id=1, replica_groups=mesh['layer'=8,'front'=32] {'front'}, dimensions={0} | all-to-all | bytes 524288 | tf_op jit(solution)/shard_map/all_to_all | solution.py:598
  124.1 13.8 %all_to_all.83.refs_3_ = f32[64,8,128]{2,1,0:T(8,128)S(1)} all-to-all(f32[64,8,128]{2,1,0:T(8,128)S(1)} %shard_map.112), channel_id=1, replica_groups=mesh['layer'=8,'front'=32] {'front'}, dimensions={0} | all-to-all | bytes 524288 | tf_op jit(solution)/shard_map/all_to_all | solution.py:598
  140.3 13.8 %all_to_all.84.arrived_ref = f32[64,8,128]{2,1,0:T(8,128)S(1)} all-to-all(f32[64,8,128]{2,1,0:T(8,128)S(1)} %get-tuple-element.61), channel_id=1, replica_groups=mesh['layer'=8,'front'=32] {'front'}, dimensions={0} | all-to-all | bytes 524288 | tf_op jit(solution)/shard_map/all_to_all | solution.py:598
  155.5 13.9 %all_to_all.85.returned_ref = f32[64,8,128]{2,1,0:T(8,128)S(1)} all-to-all(f32[64,8,128]{2,1,0:T(8,128)S(1)} %shard_map.114), channel_id=1, replica_groups=mesh['layer'=8,'front'=32] {'front'}, dimensions={0} | all-to-all | bytes 524288 | tf_op jit(solution)/shard_map/all_to_all | solution.py:598
  173.6 13.8 %all_to_all.86.arrived_ref = f32[64,8,128]{2,1,0:T(8,128)S(1)} all-to-all(f32[64,8,128]{2,1,0:T(8,128)S(1)} %get-tuple-element.65), channel_id=1, replica_groups=mesh['layer'=8,'front'=32] {'front'}, dimensions={0} | all-to-all | bytes 524288 | tf_op jit(solution)/shard_map/all_to_all | solution.py:598
  188.8 13.6 %all_to_all.87.refs_3_ = f32[64,8,128]{2,1,0:T(8,128)S(1)} all-to-all(f32[64,8,128]{2,1,0:T(8,128)S(1)} %shard_map.117), channel_id=1, replica_groups=mesh['layer'=8,'front'=32] {'front'}, dimensions={0} | all-to-all | bytes 524288 | tf_op jit(solution)/shard_map/all_to_all | solution.py:598
  204.8 13.7 %all_to_all.88.arrived_ref = f32[64,8,128]{2,1,0:T(8,128)S(1)} all-to-all(f32[64,8,128]{2,1,0:T(8,128)S(1)} %get-tuple-element.68), channel_id=1, replica_groups=mesh['layer'=8,'front'=32] {'front'}, dimensions={0} | all-to-all | bytes 524288 | tf_op jit(solution)/shard_map/all_to_all | solution.py:598
  219.9 15.1 %all_to_all.89.returned_ref = f32[64,8,128]{2,1,0:T(8,128)S(1)} all-to-all(f32[64,8,128]{2,1,0:T(8,128)S(1)} %shard_map.119), channel_id=1, replica_groups=mesh['layer'=8,'front'=32] {'front'}, dimensions={0} | all-to-all | bytes 524288 | tf_op jit(solution)/shard_map/all_to_all | solution.py:598
  238.7 8.6 %collective-permute-done.9.trace_ref = f32[4,8,128]{2,1,0:T(8,128)S(1)} collective-permute-done((f32[4,8,128]{2,1,0:T(8,128)S(1)}, f32[4,8,128]{2,1,0:T(8,128)S(1)}, u32[]{:S(2)}, u32[]{:S(2)}) %collective-permute-start.9) | collective-permute-done | bytes 16416 | tf_op jit(solution)/shard_map/ppermute | solution.py:604
  248.5 14.2 %all_to_all.90.arrived_ref = f32[64,8,128]{2,1,0:T(8,128)S(1)} all-to-all(f32[64,8,128]{2,1,0:T(8,128)S(1)} %get-tuple-element.72), channel_id=1, replica_groups=mesh['layer'=8,'front'=32] {'front'}, dimensions={0} | all-to-all | bytes 524288 | tf_op jit(solution)/shard_map/all_to_all | solution.py:598
  264.1 13.8 %all_to_all.91.refs_3_ = f32[64,8,128]{2,1,0:T(8,128)S(1)} all-to-all(f32[64,8,128]{2,1,0:T(8,128)S(1)} %shard_map.122), channel_id=1, replica_groups=mesh['layer'=8,'front'=32] {'front'}, dimensions={0} | all-to-all | bytes 524288 | tf_op jit(solution)/shard_map/all_to_all | solution.py:598
  280.3 13.8 %all_to_all.92.arrived_ref = f32[64,8,128]{2,1,0:T(8,128)S(1)} all-to-all(f32[64,8,128]{2,1,0:T(8,128)S(1)} %get-tuple-element.75), channel_id=1, replica_groups=mesh['layer'=8,'front'=32] {'front'}, dimensions={0} | all-to-all | bytes 524288 | tf_op jit(solution)/shard_map/all_to_all | solution.py:598
  295.5 13.8 %all_to_all.93.returned_ref = f32[64,8,128]{2,1,0:T(8,128)S(1)} all-to-all(f32[64,8,128]{2,1,0:T(8,128)S(1)} %shard_map.124), channel_id=1, replica_groups=mesh['layer'=8,'front'=32] {'front'}, dimensions={0} | all-to-all | bytes 524288 | tf_op jit(solution)/shard_map/all_to_all | solution.py:598
  313.2 23.8 %collective-permute-start.10 = (f32[2,2,16,256]{3,2,1,0:T(8,128)S(1)}, f32[2,2,16,256]{3,2,1,0:T(8,128)S(1)}, u32[]{:S(2)}, u32[]{:S(2)}) collective-permute-start(f32[2,2,16,256]{3,2,1,0:T(8,128)S(1)} %get-tuple-element.79), channel_id=1, source_target_pairs={{0,32},{32,0},{64,96},{96,64},{128,160},{160,128},{192,224},{224,1... | collective-permute-start | bytes 196616 | tf_op jit(solution)/shard_map/ppermute | solution.py:594
  (90 shorter events, 63.1 us)
Async XLA Ops:
  4.1 11.8 %copy-start.16 = (f32[2,16,8,128]{3,2,1,0:T(8,128)S(1)}, f32[2,16,8,128]{3,2,1,0:T(8,128)}, u32[]{:S(2)}) copy-start(f32[2,16,8,128]{3,2,1,0:T(8,128)} %get-tuple-element.42.own_u_ref.refs_4_.refs_5_) | copy-start | bytes 393220
  4.1 60.3 %copy-start.12 = (f32[2,256,128]{2,1,0:T(8,128)S(1)}, f32[2,256,128]{2,1,0:T(8,128)}, u32[]{:S(2)}) copy-start(f32[2,256,128]{2,1,0:T(8,128)} %get-tuple-element.48.refs_6_.own_y_ref.refs_7_) | copy-start | bytes 786436
  9.3 55.1 %copy-start = (f32[2,768,256]{2,1,0:T(8,128)S(1)}, f32[2,768,256]{2,1,0:T(8,128)}, u32[]{:S(2)}) copy-start(f32[2,768,256]{2,1,0:T(8,128)} %get-tuple-element.51.refs_10_.own_forward_ref.refs_11_) | copy-start | bytes 4718596
  9.3 53.9 %collective-permute-start.6 = (f32[2,768,256]{2,1,0:T(8,128)}, f32[2,768,256]{2,1,0:T(8,128)S(1)}, u32[]{:S(2)}, u32[]{:S(2)}) collective-permute-start(f32[2,768,256]{2,1,0:T(8,128)} %get-tuple-element.51.refs_10_.own_forward_ref.refs_11_), channel_id=1, source_target_pairs={{0,32},{32,0},{64,96},{96,64},{128,160},{160,128},{192,224},{224,1... | collective-permute-start | bytes 4718600 | tf_op jit(solution)/shard_map/ppermute | solution.py:594
  12.6 3.2 collective-permute-start.2
  12.7 3.0 collective-permute-start
  13.1 2.7 collective-permute-start.1
  18.8 23.4 %all-to-all-start = ((f32[32,24,128]{2,1,0:T(8,128)}), f32[32,24,128]{2,1,0:T(8,128)}, u32[]{:S(2)}, u32[]{:S(2)}) async-start(f32[32,24,128]{2,1,0:T(8,128)} %copy-done.20), calls=%async_computation | async-start | bytes 786432 | tf_op jit(solution)/shard_map/all_to_all | solution.py:598
  28.3 28.6 %collective-permute-start.5 = (f32[2,256,512]{2,1,0:T(8,128)}, f32[2,256,512]{2,1,0:T(8,128)}, u32[]{:S(2)}, u32[]{:S(2)}) collective-permute-start(f32[2,256,512]{2,1,0:T(8,128)} %get-tuple-element.50.refs_8_.own_back_ref.refs_9_), channel_id=1, source_target_pairs={{0,32},{32,0},{64,96},{96,64},{128,160},{160,128},{192,224},{224,1... | collective-permute-start | bytes 3145736 | tf_op jit(solution)/shard_map/ppermute | solution.py:594
  29.0 3.2 collective-permute-start.3
  47.8 15.4 %all-to-all-start.1 = ((f32[64,8,128]{2,1,0:T(8,128)}), f32[64,8,128]{2,1,0:T(8,128)}, u32[]{:S(2)}, u32[]{:S(2)}) async-start(f32[64,8,128]{2,1,0:T(8,128)} %copy-done.21), calls=%async_computation.1 | async-start | bytes 524288 | tf_op jit(solution)/shard_map/all_to_all | solution.py:598
  52.8 3.3 collective-permute-start.4
  67.4 18.2 %copy-start.8 = (f32[1,1,2,256,256]{4,3,2,1,0:T(8,128)S(1)}, f32[1,1,2,256,256]{4,3,2,1,0:T(8,128)}, u32[]{:S(2)}) copy-start(f32[1,1,2,256,256]{4,3,2,1,0:T(8,128)} %param.13) | copy-start | bytes 1572868
  67.4 18.2 %copy-start.11 = (f32[2,256,256]{2,1,0:T(8,128)S(1)}, f32[2,256,256]{2,1,0:T(8,128)}, u32[]{:S(2)}) copy-start(f32[2,256,256]{2,1,0:T(8,128)} %copy-done.9) | copy-start | bytes 1572868
  70.7 30.6 %copy-start.6 = (f32[2,256,512]{2,1,0:T(8,128)S(1)}, f32[2,256,512]{2,1,0:T(8,128)}, u32[]{:S(2)}) copy-start(f32[2,256,512]{2,1,0:T(8,128)} %get-tuple-element.50.refs_8_.own_back_ref.refs_9_) | copy-start | bytes 3145732
  87.1 20.6 %copy-start.2 = (f32[2,768,256]{2,1,0:T(8,128)S(1)}, f32[2,768,256]{2,1,0:T(8,128)}, u32[]{:S(2)}) copy-start(f32[2,768,256]{2,1,0:T(8,128)} %copy-done.1) | copy-start | bytes 4718596
  87.1 20.5 %copy-start.15 = (f32[2,256,128]{2,1,0:T(8,128)S(1)}, f32[2,256,128]{2,1,0:T(8,128)}, u32[]{:S(2)}) copy-start(f32[2,256,128]{2,1,0:T(8,128)} %copy-done.13) | copy-start | bytes 786436
  87.1 20.5 %copy-start.19 = (f32[2,16,8,128]{3,2,1,0:T(8,128)S(1)}, f32[2,16,8,128]{3,2,1,0:T(8,128)}, u32[]{:S(2)}) copy-start(f32[2,16,8,128]{3,2,1,0:T(8,128)} %copy-done.17) | copy-start | bytes 393220
  102.8 4.8 %collective-permute-start.7 = (f32[4,8,128]{2,1,0:T(8,128)S(1)}, f32[4,8,128]{2,1,0:T(8,128)S(1)}, u32[]{:S(2)}, u32[]{:S(2)}) collective-permute-start(f32[4,8,128]{2,1,0:T(8,128)S(1)} %get-tuple-element.57), channel_id=1, source_target_pairs={{0,64},{32,96},{192,128},{224,160},{1,65},{33,97},{193,129},{225,1... | collective-permute-start | bytes 49160 | tf_op jit(solution)/shard_map/ppermute | solution.py:604
  155.4 17.0 %copy-start.3 = (f32[2,768,256]{2,1,0:T(8,128)S(1)}, f32[2,768,256]{2,1,0:T(8,128)}, u32[]{:S(2)}) copy-start(f32[2,768,256]{2,1,0:T(8,128)} %copy-done.1) | copy-start | bytes 4718596
  171.7 0.7 collective-permute-start.8
  219.9 27.4 %copy-start.4 = (f32[2,768,256]{2,1,0:T(8,128)S(1)}, f32[2,768,256]{2,1,0:T(8,128)}, u32[]{:S(2)}) copy-start(f32[2,768,256]{2,1,0:T(8,128)} %copy-done.1) | copy-start | bytes 4718596
  237.4 9.9 %collective-permute-start.9 = (f32[4,8,128]{2,1,0:T(8,128)S(1)}, f32[4,8,128]{2,1,0:T(8,128)S(1)}, u32[]{:S(2)}, u32[]{:S(2)}) collective-permute-start(f32[4,8,128]{2,1,0:T(8,128)S(1)} %get-tuple-element.71), channel_id=1, source_target_pairs={{128,192},{160,224},{64,0},{96,32},{129,193},{161,225},{65,1},{97,... | collective-permute-start | bytes 49160 | tf_op jit(solution)/shard_map/ppermute | solution.py:604
  313.2 24.7 %collective-permute-start.10 = (f32[2,2,16,256]{3,2,1,0:T(8,128)S(1)}, f32[2,2,16,256]{3,2,1,0:T(8,128)S(1)}, u32[]{:S(2)}, u32[]{:S(2)}) collective-permute-start(f32[2,2,16,256]{3,2,1,0:T(8,128)S(1)} %get-tuple-element.79), channel_id=1, source_target_pairs={{0,32},{32,0},{64,96},{96,64},{128,160},{160,128},{192,224},{224,1... | collective-permute-start | bytes 196616 | tf_op jit(solution)/shard_map/ppermute | solution.py:594
  (14 other events, 36.2 us)

commit v3 on v2

--- a/solution.py
+++ b/solution.py
@@ -55,6 +55,16 @@
     second_high, second_low = halves(second)
     both = dot(first_high, jnp.concatenate([second_high, second_low], axis=1))
     return both[:, :LANES] + both[:, LANES:] + dot(first_low, second_high)
+
+
+def stacked(value):
+    return jnp.concatenate(halves(value), axis=0)
+
+
+def stacked_product(first, second):
+    rows = first.shape[0] // 2
+    both = dot(first, jnp.concatenate(halves(second), axis=1))
+    return (both[:rows, :LANES] + both[:rows, LANES:]) + (both[rows:, :LANES] + both[rows:, LANES:])
 
 
 def complex_pair(first, second, dims=NN):
@@ -182,12 +192,16 @@
     coupling_hbm,
     top_hbm,
     bottom_hbm,
+    own_sep_hbm,
+    other_sep_hbm,
     forward_ref,
     back_ref,
+    seps_ref,
     leaf_ref,
     coupling_ref,
     top_ref,
     bottom_ref,
+    sep_ref,
     semaphores,
 ):
     copies = [
@@ -198,6 +212,8 @@
                 (top_hbm, top_ref),
                 (bottom_hbm, bottom_ref),
                 (coupling_hbm, coupling_ref),
+                (own_sep_hbm, sep_ref.at[0]),
+                (other_sep_hbm, sep_ref.at[1]),
             )
         )
     ]
@@ -222,6 +238,55 @@
     back = complex_pair(leaf, coupling, NT)
     back_ref[0] = back[0]
     back_ref[1] = back[1]
+    for side in range(2):
+        copies[4 + side].wait()
+        for part in range(2):
+            seps_ref[side, part] = stacked(sep_ref[side, part])
+
+
+def gather_kernel(
+    own_u_hbm,
+    other_u_hbm,
+    own_y_hbm,
+    other_y_hbm,
+    own_back_hbm,
+    other_back_hbm,
+    own_forward_hbm,
+    other_forward_hbm,
+    u_ref,
+    y_ref,
+    backs_ref,
+    forwards_ref,
+    back_ref,
+    forward_ref,
+    semaphores,
+):
+    copies = [
+        pltpu.make_async_copy(source, target, semaphores.at[index])
+        for index, (source, target) in enumerate(
+            (
+                (own_back_hbm, back_ref.at[0]),
+                (own_forward_hbm, forward_ref.at[0]),
+                (other_back_hbm, back_ref.at[1]),
+                (other_forward_hbm, forward_ref.at[1]),
+                (own_u_hbm, u_ref.at[0]),
+                (other_u_hbm, u_ref.at[1]),
+                (own_y_hbm, y_ref.at[0]),
+                (other_y_hbm, y_ref.at[1]),
+            )
+        )
+    ]
+    for copy in copies:
+        copy.start()
+    for side in range(2):
+        copies[2 * side].wait()
+        for part in range(2):
+            backs_ref[side, part] = stacked(back_ref[side, part])
+        copies[2 * side + 1].wait()
+        for sweep in range(2):
+            forwards_ref[side, sweep] = stacked(forward_ref[side, sweep])
+    for copy in copies[4:]:
+        copy.wait()
 
 
 def stage_place(place_ref, stage):
@@ -230,16 +295,6 @@
     sweep = jnp.where(row == stage, 0, 1)
     first = jnp.where(sweep == core, 0, 1)
     return sweep, first
-
-
-def start_either(choice, first_ref, second_ref, target_ref, semaphore):
-    @pl.when(choice == 0)
-    def _():
-        pltpu.make_async_copy(first_ref, target_ref, semaphore).start()
-
-    @pl.when(choice != 0)
-    def _():
-        pltpu.make_async_copy(second_ref, target_ref, semaphore).start()
 
 
 def wait_for(source_ref, target_ref, semaphore):
@@ -298,7 +353,7 @@
         send_ref[slot // CAP, pl.ds(row, 8), :] = packed[block]
 
 
-def separator_solve(choice, offsets_ref, arrived, reply_ref, sep, even_ref, odd_ref, solved_ref):
+def separator_solve(choice, offsets_ref, arrived, seps_ref, reply_ref, even_ref, odd_ref, solved_ref):
     leaves = reply_ref.shape[0] // CAP
     even_ref[...] = jnp.zeros_like(even_ref)
     odd_ref[...] = jnp.zeros_like(odd_ref)
@@ -309,8 +364,9 @@
             places.append(place)
             total_ref[place] = total_ref[place] + arrived(leaf, rank)
     rhs, rhs_turned = unpack_both(even_ref[:QB] + odd_ref[:QB])
-    sep_ref = sep()
-    solved = narrow_product(sep_ref[0], rhs) + narrow_product(sep_ref[1], rhs_turned)
+    solved = stacked_product(seps_ref[choice, 0], rhs) + stacked_product(
+        seps_ref[choice, 1], rhs_turned
+    )
     solved_ref[:QB] = pack(solved)
     solved_ref[QB] = jnp.zeros((8, LANES), f32)
     for slot, place in enumerate(places):
@@ -318,95 +374,87 @@
 
 
 def separator_kernel(
-    stage,
-    step,
-    place_ref,
-    offsets_ref,
-    arrived_ref,
-    own_sep_ref,
-    other_sep_ref,
-    reply_ref,
-    sep_ref,
-    even_ref,
-    odd_ref,
-    solved_ref,
-    semaphore,
+    stage, step, place_ref, offsets_ref, arrived_ref, seps_ref, reply_ref, *scratch
 ):
     sweep, first = stage_place(place_ref, stage)
-    choice = first if step == 0 else 1 - first
-    start_either(choice, own_sep_ref, other_sep_ref, sep_ref, semaphore)
-
-    def sep():
-        wait_for(own_sep_ref, sep_ref, semaphore)
-        return sep_ref
-
     separator_solve(
-        choice,
+        first if step == 0 else 1 - first,
         offsets_ref,
         lambda leaf, rank: arrived_ref[CAP * leaf + rank],
+        seps_ref,
         reply_ref,
-        sep,
-        even_ref,
-        odd_ref,
-        solved_ref,
+        *scratch,
     )
 
 
 def first_separator_kernel(
     place_ref,
     arrived_ref,
-    own_sep_ref,
-    other_sep_ref,
+    seps_ref,
+    forward_in_hbm,
+    back_in_hbm,
     offsets_ref,
     reply_ref,
-    sep_ref,
-    even_ref,
-    odd_ref,
-    solved_ref,
+    forward_out_hbm,
+    back_out_hbm,
     notes_ref,
-    semaphores,
+    semaphore,
+    *scratch,
 ):
     sweep, first = stage_place(place_ref, 0)
-    start_either(first, own_sep_ref, other_sep_ref, sep_ref, semaphores.at[0])
     leaves = arrived_ref.shape[0]
     notes = arrived_ref[:, CAP * 8, :]
     whole = jnp.concatenate([notes, jnp.zeros((LANES - leaves, LANES), f32)], axis=0)
     notes_ref[...] = whole.T[:8].astype(jnp.int32)
-    copy = pltpu.make_async_copy(notes_ref, offsets_ref, semaphores.at[1])
+    copy = pltpu.make_async_copy(notes_ref, offsets_ref, semaphore)
     copy.start()
     copy.wait()
-
-    def sep():
-        wait_for(own_sep_ref, sep_ref, semaphores.at[0])
-        return sep_ref
-
     separator_solve(
         first,
         offsets_ref,
         lambda leaf, rank: arrived_ref[leaf, 8 * rank : 8 * rank + 8, :],
+        seps_ref,
         reply_ref,
-        sep,
-        even_ref,
-        odd_ref,
-        solved_ref,
-    )
-
-
-def leaf_finish(choice, own_slots_ref, other_slots_ref, returned_ref, back_ref, wait, base):
+        *scratch,
+    )
+
+
+def leaf_finish(choice, own_slots_ref, other_slots_ref, returned_ref, backs_ref, base):
     blocks = []
     for block in range(NB):
         slot = jnp.where(choice == 0, own_slots_ref[block], other_slots_ref[block])
         blocks.append(returned_ref[slot])
     mine, mine_turned = unpack_both(jnp.stack(blocks, axis=0))
-    wait()
-    return base + narrow_product(back_ref[0], mine) + narrow_product(back_ref[1], mine_turned)
-
-
-def leaf_begin(sweep, choice, trace, trace_turned, forward, u_refs, y_refs, slots_refs, send_ref, base_ref):
-    driven = narrow_product(forward, jnp.concatenate([trace, trace_turned], axis=0))
-    packed = pack(driven[: NB * RB]) + jnp.where(choice == 0, u_refs[0][sweep], u_refs[1][sweep])
-    send_blocks(choice, slots_refs[0], slots_refs[1], packed, send_ref)
-    base_ref[...] = driven[NB * RB :] + jnp.where(choice == 0, y_refs[0][sweep], y_refs[1][sweep])
+    return (
+        base
+        + stacked_product(backs_ref[choice, 0], mine)
+        + stacked_product(backs_ref[choice, 1], mine_turned)
+    )
+
+
+def leaf_begin(
+    sweep,
+    choice,
+    trace,
+    trace_turned,
+    own_slots_ref,
+    other_slots_ref,
+    u_ref,
+    y_ref,
+    forwards_ref,
+    send_ref,
+    base_ref,
+):
+    driven = stacked_product(
+        forwards_ref[choice, sweep], jnp.concatenate([trace, trace_turned], axis=0)
+    )
+    packed = pack(driven[: NB * RB]) + u_ref[choice, sweep]
+    send_blocks(choice, own_slots_ref, other_slots_ref, packed, send_ref)
+    base_ref[...] = driven[NB * RB :] + y_ref[choice, sweep]
+
+
+def trace_rows(sweep, field_ref):
+    return field_ref[pl.ds(pl.multiple_of((1 - sweep) * TR, TR), TR), :]
 
 
 def middle_kernel(
@@ -414,53 +462,32 @@
     place_ref,
     own_slots_ref,
     other_slots_ref,
+    u_ref,
+    y_ref,
+    forwards_ref,
+    backs_ref,
     returned_ref,
     base_refs,
-    own_u_ref,
-    other_u_ref,
-    own_y_ref,
-    other_y_ref,
-    own_back_ref,
-    other_back_ref,
-    own_forward_ref,
-    other_forward_ref,
     field_ref,
     send_ref,
     next_base_ref,
-    back_ref,
-    forward_ref,
-    semaphores,
 ):
     sweep, first = stage_place(place_ref, stage)
-    second = 1 - first
-    start_either(first, own_back_ref, other_back_ref, back_ref, semaphores.at[0])
-    start_either(
-        second, own_forward_ref.at[sweep], other_forward_ref.at[sweep], forward_ref, semaphores.at[1]
-    )
-    if len(base_refs) == 1:
-        base = base_refs[0][...]
-    else:
-        base = jnp.where(first == 0, own_y_ref[sweep], other_y_ref[sweep])
+    base = base_refs[0][...] if base_refs else y_ref[first, sweep]
     field_ref[...] = leaf_finish(
-        first,
+        first, own_slots_ref, other_slots_ref, returned_ref, backs_ref, base
+    )
+    trace = trace_rows(sweep, field_ref)
+    leaf_begin(
+        sweep,
+        1 - first,
+        trace,
+        turned(trace),
         own_slots_ref,
         other_slots_ref,
-        returned_ref,
-        back_ref,
-        lambda: wait_for(own_back_ref, back_ref, semaphores.at[0]),
-        base,
-    )
-    trace = field_ref[pl.ds(pl.multiple_of((1 - sweep) * TR, TR), TR), :]
-    wait_for(own_forward_ref.at[0], forward_ref, semaphores.at[1])
-    leaf_begin(
-        sweep,
-        second,
-        trace,
-        turned(trace),
-        forward_ref[...],
-        (own_u_ref, other_u_ref),
-        (own_y_ref, other_y_ref),
-        (own_slots_ref, other_slots_ref),
+        u_ref,
+        y_ref,
+        forwards_ref,
         send_ref,
         next_base_ref,
     )
@@ -471,28 +498,17 @@
     place_ref,
     own_slots_ref,
     other_slots_ref,
+    backs_ref,
     returned_ref,
     base_ref,
-    own_back_ref,
-    other_back_ref,
     field_ref,
     trace_ref,
-    back_ref,
-    semaphore,
 ):
     sweep, first = stage_place(place_ref, stage)
-    second = 1 - first
-    start_either(second, own_back_ref, other_back_ref, back_ref, semaphore)
     field_ref[...] = leaf_finish(
-        second,
-        own_slots_ref,
-        other_slots_ref,
-        returned_ref,
-        back_ref,
-        lambda: wait_for(own_back_ref, back_ref, semaphore),
-        base_ref[...],
-    )
-    trace_ref[...] = pack(field_ref[pl.ds(pl.multiple_of((1 - sweep) * TR, TR), TR), :])
+        1 - first, own_slots_ref, other_slots_ref, returned_ref, backs_ref, base_ref[...]
+    )
+    trace_ref[...] = pack(trace_rows(sweep, field_ref))
 
 
 def enter_kernel(
@@ -500,33 +516,25 @@
     place_ref,
     own_slots_ref,
     other_slots_ref,
+    u_ref,
+    y_ref,
+    forwards_ref,
     trace_ref,
-    own_u_ref,
-    other_u_ref,
-    own_y_ref,
-    other_y_ref,
-    own_forward_ref,
-    other_forward_ref,
     send_ref,
     next_base_ref,
-    forward_ref,
-    semaphore,
 ):
     sweep, first = stage_place(place_ref, stage)
-    start_either(
-        first, own_forward_ref.at[sweep], other_forward_ref.at[sweep], forward_ref, semaphore
-    )
     trace, trace_turned = unpack_both(trace_ref[...])
-    wait_for(own_forward_ref.at[0], forward_ref, semaphore)
     leaf_begin(
         sweep,
         first,
         trace,
         trace_turned,
-        forward_ref[...],
-        (own_u_ref, other_u_ref),
-        (own_y_ref, other_y_ref),
-        (own_slots_ref, other_slots_ref),
+        own_slots_ref,
+        other_slots_ref,
+        u_ref,
+        y_ref,
+        forwards_ref,
         send_ref,
         next_base_ref,
     )
@@ -569,7 +577,9 @@
             ]
 
 
-def call(kernel, outs, in_specs, out_specs, scratch=(), cost=None, limit=VMEM_LIMIT):
+def call(
+    kernel, outs, in_specs, out_specs, scratch=(), cost=None, limit=VMEM_LIMIT, aliases=None
+):
     return pl.pallas_call(
         kernel,
         out_shape=outs,
@@ -578,6 +588,7 @@
         scratch_shapes=list(scratch),
         compiler_params=pltpu.CompilerParams(vmem_limit_bytes=limit),
         cost_estimate=cost,
+        input_output_aliases=aliases or {},
     )
 
 
@@ -649,62 +660,82 @@
     )(place, sources_down[0, 0], sources_up[0, 0], leaf, rows)
     other_u = across_cores(to_other_u)
 
-    own_forward, own_back = call(
-        operator_kernel,
-        (shape(2, NB * RB + P_SIZE, 2 * TR), shape(2, P_SIZE, NB * RB)),
-        [hbm] * 5,
-        (vmem,) * 2,
-        [
-            leaf_scratch,
-            rows_scratch,
-            inject_scratch,
-            inject_scratch,
-            pltpu.SemaphoreType.DMA((4,)),
-        ],
-        cost_of(4_000_000_000, 5_000_000),
-        ALMOST_ALL_VMEM,
-    )(to_other_u, leaf, rows, inject_top[0, 0], inject_bottom[0, 0])
-    other_y = across_cores(to_other_y)
-    other_back = across_cores(own_back)
-    other_forward = across_cores(own_forward)
-
     slot_shape = shape(slots, 8, LANES)
     field_shape = shape(P_SIZE, LANES)
     slots_shape = shape(NB, dtype=jnp.int32)
-    back_scratch = pltpu.VMEM((2, P_SIZE, NB * RB), f32)
-    forward_scratch = pltpu.VMEM((NB * RB + P_SIZE, 2 * TR), f32)
-    separator_scratch = [
-        pltpu.VMEM((2, Q, Q), f32),
-        pltpu.VMEM((QB + 1, 8, LANES), f32),
-        pltpu.VMEM((QB + 1, 8, LANES), f32),
-        pltpu.VMEM((QB + 1, 8, LANES), f32),
-    ]
-
     own_slots, other_slots, send = call(
         first_kernel,
         (slots_shape, slots_shape, shape(leaves, (CAP + 1) * 8, LANES)),
         [smem] * 5 + [vmem] * 2,
         (smem, smem, vmem),
     )(place, own_targets, other_targets, offsets[0, 0], other_offsets, own_u, other_u)
-    places, reply = call(
+    arrived = exchange(send)
+
+    own_forward, own_back, seps = call(
+        operator_kernel,
+        (
+            shape(2, NB * RB + P_SIZE, 2 * TR),
+            shape(2, P_SIZE, NB * RB),
+            shape(2, 2, 2 * Q, Q, dtype=bf16),
+        ),
+        [hbm] * 7,
+        (vmem,) * 3,
+        [
+            leaf_scratch,
+            rows_scratch,
+            inject_scratch,
+            inject_scratch,
+            pltpu.VMEM((2, 2, Q, Q), f32),
+            pltpu.SemaphoreType.DMA((6,)),
+        ],
+        cost_of(4_000_000_000, 5_000_000),
+    )(send, leaf, rows, inject_top[0, 0], inject_bottom[0, 0], sep, other_sep)
+    separator_scratch = [pltpu.VMEM((QB + 1, 8, LANES), f32)] * 3
+    places, reply, own_forward, own_back = call(
         first_separator_kernel,
-        (shape(8, LANES, dtype=jnp.int32), slot_shape),
-        [smem, vmem, hbm, hbm],
-        (smem, vmem),
-        separator_scratch
-        + [pltpu.VMEM((8, LANES), jnp.int32), pltpu.SemaphoreType.DMA((2,))],
+        (
+            shape(8, LANES, dtype=jnp.int32),
+            slot_shape,
+            shape(*own_forward.shape),
+            shape(*own_back.shape),
+        ),
+        [smem, vmem, vmem, hbm, hbm],
+        (smem, vmem, hbm, hbm),
+        [pltpu.VMEM((8, LANES), jnp.int32), pltpu.SemaphoreType.DMA] + separator_scratch,
         cost_of(100_000_000, 1_100_000),
-    )(place, exchange(send), sep, other_sep)
+        aliases={3: 2, 4: 3},
+    )(place, arrived, seps, own_forward, own_back)
+    other_y = across_cores(to_other_y)
+    other_back = across_cores(own_back)
+    other_forward = across_cores(own_forward)
+
+    u, y, backs, forwards = call(
+        gather_kernel,
+        (
+            shape(2, 2, NB, 8, LANES),
+            shape(2, 2, P_SIZE, LANES),
+            shape(2, 2, 2 * P_SIZE, NB * RB, dtype=bf16),
+            shape(2, 2, 2 * (NB * RB + P_SIZE), 2 * TR, dtype=bf16),
+        ),
+        [hbm] * 8,
+        (vmem,) * 4,
+        [
+            pltpu.VMEM((2, 2, P_SIZE, NB * RB), f32),
+            pltpu.VMEM((2, 2, NB * RB + P_SIZE, 2 * TR), f32),
+            pltpu.SemaphoreType.DMA((8,)),
+        ],
+        cost_of(10_000_000, 12_000_000),
+    )(own_u, other_u, own_y, other_y, own_back, other_back, own_forward, other_forward)
 
     def separator(stage, step, arrived):
         return call(
             functools.partial(separator_kernel, stage, step),
             slot_shape,
-            [smem] * 2 + [vmem] + [hbm] * 2,
+            [smem] * 2 + [vmem] * 2,
             vmem,
-            separator_scratch + [pltpu.SemaphoreType.DMA],
+            separator_scratch,
             cost_of(100_000_000, 1_100_000),
-        )(place, places, arrived, sep, other_sep)
+        )(place, places, arrived, seps)
 
     fields = []
     base = None
@@ -714,62 +745,34 @@
             send, base = call(
                 functools.partial(enter_kernel, stage),
                 (slot_shape, field_shape),
-                [smem] * 3 + [vmem] * 5 + [hbm] * 2,
+                [smem] * 3 + [vmem] * 4,
                 (vmem, vmem),
-                [forward_scratch, pltpu.SemaphoreType.DMA],
-                cost_of(100_000_000, 2_000_000),
-            )(
-                place,
-                own_slots,
-                other_slots,
-                trace,
-                own_u,
-                other_u,
-                own_y,
-                other_y,
-                own_forward,
-                other_forward,
-            )
+                cost=cost_of(100_000_000, 2_000_000),
+            )(place, own_slots, other_slots, u, y, forwards, trace)
             reply = separator(stage, 0, exchange(send))
         returned = exchange(reply)
         bases = [] if base is None else [base]
 
         def middle(*refs, stage=stage, count=len(bases)):
-            head, rest = refs[:4], refs[4:]
+            head, rest = refs[:8], refs[8:]
             middle_kernel(stage, *head, rest[:count], *rest[count:])
 
         field, send, base = call(
             middle,
             (field_shape, slot_shape, field_shape),
-            [smem] * 3 + [vmem] * (1 + len(bases)) + [vmem] * 4 + [hbm] * 4,
+            [smem] * 3 + [vmem] * (5 + len(bases)),
             (vmem,) * 3,
-            [back_scratch, forward_scratch, pltpu.SemaphoreType.DMA((2,))],
-            cost_of(300_000_000, 3_000_000),
-        )(
-            place,
-            own_slots,
-            other_slots,
-            returned,
-            *bases,
-            own_u,
-            other_u,
-            own_y,
-            other_y,
-            own_back,
-            other_back,
-            own_forward,
-            other_forward,
-        )
+            cost=cost_of(300_000_000, 3_000_000),
+        )(place, own_slots, other_slots, u, y, forwards, backs, returned, *bases)
         fields.append(field)
         returned = exchange(separator(stage, 1, exchange(send)))
         field, trace = call(
             functools.partial(last_kernel, stage),
             (field_shape, shape(TR // RB, 8, LANES)),
-            [smem] * 3 + [vmem] * 2 + [hbm] * 2,
+            [smem] * 3 + [vmem] * 3,
             (vmem, vmem),
-            [back_scratch, pltpu.SemaphoreType.DMA],
-            cost_of(200_000_000, 2_000_000),
-        )(place, own_slots, other_slots, returned, base, own_back, other_back)
+            cost=cost_of(200_000_000, 2_000_000),
+        )(place, own_slots, other_slots, backs, returned, base)
         fields.append(field)
         if stage < 3:
             trace = to_next_stage(trace, stage)

time: 340 us -> 328 us (0.965)
  waiting for transfers between devices: 33 us -> 20.2 us
  blocking collectives: 196 us -> 204 us
  starting transfers between devices: 50.9 us -> 46.1 us
    all_to_all x14, blocking collectives: 196 us -> 204 us  [exchange(): lax.all_to_all(value, 'front', split_axis=0, concat_axis=0, tiled=True)]
    all_to_all x2, waiting for transfers between devices: 15.5 us -> 8.53 us  [exchange(): lax.all_to_all(value, 'front', split_axis=0, concat_axis=0, tiled=True)]
    ppermute x8, waiting for transfers between devices: 8.03 us -> 3.09 us  [across_cores(): lax.ppermute(value, 'layer', [(index, index ^ 1) for index in range(layer...]
    pallas_call x0 -> x1, Pallas kernels: none -> 4.8 us  [body(): call(gather_kernel, (shape(2, 2, NB, 8, LANES), shape(2, 2, P_SIZE, LANES...]
    pallas_call x4, Pallas kernels: 9.29 us -> 5.22 us  [body(): call(functools.partial(last_kernel, stage), (field_shape, shape(TR // RB,...]
    unnamed x50 -> x36, local copies, waits for them, and re-layouts: 9.98 us -> 8.62 us
  transfers between devices with their start and end apart: 13 -> 13, of which waited for: 9 -> 8; matrix products, arithmetic and copies ran while one was open for 0% -> 0% of each run, Pallas kernels for 1% -> 4%
where the time goes in v3:
time: 328 us; the launch traced here: 327 us
  blocking collectives  204 us (62%)
  Pallas kernels  47.6 us (15%)
  starting transfers between devices  46.1 us (14%)
  waiting for transfers between devices  20.2 us (6%)
  local copies, waits for them, and re-layouts  8.62 us (3%)
    all_to_all x14, blocking collectives, exchange(): lax.all_to_all(value, 'front', split_axis=0, concat_axis=0, tiled=True)  204 us
    ppermute x8, starting transfers between devices, across_cores(): lax.ppermute(value, 'layer', [(index, index ^ 1) for index in range(layer...  27.7 us
    all_to_all x2, starting transfers between devices, exchange(): lax.all_to_all(value, 'front', split_axis=0, concat_axis=0, tiled=True)  13.2 us
    pallas_call x4, Pallas kernels, body(): call(middle, (field_shape, slot_shape, field_shape), [smem] * 3 + [vmem]...  11.9 us
    pallas_call x7, Pallas kernels, separator(): call(functools.partial(separator_kernel, stage, step), slot_shape, [smem]...  9.24 us
    unnamed x36, local copies, waits for them, and re-layouts  8.62 us
    ppermute x3, waiting for transfers between devices, to_next_stage(): return lax.ppermute(value, 'layer', pairs)  8.54 us
    all_to_all x2, waiting for transfers between devices, exchange(): lax.all_to_all(value, 'front', split_axis=0, concat_axis=0, tiled=True)  8.53 us
  transfers between devices with their start and end apart: 13, of which 8 were waited for; matrix products, arithmetic and copies ran while one was open for 0% of the time, Pallas kernels for 4%

profile of v3, /device:TPU:1, one launch (start us, length us, event | category | flops | bytes accessed | tf_op | source)
XLA Modules:
  0.0 326.9 jit_solution(13159110441018846484)
XLA Ops:
  0.7 3.3 %collective-permute-start.4 = (f32[2,256,256]{2,1,0:T(8,128)}, f32[2,256,256]{2,1,0:T(8,128)S(1)}, u32[]{:S(2)}, u32[]{:S(2)}) collective-permute-start(f32[2,256,256]{2,1,0:T(8,128)} %bitcast.20), channel_id=1, source_target_pairs={{0,32},{32,0},{64,96},{96,64},{128,160},{160,128},{192,224},{224,1... | collective-permute-start | bytes 1572872 | tf_op jit(solution)/shard_map/ppermute | solution.py:605
  4.0 3.4 %shard_map.104 = (f32[2,16,8,128]{3,2,1,0:T(8,128)}, f32[2,16,8,128]{3,2,1,0:T(8,128)}, f32[2,256,128]{2,1,0:T(8,128)}, f32[2,256,128]{2,1,0:T(8,128)}) custom-call(s32[1]{0:T(128)} %bitcast.place_ref.refs_0_, f32[2,32,256]{2,1,0:T(8,128)} %bitcast.24, f32[2,32,256]{2,1,0:T(8,128)} %bitcast.25, f32[2,256,256]{2,1,0:T(8,128)} %bitcast.18, f32[2,512,256]{2,1,0:T(8,128)} %bitcast.16), custom_call_target="tpu_custom_call" | custom-call | flops 600000000 | bytes 2500000 | tf_op jit(solution)/shard_map/pallas_call | solution.py:646
  11.9 9.3 %all-to-all-start = ((f32[32,24,128]{2,1,0:T(8,128)}), f32[32,24,128]{2,1,0:T(8,128)S(1)}, u32[]{:S(2)}, u32[]{:S(2)}) async-start(f32[32,24,128]{2,1,0:T(8,128)} %get-tuple-element.55.after_ref), calls=%async_computation | async-start | bytes 786432 | tf_op jit(solution)/shard_map/all_to_all | solution.py:609
  26.4 4.5 %shard_map.106 = (f32[2,768,256]{2,1,0:T(8,128)}, f32[2,256,512]{2,1,0:T(8,128)S(1)}, bf16[2,2,512,256]{3,2,1,0:T(8,128)(2,1)S(1)}) custom-call(f32[32,24,128]{2,1,0:T(8,128)} %get-tuple-element.55.after_ref, f32[2,256,256]{2,1,0:T(8,128)S(1)} %bitcast.19, f32[2,512,256]{2,1,0:T(8,128)S(1)} %bitcast.17, f32[2,128,256]{2,1,0:T(8,128)S(1)} %bitcast.22, ...), custom_call_target="tpu_custom_call" | custom-call | flops 4000000000 | bytes 5000000 | tf_op jit(solution)/shard_map/pallas_call | solution.py:674
  30.8 4.7 %all-to-all-done.arrived_ref = f32[32,24,128]{2,1,0:T(8,128)S(1)} async-done(((f32[32,24,128]{2,1,0:T(8,128)}), f32[32,24,128]{2,1,0:T(8,128)S(1)}, u32[]{:S(2)}, u32[]{:S(2)}) %all-to-all-start) | async-done | bytes 393248 | tf_op jit(solution)/shard_map/all_to_all | solution.py:609
  39.8 3.9 %all-to-all-start.1 = ((f32[64,8,128]{2,1,0:T(8,128)}), f32[64,8,128]{2,1,0:T(8,128)S(1)}, u32[]{:S(2)}, u32[]{:S(2)}) async-start(f32[64,8,128]{2,1,0:T(8,128)} %get-tuple-element.65), calls=%async_computation.1 | async-start | bytes 524288 | tf_op jit(solution)/shard_map/all_to_all | solution.py:609
  46.7 4.8 %shard_map.108 = (f32[2,2,16,8,128]{4,3,2,1,0:T(8,128)S(1)}, f32[2,2,256,128]{3,2,1,0:T(8,128)S(1)}, bf16[2,2,512,512]{3,2,1,0:T(8,128)(2,1)}, bf16[2,2,1536,256]{3,2,1,0:T(8,128)(2,1)}) custom-call(f32[2,16,8,128]{3,2,1,0:T(8,128)S(1)} %copy-done.6, f32[2,16,8,128]{3,2,1,0:T(8,128)S(1)} %collective-permute-done.2.other_u_ref.other_u_hbm, ...), custom_call_target="tpu_custom_call" | custom-call | flops 10000000 | bytes 12000000 | tf_op jit(solution)/shard_map/pallas_call | solution.py:712
  51.5 3.8 %all-to-all-done.1.refs_7_ = f32[64,8,128]{2,1,0:T(8,128)S(1)} async-done(((f32[64,8,128]{2,1,0:T(8,128)}), f32[64,8,128]{2,1,0:T(8,128)S(1)}, u32[]{:S(2)}, u32[]{:S(2)}) %all-to-all-start.1) | async-done | bytes 262176 | tf_op jit(solution)/shard_map/all_to_all | solution.py:609
  60.0 17.1 %all_to_all.80.arrived_ref = f32[64,8,128]{2,1,0:T(8,128)S(1)} all-to-all(f32[64,8,128]{2,1,0:T(8,128)S(1)} %get-tuple-element.68), channel_id=1, replica_groups=mesh['layer'=8,'front'=32] {'front'}, dimensions={0} | all-to-all | bytes 524288 | tf_op jit(solution)/shard_map/all_to_all | solution.py:609
  78.4 15.0 %all_to_all.81.returned_ref = f32[64,8,128]{2,1,0:T(8,128)S(1)} all-to-all(f32[64,8,128]{2,1,0:T(8,128)S(1)} %shard_map.110), channel_id=1, replica_groups=mesh['layer'=8,'front'=32] {'front'}, dimensions={0} | all-to-all | bytes 524288 | tf_op jit(solution)/shard_map/all_to_all | solution.py:609
  99.7 15.3 %all_to_all.82.arrived_ref = f32[64,8,128]{2,1,0:T(8,128)S(1)} all-to-all(f32[64,8,128]{2,1,0:T(8,128)S(1)} %get-tuple-element.72), channel_id=1, replica_groups=mesh['layer'=8,'front'=32] {'front'}, dimensions={0} | all-to-all | bytes 524288 | tf_op jit(solution)/shard_map/all_to_all | solution.py:609
  116.3 14.0 %all_to_all.83.refs_7_ = f32[64,8,128]{2,1,0:T(8,128)S(1)} all-to-all(f32[64,8,128]{2,1,0:T(8,128)S(1)} %shard_map.113), channel_id=1, replica_groups=mesh['layer'=8,'front'=32] {'front'}, dimensions={0} | all-to-all | bytes 524288 | tf_op jit(solution)/shard_map/all_to_all | solution.py:609
  133.3 13.9 %all_to_all.84.arrived_ref = f32[64,8,128]{2,1,0:T(8,128)S(1)} all-to-all(f32[64,8,128]{2,1,0:T(8,128)S(1)} %get-tuple-element.75), channel_id=1, replica_groups=mesh['layer'=8,'front'=32] {'front'}, dimensions={0} | all-to-all | bytes 524288 | tf_op jit(solution)/shard_map/all_to_all | solution.py:609
  148.5 13.9 %all_to_all.85.returned_ref = f32[64,8,128]{2,1,0:T(8,128)S(1)} all-to-all(f32[64,8,128]{2,1,0:T(8,128)S(1)} %shard_map.115), channel_id=1, replica_groups=mesh['layer'=8,'front'=32] {'front'}, dimensions={0} | all-to-all | bytes 524288 | tf_op jit(solution)/shard_map/all_to_all | solution.py:609
  165.2 13.8 %all_to_all.86.arrived_ref = f32[64,8,128]{2,1,0:T(8,128)S(1)} all-to-all(f32[64,8,128]{2,1,0:T(8,128)S(1)} %get-tuple-element.79), channel_id=1, replica_groups=mesh['layer'=8,'front'=32] {'front'}, dimensions={0} | all-to-all | bytes 524288 | tf_op jit(solution)/shard_map/all_to_all | solution.py:609
  180.3 13.8 %all_to_all.87.refs_7_ = f32[64,8,128]{2,1,0:T(8,128)S(1)} all-to-all(f32[64,8,128]{2,1,0:T(8,128)S(1)} %shard_map.118), channel_id=1, replica_groups=mesh['layer'=8,'front'=32] {'front'}, dimensions={0} | all-to-all | bytes 524288 | tf_op jit(solution)/shard_map/all_to_all | solution.py:609
  197.0 13.8 %all_to_all.88.arrived_ref = f32[64,8,128]{2,1,0:T(8,128)S(1)} all-to-all(f32[64,8,128]{2,1,0:T(8,128)S(1)} %get-tuple-element.82), channel_id=1, replica_groups=mesh['layer'=8,'front'=32] {'front'}, dimensions={0} | all-to-all | bytes 524288 | tf_op jit(solution)/shard_map/all_to_all | solution.py:609
  212.1 13.8 %all_to_all.89.returned_ref = f32[64,8,128]{2,1,0:T(8,128)S(1)} all-to-all(f32[64,8,128]{2,1,0:T(8,128)S(1)} %shard_map.120), channel_id=1, replica_groups=mesh['layer'=8,'front'=32] {'front'}, dimensions={0} | all-to-all | bytes 524288 | tf_op jit(solution)/shard_map/all_to_all | solution.py:609
  228.3 7.7 %collective-permute-done.9.trace_ref = f32[4,8,128]{2,1,0:T(8,128)S(1)} collective-permute-done((f32[4,8,128]{2,1,0:T(8,128)S(1)}, f32[4,8,128]{2,1,0:T(8,128)S(1)}, u32[]{:S(2)}, u32[]{:S(2)}) %collective-permute-start.9) | collective-permute-done | bytes 16416 | tf_op jit(solution)/shard_map/ppermute | solution.py:615
  237.0 13.5 %all_to_all.90.arrived_ref = f32[64,8,128]{2,1,0:T(8,128)S(1)} all-to-all(f32[64,8,128]{2,1,0:T(8,128)S(1)} %get-tuple-element.86), channel_id=1, replica_groups=mesh['layer'=8,'front'=32] {'front'}, dimensions={0} | all-to-all | bytes 524288 | tf_op jit(solution)/shard_map/all_to_all | solution.py:609
  251.9 15.5 %all_to_all.91.refs_7_ = f32[64,8,128]{2,1,0:T(8,128)S(1)} all-to-all(f32[64,8,128]{2,1,0:T(8,128)S(1)} %shard_map.123), channel_id=1, replica_groups=mesh['layer'=8,'front'=32] {'front'}, dimensions={0} | all-to-all | bytes 524288 | tf_op jit(solution)/shard_map/all_to_all | solution.py:609
  270.3 16.2 %all_to_all.92.arrived_ref = f32[64,8,128]{2,1,0:T(8,128)S(1)} all-to-all(f32[64,8,128]{2,1,0:T(8,128)S(1)} %get-tuple-element.89), channel_id=1, replica_groups=mesh['layer'=8,'front'=32] {'front'}, dimensions={0} | all-to-all | bytes 524288 | tf_op jit(solution)/shard_map/all_to_all | solution.py:609
  287.8 14.2 %all_to_all.93.returned_ref = f32[64,8,128]{2,1,0:T(8,128)S(1)} all-to-all(f32[64,8,128]{2,1,0:T(8,128)S(1)} %shard_map.125), channel_id=1, replica_groups=mesh['layer'=8,'front'=32] {'front'}, dimensions={0} | all-to-all | bytes 524288 | tf_op jit(solution)/shard_map/all_to_all | solution.py:609
  304.7 20.6 %collective-permute-start.10 = (f32[2,2,16,256]{3,2,1,0:T(8,128)S(1)}, f32[2,2,16,256]{3,2,1,0:T(8,128)S(1)}, u32[]{:S(2)}, u32[]{:S(2)}) collective-permute-start(f32[2,2,16,256]{3,2,1,0:T(8,128)S(1)} %get-tuple-element.93), channel_id=1, source_target_pairs={{0,32},{32,0},{64,96},{96,64},{128,160},{160,128},{192,224},{224,1... | collective-permute-start | bytes 196616 | tf_op jit(solution)/shard_map/ppermute | solution.py:605
  (77 shorter events, 56.3 us)
Async XLA Ops:
  0.6 6.9 %copy-start.8 = (s32[1,1,16,1]{2,3,1,0:T(1,128)S(1)}, s32[1,1,16,1]{2,3,1,0:T(1,128)}, u32[]{:S(2)}) copy-start(s32[1,1,16,1]{2,3,1,0:T(1,128)} %param.16) | copy-start | bytes 196
  0.6 7.4 %copy-start.9 = (s32[1,1,16]{2,1,0:T(1,128)S(1)}, s32[1,1,16]{2,1,0:T(1,128)}, u32[]{:S(2)}) copy-start(s32[1,1,16]{2,1,0:T(1,128)} %param.17) | copy-start | bytes 196
  0.7 20.5 %collective-permute-start.4 = (f32[2,256,256]{2,1,0:T(8,128)}, f32[2,256,256]{2,1,0:T(8,128)S(1)}, u32[]{:S(2)}, u32[]{:S(2)}) collective-permute-start(f32[2,256,256]{2,1,0:T(8,128)} %bitcast.20), channel_id=1, source_target_pairs={{0,32},{32,0},{64,96},{96,64},{128,160},{160,128},{192,224},{224,1... | collective-permute-start | bytes 1572872 | tf_op jit(solution)/shard_map/ppermute | solution.py:605
  4.0 18.0 %copy-start.15 = (f32[1,1,2,128,256]{4,3,2,1,0:T(8,128)S(1)}, f32[1,1,2,128,256]{4,3,2,1,0:T(8,128)}, u32[]{:S(2)}) copy-start(f32[1,1,2,128,256]{4,3,2,1,0:T(8,128)} %param.14) | copy-start | bytes 786436
  4.0 18.0 %copy-start.16 = (f32[1,1,2,128,256]{4,3,2,1,0:T(8,128)S(1)}, f32[1,1,2,128,256]{4,3,2,1,0:T(8,128)}, u32[]{:S(2)}) copy-start(f32[1,1,2,128,256]{4,3,2,1,0:T(8,128)} %param.15) | copy-start | bytes 786436
  7.4 1.7 collective-permute-start.2
  7.6 1.3 collective-permute-start
  8.0 1.1 collective-permute-start.1
  11.9 23.6 %all-to-all-start = ((f32[32,24,128]{2,1,0:T(8,128)}), f32[32,24,128]{2,1,0:T(8,128)S(1)}, u32[]{:S(2)}, u32[]{:S(2)}) async-start(f32[32,24,128]{2,1,0:T(8,128)} %get-tuple-element.55.after_ref), calls=%async_computation | async-start | bytes 786432 | tf_op jit(solution)/shard_map/all_to_all | solution.py:609
  35.5 8.3 %copy-start.17 = (f32[2,256,128]{2,1,0:T(8,128)S(1)}, f32[2,256,128]{2,1,0:T(8,128)}, u32[]{:S(2)}) copy-start(f32[2,256,128]{2,1,0:T(8,128)} %get-tuple-element.54) | copy-start | bytes 786436
  35.5 10.2 %copy-start.6 = (f32[2,16,8,128]{3,2,1,0:T(8,128)S(1)}, f32[2,16,8,128]{3,2,1,0:T(8,128)}, u32[]{:S(2)}) copy-start(f32[2,16,8,128]{3,2,1,0:T(8,128)} %get-tuple-element.49.own_u_ref.own_u_hbm) | copy-start | bytes 393220
  37.6 8.1 %collective-permute-start.6 = (f32[2,768,256]{2,1,0:T(8,128)}, f32[2,768,256]{2,1,0:T(8,128)}, u32[]{:S(2)}, u32[]{:S(2)}) collective-permute-start(f32[2,768,256]{2,1,0:T(8,128)} %get-tuple-element.60.own_forward_hbm), channel_id=1, source_target_pairs={{0,32},{32,0},{64,96},{96,64},{128,160},{160,128},{192,224},{224,1... | collective-permute-start | bytes 4718600 | tf_op jit(solution)/shard_map/ppermute | solution.py:605
  39.7 6.0 %collective-permute-start.5 = (f32[2,256,512]{2,1,0:T(8,128)S(1)}, f32[2,256,512]{2,1,0:T(8,128)}, u32[]{:S(2)}, u32[]{:S(2)}) collective-permute-start(f32[2,256,512]{2,1,0:T(8,128)S(1)} %get-tuple-element.59.own_back_hbm), channel_id=1, source_target_pairs={{0,32},{32,0},{64,96},{96,64},{128,160},{160,128},{192,224},{224,1... | collective-permute-start | bytes 3145736 | tf_op jit(solution)/shard_map/ppermute | solution.py:605
  39.8 15.5 %all-to-all-start.1 = ((f32[64,8,128]{2,1,0:T(8,128)}), f32[64,8,128]{2,1,0:T(8,128)S(1)}, u32[]{:S(2)}, u32[]{:S(2)}) async-start(f32[64,8,128]{2,1,0:T(8,128)} %get-tuple-element.65), calls=%async_computation.1 | async-start | bytes 524288 | tf_op jit(solution)/shard_map/all_to_all | solution.py:609
  43.8 1.9 collective-permute-start.3
  55.3 1.6 copy-start.3
  56.9 36.5 %copy-start.4 = (bf16[2,2,512,512]{3,2,1,0:T(8,128)(2,1)S(1)}, bf16[2,2,512,512]{3,2,1,0:T(8,128)(2,1)}, u32[]{:S(2)}) copy-start(bf16[2,2,512,512]{3,2,1,0:T(8,128)(2,1)} %get-tuple-element.64.refs_6_.backs_ref) | copy-start | bytes 6291460
  77.1 21.6 %copy-start = (bf16[2,2,1536,256]{3,2,1,0:T(8,128)(2,1)S(1)}, bf16[2,2,1536,256]{3,2,1,0:T(8,128)(2,1)}, u32[]{:S(2)}) copy-start(bf16[2,2,1536,256]{3,2,1,0:T(8,128)(2,1)} %get-tuple-element.63.refs_5_.forwards_ref) | copy-start | bytes 9437188
  94.5 4.1 %collective-permute-start.7 = (f32[4,8,128]{2,1,0:T(8,128)S(1)}, f32[4,8,128]{2,1,0:T(8,128)S(1)}, u32[]{:S(2)}, u32[]{:S(2)}) collective-permute-start(f32[4,8,128]{2,1,0:T(8,128)S(1)} %get-tuple-element.71), channel_id=1, source_target_pairs={{0,64},{32,96},{192,128},{224,160},{1,65},{33,97},{193,129},{225,1... | collective-permute-start | bytes 49160 | tf_op jit(solution)/shard_map/ppermute | solution.py:615
  147.1 17.0 %copy-start.1 = (bf16[2,2,1536,256]{3,2,1,0:T(8,128)(2,1)S(1)}, bf16[2,2,1536,256]{3,2,1,0:T(8,128)(2,1)}, u32[]{:S(2)}) copy-start(bf16[2,2,1536,256]{3,2,1,0:T(8,128)(2,1)} %get-tuple-element.63.refs_5_.forwards_ref) | copy-start | bytes 9437188
  163.5 0.7 collective-permute-start.8
  210.8 25.2 %copy-start.2 = (bf16[2,2,1536,256]{3,2,1,0:T(8,128)(2,1)S(1)}, bf16[2,2,1536,256]{3,2,1,0:T(8,128)(2,1)}, u32[]{:S(2)}) copy-start(bf16[2,2,1536,256]{3,2,1,0:T(8,128)(2,1)} %get-tuple-element.63.refs_5_.forwards_ref) | copy-start | bytes 9437188
  227.0 9.0 %collective-permute-start.9 = (f32[4,8,128]{2,1,0:T(8,128)S(1)}, f32[4,8,128]{2,1,0:T(8,128)S(1)}, u32[]{:S(2)}, u32[]{:S(2)}) collective-permute-start(f32[4,8,128]{2,1,0:T(8,128)S(1)} %get-tuple-element.85), channel_id=1, source_target_pairs={{128,192},{160,224},{64,0},{96,32},{129,193},{161,225},{65,1},{97,... | collective-permute-start | bytes 49160 | tf_op jit(solution)/shard_map/ppermute | solution.py:615
  304.7 21.5 %collective-permute-start.10 = (f32[2,2,16,256]{3,2,1,0:T(8,128)S(1)}, f32[2,2,16,256]{3,2,1,0:T(8,128)S(1)}, u32[]{:S(2)}, u32[]{:S(2)}) collective-permute-start(f32[2,2,16,256]{3,2,1,0:T(8,128)S(1)} %get-tuple-element.93), channel_id=1, source_target_pairs={{0,32},{32,0},{64,96},{96,64},{128,160},{160,128},{192,224},{224,1... | collective-permute-start | bytes 196616 | tf_op jit(solution)/shard_map/ppermute | solution.py:605
  (7 other events, 7.0 us)

commit v4 on v3

--- a/solution.py
+++ b/solution.py
@@ -22,7 +22,7 @@
 
 f32 = jnp.float32
 bf16 = jnp.bfloat16
-VMEM_LIMIT = 48 * 1024 * 1024
+VMEM_LIMIT = 52 * 1024 * 1024
 ALMOST_ALL_VMEM = 60 * 1024 * 1024
 smem = pl.BlockSpec(memory_space=pltpu.SMEM)
 vmem = pl.BlockSpec(memory_space=pltpu.VMEM)
@@ -61,10 +61,19 @@
     return jnp.concatenate(halves(value), axis=0)
 
 
-def stacked_product(first, second):
-    rows = first.shape[0] // 2
-    both = dot(first, jnp.concatenate(halves(second), axis=1))
-    return (both[:rows, :LANES] + both[:rows, LANES:]) + (both[rows:, :LANES] + both[rows:, LANES:])
+def shared(value):
+    low = value - value.astype(bf16).astype(f32)
+    return jnp.where(lane_ids(value.shape[0]) < LANES // 2, value, low).astype(bf16)
+
+
+def stacked_product(pairs):
+    total = None
+    for first, second in pairs:
+        both = dot(first, shared(second))
+        total = both if total is None else total + both
+    rows = total.shape[0] // 2
+    total = total[:rows] + total[rows:]
+    return total + pltpu.roll(total, LANES // 2, 1)
 
 
 def complex_pair(first, second, dims=NN):
@@ -353,19 +362,23 @@
         send_ref[slot // CAP, pl.ds(row, 8), :] = packed[block]
 
 
-def separator_solve(choice, offsets_ref, arrived, seps_ref, reply_ref, even_ref, odd_ref, solved_ref):
+def separator_solve(choice, offsets_ref, arrived, seps_ref, reply_ref, solved_ref, *total_refs):
     leaves = reply_ref.shape[0] // CAP
-    even_ref[...] = jnp.zeros_like(even_ref)
-    odd_ref[...] = jnp.zeros_like(odd_ref)
+    for total_ref in total_refs:
+        total_ref[...] = jnp.zeros_like(total_ref)
     places = []
     for leaf in range(leaves):
-        for rank, total_ref in enumerate((even_ref, odd_ref)):
+        for rank in range(CAP):
             place = offsets_ref[CAP * choice + rank, leaf]
+            total_ref = total_refs[len(places) % len(total_refs)]
             places.append(place)
             total_ref[place] = total_ref[place] + arrived(leaf, rank)
-    rhs, rhs_turned = unpack_both(even_ref[:QB] + odd_ref[:QB])
-    solved = stacked_product(seps_ref[choice, 0], rhs) + stacked_product(
-        seps_ref[choice, 1], rhs_turned
+    total = total_refs[0][:QB]
+    for total_ref in total_refs[1:]:
+        total = total + total_ref[:QB]
+    rhs, rhs_turned = unpack_both(total)
+    solved = stacked_product(
+        ((seps_ref[choice, 0], rhs), (seps_ref[choice, 1], rhs_turned))
     )
     solved_ref[:QB] = pack(solved)
     solved_ref[QB] = jnp.zeros((8, LANES), f32)
@@ -425,10 +438,8 @@
         slot = jnp.where(choice == 0, own_slots_ref[block], other_slots_ref[block])
         blocks.append(returned_ref[slot])
     mine, mine_turned = unpack_both(jnp.stack(blocks, axis=0))
-    return (
-        base
-        + stacked_product(backs_ref[choice, 0], mine)
-        + stacked_product(backs_ref[choice, 1], mine_turned)
+    return base + stacked_product(
+        ((backs_ref[choice, 0], mine), (backs_ref[choice, 1], mine_turned))
     )
 
 
@@ -446,7 +457,7 @@
     base_ref,
 ):
     driven = stacked_product(
-        forwards_ref[choice, sweep], jnp.concatenate([trace, trace_turned], axis=0)
+        ((forwards_ref[choice, sweep], jnp.concatenate([trace, trace_turned], axis=0)),)
     )
     packed = pack(driven[: NB * RB]) + u_ref[choice, sweep]
     send_blocks(choice, own_slots_ref, other_slots_ref, packed, send_ref)
@@ -690,7 +701,7 @@
         ],
         cost_of(4_000_000_000, 5_000_000),
     )(send, leaf, rows, inject_top[0, 0], inject_bottom[0, 0], sep, other_sep)
-    separator_scratch = [pltpu.VMEM((QB + 1, 8, LANES), f32)] * 3
+    separator_scratch = [pltpu.VMEM((QB + 1, 8, LANES), f32)] * 5
     places, reply, own_forward, own_back = call(
         first_separator_kernel,
         (

time: 328 us -> 341 us (1.040)
  Pallas kernels: 47.6 us -> 63.3 us
  local copies, waits for them, and re-layouts: 8.62 us -> 2.98 us
    unnamed x36 -> x26, local copies, waits for them, and re-layouts: 8.62 us -> 2.98 us
    pallas_call x4, Pallas kernels: 11.9 us -> 16.7 us  [body(): call(middle, (field_shape, slot_shape, field_shape), [smem] * 3 + [vmem]...]
    pallas_call x4, Pallas kernels: 5.22 us -> 9.72 us  [body(): call(functools.partial(last_kernel, stage), (field_shape, shape(TR // RB,...]
    pallas_call x3, Pallas kernels: 3.11 us -> 7.37 us  [body(): call(functools.partial(enter_kernel, stage), (slot_shape, field_shape), [...]
  transfers between devices with their start and end apart: 13 -> 13, of which waited for: 8 -> 8; matrix products, arithmetic and copies ran while one was open for 0% -> 0% of each run, Pallas kernels for 4% -> 5%
where the time goes in v4:
time: 341 us; the launch traced here: 340 us
  blocking collectives  204 us (60%)
  Pallas kernels  63.3 us (19%)
  starting transfers between devices  46 us (13%)
  waiting for transfers between devices  23.1 us (7%)
    all_to_all x14, blocking collectives, exchange(): lax.all_to_all(value, 'front', split_axis=0, concat_axis=0, tiled=True)  204 us
    ppermute x8, starting transfers between devices, across_cores(): lax.ppermute(value, 'layer', [(index, index ^ 1) for index in range(layer...  27.6 us
    pallas_call x4, Pallas kernels, body(): call(middle, (field_shape, slot_shape, field_shape), [smem] * 3 + [vmem]...  16.7 us
    all_to_all x2, starting transfers between devices, exchange(): lax.all_to_all(value, 'front', split_axis=0, concat_axis=0, tiled=True)  13.2 us
    all_to_all x2, waiting for transfers between devices, exchange(): lax.all_to_all(value, 'front', split_axis=0, concat_axis=0, tiled=True)  11.5 us
    pallas_call x4, Pallas kernels, body(): call(functools.partial(last_kernel, stage), (field_shape, shape(TR // RB,...  9.72 us
    pallas_call x7, Pallas kernels, separator(): call(functools.partial(separator_kernel, stage, step), slot_shape, [smem]...  9.03 us
    ppermute x3, waiting for transfers between devices, to_next_stage(): return lax.ppermute(value, 'layer', pairs)  8.57 us
  transfers between devices with their start and end apart: 13, of which 8 were waited for; matrix products, arithmetic and copies ran while one was open for 0% of the time, Pallas kernels for 5%

profile of v4, /device:TPU:1, one launch (start us, length us, event | category | flops | bytes accessed | tf_op | source)
XLA Modules:
  0.0 340.2 jit_solution(16915183992222223937)
XLA Ops:
  11.9 9.3 %all-to-all-start = ((f32[32,24,128]{2,1,0:T(8,128)}), f32[32,24,128]{2,1,0:T(8,128)S(1)}, u32[]{:S(2)}, u32[]{:S(2)}) async-start(f32[32,24,128]{2,1,0:T(8,128)} %get-tuple-element.55.after_ref), calls=%async_computation | async-start | bytes 786432 | tf_op jit(solution)/shard_map/all_to_all | solution.py:620
  22.1 5.3 %shard_map.106 = (f32[2,768,256]{2,1,0:T(8,128)}, f32[2,256,512]{2,1,0:T(8,128)}, bf16[2,2,512,256]{3,2,1,0:T(8,128)(2,1)}) custom-call(f32[32,24,128]{2,1,0:T(8,128)} %get-tuple-element.55.after_ref, f32[2,256,256]{2,1,0:T(8,128)S(1)} %bitcast.17, f32[2,512,256]{2,1,0:T(8,128)} %bitcast.23, f32[2,128,256]{2,1,0:T(8,128)S(1)} %bitcast.20, ...), custom_call_target="tpu_custom_call" | custom-call | flops 4000000000 | bytes 5000000 | tf_op jit(solution)/shard_map/pallas_call | solution.py:685
  27.4 8.2 %all-to-all-done.arrived_ref = f32[32,24,128]{2,1,0:T(8,128)S(1)} async-done(((f32[32,24,128]{2,1,0:T(8,128)}), f32[32,24,128]{2,1,0:T(8,128)S(1)}, u32[]{:S(2)}, u32[]{:S(2)}) %all-to-all-start) | async-done | bytes 393248 | tf_op jit(solution)/shard_map/all_to_all | solution.py:620
  48.3 5.1 %shard_map.108 = (f32[2,2,16,8,128]{4,3,2,1,0:T(8,128)S(1)}, f32[2,2,256,128]{3,2,1,0:T(8,128)S(1)}, bf16[2,2,512,512]{3,2,1,0:T(8,128)(2,1)}, bf16[2,2,1536,256]{3,2,1,0:T(8,128)(2,1)}) custom-call(f32[2,16,8,128]{3,2,1,0:T(8,128)S(1)} %copy-done.2, f32[2,16,8,128]{3,2,1,0:T(8,128)S(1)} %collective-permute-done.2.other_u_ref.other_u_hbm, ...), custom_call_target="tpu_custom_call" | custom-call | flops 10000000 | bytes 12000000 | tf_op jit(solution)/shard_map/pallas_call | solution.py:723
  56.7 4.2 %shard_map.109 = (f32[256,128]{1,0:T(8,128)S(1)}, f32[64,8,128]{2,1,0:T(8,128)S(1)}, f32[256,128]{1,0:T(8,128)S(1)}) custom-call(s32[1]{0:T(128)} %bitcast.place_ref.refs_0_, s32[16]{0:T(128)S(1)} %get-tuple-element.51.refs_1_.own_slots_ref, s32[16]{0:T(128)S(1)} %get-tuple-element.52.refs_2_.other_slots_ref, ...), custom_call_target="tpu_custom_call" | custom-call | flops 300000000 | bytes 3000000 | tf_op jit(solution)/shard_map/pallas_call | solution.py:771
  60.9 17.6 %all_to_all.80.arrived_ref = f32[64,8,128]{2,1,0:T(8,128)S(1)} all-to-all(f32[64,8,128]{2,1,0:T(8,128)S(1)} %get-tuple-element.68), channel_id=1, replica_groups=mesh['layer'=8,'front'=32] {'front'}, dimensions={0} | all-to-all | bytes 524288 | tf_op jit(solution)/shard_map/all_to_all | solution.py:620
  79.8 15.2 %all_to_all.81.returned_ref = f32[64,8,128]{2,1,0:T(8,128)S(1)} all-to-all(f32[64,8,128]{2,1,0:T(8,128)S(1)} %shard_map.110), channel_id=1, replica_groups=mesh['layer'=8,'front'=32] {'front'}, dimensions={0} | all-to-all | bytes 524288 | tf_op jit(solution)/shard_map/all_to_all | solution.py:620
  103.8 15.3 %all_to_all.82.arrived_ref = f32[64,8,128]{2,1,0:T(8,128)S(1)} all-to-all(f32[64,8,128]{2,1,0:T(8,128)S(1)} %get-tuple-element.72), channel_id=1, replica_groups=mesh['layer'=8,'front'=32] {'front'}, dimensions={0} | all-to-all | bytes 524288 | tf_op jit(solution)/shard_map/all_to_all | solution.py:620
  120.4 14.0 %all_to_all.83.refs_7_ = f32[64,8,128]{2,1,0:T(8,128)S(1)} all-to-all(f32[64,8,128]{2,1,0:T(8,128)S(1)} %shard_map.113), channel_id=1, replica_groups=mesh['layer'=8,'front'=32] {'front'}, dimensions={0} | all-to-all | bytes 524288 | tf_op jit(solution)/shard_map/all_to_all | solution.py:620
  134.4 4.1 %shard_map.114 = (f32[256,128]{1,0:T(8,128)S(1)}, f32[64,8,128]{2,1,0:T(8,128)S(1)}, f32[256,128]{1,0:T(8,128)S(1)}) custom-call(s32[1]{0:T(128)} %bitcast.place_ref.refs_0_, s32[16]{0:T(128)S(1)} %get-tuple-element.51.refs_1_.own_slots_ref, s32[16]{0:T(128)S(1)} %get-tuple-element.52.refs_2_.other_slots_ref, ...), custom_call_target="tpu_custom_call" | custom-call | flops 300000000 | bytes 3000000 | tf_op jit(solution)/shard_map/pallas_call | solution.py:771
  138.6 13.9 %all_to_all.84.arrived_ref = f32[64,8,128]{2,1,0:T(8,128)S(1)} all-to-all(f32[64,8,128]{2,1,0:T(8,128)S(1)} %get-tuple-element.75), channel_id=1, replica_groups=mesh['layer'=8,'front'=32] {'front'}, dimensions={0} | all-to-all | bytes 524288 | tf_op jit(solution)/shard_map/all_to_all | solution.py:620
  153.8 13.9 %all_to_all.85.returned_ref = f32[64,8,128]{2,1,0:T(8,128)S(1)} all-to-all(f32[64,8,128]{2,1,0:T(8,128)S(1)} %shard_map.115), channel_id=1, replica_groups=mesh['layer'=8,'front'=32] {'front'}, dimensions={0} | all-to-all | bytes 524288 | tf_op jit(solution)/shard_map/all_to_all | solution.py:620
  173.1 13.8 %all_to_all.86.arrived_ref = f32[64,8,128]{2,1,0:T(8,128)S(1)} all-to-all(f32[64,8,128]{2,1,0:T(8,128)S(1)} %get-tuple-element.79), channel_id=1, replica_groups=mesh['layer'=8,'front'=32] {'front'}, dimensions={0} | all-to-all | bytes 524288 | tf_op jit(solution)/shard_map/all_to_all | solution.py:620
  188.1 13.8 %all_to_all.87.refs_7_ = f32[64,8,128]{2,1,0:T(8,128)S(1)} all-to-all(f32[64,8,128]{2,1,0:T(8,128)S(1)} %shard_map.118), channel_id=1, replica_groups=mesh['layer'=8,'front'=32] {'front'}, dimensions={0} | all-to-all | bytes 524288 | tf_op jit(solution)/shard_map/all_to_all | solution.py:620
  201.9 4.1 %shard_map.119 = (f32[256,128]{1,0:T(8,128)S(1)}, f32[64,8,128]{2,1,0:T(8,128)S(1)}, f32[256,128]{1,0:T(8,128)S(1)}) custom-call(s32[1]{0:T(128)} %bitcast.place_ref.refs_0_, s32[16]{0:T(128)S(1)} %get-tuple-element.51.refs_1_.own_slots_ref, s32[16]{0:T(128)S(1)} %get-tuple-element.52.refs_2_.other_slots_ref, ...), custom_call_target="tpu_custom_call" | custom-call | flops 300000000 | bytes 3000000 | tf_op jit(solution)/shard_map/pallas_call | solution.py:771
  206.0 13.8 %all_to_all.88.arrived_ref = f32[64,8,128]{2,1,0:T(8,128)S(1)} all-to-all(f32[64,8,128]{2,1,0:T(8,128)S(1)} %get-tuple-element.82), channel_id=1, replica_groups=mesh['layer'=8,'front'=32] {'front'}, dimensions={0} | all-to-all | bytes 524288 | tf_op jit(solution)/shard_map/all_to_all | solution.py:620
  221.1 13.8 %all_to_all.89.returned_ref = f32[64,8,128]{2,1,0:T(8,128)S(1)} all-to-all(f32[64,8,128]{2,1,0:T(8,128)S(1)} %shard_map.120), channel_id=1, replica_groups=mesh['layer'=8,'front'=32] {'front'}, dimensions={0} | all-to-all | bytes 524288 | tf_op jit(solution)/shard_map/all_to_all | solution.py:620
  238.4 7.7 %collective-permute-done.9.trace_ref = f32[4,8,128]{2,1,0:T(8,128)S(1)} collective-permute-done((f32[4,8,128]{2,1,0:T(8,128)S(1)}, f32[4,8,128]{2,1,0:T(8,128)S(1)}, u32[]{:S(2)}, u32[]{:S(2)}) %collective-permute-start.9) | collective-permute-done | bytes 16416 | tf_op jit(solution)/shard_map/ppermute | solution.py:626
  248.6 13.5 %all_to_all.90.arrived_ref = f32[64,8,128]{2,1,0:T(8,128)S(1)} all-to-all(f32[64,8,128]{2,1,0:T(8,128)S(1)} %get-tuple-element.86), channel_id=1, replica_groups=mesh['layer'=8,'front'=32] {'front'}, dimensions={0} | all-to-all | bytes 524288 | tf_op jit(solution)/shard_map/all_to_all | solution.py:620
  263.4 15.5 %all_to_all.91.refs_7_ = f32[64,8,128]{2,1,0:T(8,128)S(1)} all-to-all(f32[64,8,128]{2,1,0:T(8,128)S(1)} %shard_map.123), channel_id=1, replica_groups=mesh['layer'=8,'front'=32] {'front'}, dimensions={0} | all-to-all | bytes 524288 | tf_op jit(solution)/shard_map/all_to_all | solution.py:620
  278.9 4.1 %shard_map.124 = (f32[256,128]{1,0:T(8,128)S(1)}, f32[64,8,128]{2,1,0:T(8,128)S(1)}, f32[256,128]{1,0:T(8,128)S(1)}) custom-call(s32[1]{0:T(128)} %bitcast.place_ref.refs_0_, s32[16]{0:T(128)S(1)} %get-tuple-element.51.refs_1_.own_slots_ref, s32[16]{0:T(128)S(1)} %get-tuple-element.52.refs_2_.other_slots_ref, ...), custom_call_target="tpu_custom_call" | custom-call | flops 300000000 | bytes 3000000 | tf_op jit(solution)/shard_map/pallas_call | solution.py:771
  283.1 16.3 %all_to_all.92.arrived_ref = f32[64,8,128]{2,1,0:T(8,128)S(1)} all-to-all(f32[64,8,128]{2,1,0:T(8,128)S(1)} %get-tuple-element.89), channel_id=1, replica_groups=mesh['layer'=8,'front'=32] {'front'}, dimensions={0} | all-to-all | bytes 524288 | tf_op jit(solution)/shard_map/all_to_all | solution.py:620
  300.6 13.7 %all_to_all.93.returned_ref = f32[64,8,128]{2,1,0:T(8,128)S(1)} all-to-all(f32[64,8,128]{2,1,0:T(8,128)S(1)} %shard_map.125), channel_id=1, replica_groups=mesh['layer'=8,'front'=32] {'front'}, dimensions={0} | all-to-all | bytes 524288 | tf_op jit(solution)/shard_map/all_to_all | solution.py:620
  318.1 20.6 %collective-permute-start.10 = (f32[2,2,16,256]{3,2,1,0:T(8,128)S(1)}, f32[2,2,16,256]{3,2,1,0:T(8,128)S(1)}, u32[]{:S(2)}, u32[]{:S(2)}) collective-permute-start(f32[2,2,16,256]{3,2,1,0:T(8,128)S(1)} %get-tuple-element.93), channel_id=1, source_target_pairs={{0,32},{32,0},{64,96},{96,64},{128,160},{160,128},{192,224},{224,1... | collective-permute-start | bytes 196616 | tf_op jit(solution)/shard_map/ppermute | solution.py:616
  (67 shorter events, 62.6 us)
Async XLA Ops:
  0.6 7.0 %copy-start.4 = (s32[1,1,16,1]{2,3,1,0:T(1,128)S(1)}, s32[1,1,16,1]{2,3,1,0:T(1,128)}, u32[]{:S(2)}) copy-start(s32[1,1,16,1]{2,3,1,0:T(1,128)} %param.16) | copy-start | bytes 196
  0.6 7.5 %copy-start.5 = (s32[1,1,16]{2,1,0:T(1,128)S(1)}, s32[1,1,16]{2,1,0:T(1,128)}, u32[]{:S(2)}) copy-start(s32[1,1,16]{2,1,0:T(1,128)} %param.17) | copy-start | bytes 196
  0.7 20.6 %collective-permute-start.4 = (f32[2,256,256]{2,1,0:T(8,128)}, f32[2,256,256]{2,1,0:T(8,128)S(1)}, u32[]{:S(2)}, u32[]{:S(2)}) collective-permute-start(f32[2,256,256]{2,1,0:T(8,128)} %bitcast.18), channel_id=1, source_target_pairs={{0,32},{32,0},{64,96},{96,64},{128,160},{160,128},{192,224},{224,1... | collective-permute-start | bytes 1572872 | tf_op jit(solution)/shard_map/ppermute | solution.py:616
  4.0 18.1 %copy-start.6 = (f32[1,1,2,256,256]{4,3,2,1,0:T(8,128)S(1)}, f32[1,1,2,256,256]{4,3,2,1,0:T(8,128)}, u32[]{:S(2)}) copy-start(f32[1,1,2,256,256]{4,3,2,1,0:T(8,128)} %param.11) | copy-start | bytes 1572868
  4.0 18.1 %copy-start.7 = (f32[1,1,2,256,256]{4,3,2,1,0:T(8,128)S(1)}, f32[1,1,2,256,256]{4,3,2,1,0:T(8,128)}, u32[]{:S(2)}) copy-start(f32[1,1,2,256,256]{4,3,2,1,0:T(8,128)} %param.13) | copy-start | bytes 1572868
  4.0 18.1 %copy-start.8 = (f32[1,1,2,128,256]{4,3,2,1,0:T(8,128)S(1)}, f32[1,1,2,128,256]{4,3,2,1,0:T(8,128)}, u32[]{:S(2)}) copy-start(f32[1,1,2,128,256]{4,3,2,1,0:T(8,128)} %param.14) | copy-start | bytes 786436
  4.0 18.1 %copy-start.9 = (f32[1,1,2,128,256]{4,3,2,1,0:T(8,128)S(1)}, f32[1,1,2,128,256]{4,3,2,1,0:T(8,128)}, u32[]{:S(2)}) copy-start(f32[1,1,2,128,256]{4,3,2,1,0:T(8,128)} %param.15) | copy-start | bytes 786436
  7.5 1.7 collective-permute-start.2
  7.6 1.3 collective-permute-start
  8.1 1.1 collective-permute-start.1
  11.9 23.6 %all-to-all-start = ((f32[32,24,128]{2,1,0:T(8,128)}), f32[32,24,128]{2,1,0:T(8,128)S(1)}, u32[]{:S(2)}, u32[]{:S(2)}) async-start(f32[32,24,128]{2,1,0:T(8,128)} %get-tuple-element.55.after_ref), calls=%async_computation | async-start | bytes 786432 | tf_op jit(solution)/shard_map/all_to_all | solution.py:620
  35.6 9.5 %copy-start.12 = (f32[2,256,128]{2,1,0:T(8,128)S(1)}, f32[2,256,128]{2,1,0:T(8,128)}, u32[]{:S(2)}) copy-start(f32[2,256,128]{2,1,0:T(8,128)} %get-tuple-element.54) | copy-start | bytes 786436
  35.6 12.7 %copy-start.2 = (f32[2,16,8,128]{3,2,1,0:T(8,128)S(1)}, f32[2,16,8,128]{3,2,1,0:T(8,128)}, u32[]{:S(2)}) copy-start(f32[2,16,8,128]{3,2,1,0:T(8,128)} %get-tuple-element.49.own_u_ref.own_u_hbm) | copy-start | bytes 393220
  35.6 12.7 %copy-start.3 = (f32[2,256,128]{2,1,0:T(8,128)S(1)}, f32[2,256,128]{2,1,0:T(8,128)}, u32[]{:S(2)}) copy-start(f32[2,256,128]{2,1,0:T(8,128)} %get-tuple-element.53.own_y_hbm) | copy-start | bytes 786436
  39.0 8.1 %collective-permute-start.6 = (f32[2,768,256]{2,1,0:T(8,128)}, f32[2,768,256]{2,1,0:T(8,128)S(1)}, u32[]{:S(2)}, u32[]{:S(2)}) collective-permute-start(f32[2,768,256]{2,1,0:T(8,128)} %get-tuple-element.60.own_forward_hbm), channel_id=1, source_target_pairs={{0,32},{32,0},{64,96},{96,64},{128,160},{160,128},{192,224},{224,1... | collective-permute-start | bytes 4718600 | tf_op jit(solution)/shard_map/ppermute | solution.py:616
  41.1 6.0 %collective-permute-start.5 = (f32[2,256,512]{2,1,0:T(8,128)}, f32[2,256,512]{2,1,0:T(8,128)}, u32[]{:S(2)}, u32[]{:S(2)}) collective-permute-start(f32[2,256,512]{2,1,0:T(8,128)} %get-tuple-element.59.own_back_hbm), channel_id=1, source_target_pairs={{0,32},{32,0},{64,96},{96,64},{128,160},{160,128},{192,224},{224,1... | collective-permute-start | bytes 3145736 | tf_op jit(solution)/shard_map/ppermute | solution.py:616
  41.2 15.5 %all-to-all-start.1 = ((f32[64,8,128]{2,1,0:T(8,128)}), f32[64,8,128]{2,1,0:T(8,128)S(1)}, u32[]{:S(2)}, u32[]{:S(2)}) async-start(f32[64,8,128]{2,1,0:T(8,128)} %get-tuple-element.65), calls=%async_computation.1 | async-start | bytes 524288 | tf_op jit(solution)/shard_map/all_to_all | solution.py:620
  45.1 1.9 collective-permute-start.3
  47.1 1.2 copy-start.10
  56.7 21.9 %copy-start = (bf16[2,2,512,256]{3,2,1,0:T(8,128)(2,1)S(1)}, bf16[2,2,512,256]{3,2,1,0:T(8,128)(2,1)}, u32[]{:S(2)}) copy-start(bf16[2,2,512,256]{3,2,1,0:T(8,128)(2,1)} %get-tuple-element.56.seps_ref) | copy-start | bytes 3145732
  97.3 4.1 %collective-permute-start.7 = (f32[4,8,128]{2,1,0:T(8,128)S(1)}, f32[4,8,128]{2,1,0:T(8,128)S(1)}, u32[]{:S(2)}, u32[]{:S(2)}) collective-permute-start(f32[4,8,128]{2,1,0:T(8,128)S(1)} %get-tuple-element.71), channel_id=1, source_target_pairs={{0,64},{32,96},{192,128},{224,160},{1,65},{33,97},{193,129},{225,1... | collective-permute-start | bytes 49160 | tf_op jit(solution)/shard_map/ppermute | solution.py:626
  169.9 0.7 collective-permute-start.8
  237.1 9.0 %collective-permute-start.9 = (f32[4,8,128]{2,1,0:T(8,128)S(1)}, f32[4,8,128]{2,1,0:T(8,128)S(1)}, u32[]{:S(2)}, u32[]{:S(2)}) collective-permute-start(f32[4,8,128]{2,1,0:T(8,128)S(1)} %get-tuple-element.85), channel_id=1, source_target_pairs={{128,192},{160,224},{64,0},{96,32},{129,193},{161,225},{65,1},{97,... | collective-permute-start | bytes 49160 | tf_op jit(solution)/shard_map/ppermute | solution.py:626
  318.1 21.5 %collective-permute-start.10 = (f32[2,2,16,256]{3,2,1,0:T(8,128)S(1)}, f32[2,2,16,256]{3,2,1,0:T(8,128)S(1)}, u32[]{:S(2)}, u32[]{:S(2)}) collective-permute-start(f32[2,2,16,256]{3,2,1,0:T(8,128)S(1)} %get-tuple-element.93), channel_id=1, source_target_pairs={{0,32},{32,0},{64,96},{96,64},{128,160},{160,128},{192,224},{224,1... | collective-permute-start | bytes 196616 | tf_op jit(solution)/shard_map/ppermute | solution.py:616
  (2 other events, 1.7 us)

commit v5 on v4

--- a/solution.py
+++ b/solution.py
@@ -22,7 +22,7 @@
 
 f32 = jnp.float32
 bf16 = jnp.bfloat16
-VMEM_LIMIT = 52 * 1024 * 1024
+VMEM_LIMIT = 48 * 1024 * 1024
 ALMOST_ALL_VMEM = 60 * 1024 * 1024
 smem = pl.BlockSpec(memory_space=pltpu.SMEM)
 vmem = pl.BlockSpec(memory_space=pltpu.VMEM)

time: 341 us -> 330 us (0.968)
  Pallas kernels: 63.3 us -> 50 us
  local copies, waits for them, and re-layouts: 2.98 us -> 8.62 us
    unnamed x26 -> x36, local copies, waits for them, and re-layouts: 2.98 us -> 8.62 us
    pallas_call x4, Pallas kernels: 9.72 us -> 5.49 us  [body(): call(functools.partial(last_kernel, stage), (field_shape, shape(TR // RB,...]
    pallas_call x3, Pallas kernels: 7.37 us -> 3.31 us  [body(): call(functools.partial(enter_kernel, stage), (slot_shape, field_shape), [...]
  transfers between devices with their start and end apart: 13 -> 13, of which waited for: 8 -> 8; matrix products, arithmetic and copies ran while one was open for 0% -> 0% of each run, Pallas kernels for 5% -> 4%
where the time goes in v5:
time: 330 us; the launch traced here: 329 us
  blocking collectives  204 us (62%)
  Pallas kernels  50 us (15%)
  starting transfers between devices  45.7 us (14%)
  waiting for transfers between devices  20.2 us (6%)
  local copies, waits for them, and re-layouts  8.62 us (3%)
    all_to_all x14, blocking collectives, exchange(): lax.all_to_all(value, 'front', split_axis=0, concat_axis=0, tiled=True)  204 us
    ppermute x8, starting transfers between devices, across_cores(): lax.ppermute(value, 'layer', [(index, index ^ 1) for index in range(layer...  27.3 us
    pallas_call x4, Pallas kernels, body(): call(middle, (field_shape, slot_shape, field_shape), [smem] * 3 + [vmem]...  14.1 us
    all_to_all x2, starting transfers between devices, exchange(): lax.all_to_all(value, 'front', split_axis=0, concat_axis=0, tiled=True)  13.2 us
    pallas_call x7, Pallas kernels, separator(): call(functools.partial(separator_kernel, stage, step), slot_shape, [smem]...  9.05 us
    unnamed x36, local copies, waits for them, and re-layouts  8.62 us
    ppermute x3, waiting for transfers between devices, to_next_stage(): return lax.ppermute(value, 'layer', pairs)  8.56 us
    all_to_all x2, waiting for transfers between devices, exchange(): lax.all_to_all(value, 'front', split_axis=0, concat_axis=0, tiled=True)  8.53 us
  transfers between devices with their start and end apart: 13, of which 8 were waited for; matrix products, arithmetic and copies ran while one was open for 0% of the time, Pallas kernels for 4%

profile of v5, /device:TPU:1, one launch (start us, length us, event | category | flops | bytes accessed | tf_op | source)
XLA Modules:
  0.0 329.3 jit_solution(2503511080679027747)
XLA Ops:
  11.9 9.3 %all-to-all-start = ((f32[32,24,128]{2,1,0:T(8,128)}), f32[32,24,128]{2,1,0:T(8,128)S(1)}, u32[]{:S(2)}, u32[]{:S(2)}) async-start(f32[32,24,128]{2,1,0:T(8,128)} %get-tuple-element.55.after_ref), calls=%async_computation | async-start | bytes 786432 | tf_op jit(solution)/shard_map/all_to_all | solution.py:620
  26.4 4.5 %shard_map.106 = (f32[2,768,256]{2,1,0:T(8,128)}, f32[2,256,512]{2,1,0:T(8,128)S(1)}, bf16[2,2,512,256]{3,2,1,0:T(8,128)(2,1)S(1)}) custom-call(f32[32,24,128]{2,1,0:T(8,128)} %get-tuple-element.55.after_ref, f32[2,256,256]{2,1,0:T(8,128)S(1)} %bitcast.19, f32[2,512,256]{2,1,0:T(8,128)S(1)} %bitcast.17, f32[2,128,256]{2,1,0:T(8,128)S(1)} %bitcast.22, ...), custom_call_target="tpu_custom_call" | custom-call | flops 4000000000 | bytes 5000000 | tf_op jit(solution)/shard_map/pallas_call | solution.py:685
  30.8 4.7 %all-to-all-done.arrived_ref = f32[32,24,128]{2,1,0:T(8,128)S(1)} async-done(((f32[32,24,128]{2,1,0:T(8,128)}), f32[32,24,128]{2,1,0:T(8,128)S(1)}, u32[]{:S(2)}, u32[]{:S(2)}) %all-to-all-start) | async-done | bytes 393248 | tf_op jit(solution)/shard_map/all_to_all | solution.py:620
  39.8 3.9 %all-to-all-start.1 = ((f32[64,8,128]{2,1,0:T(8,128)}), f32[64,8,128]{2,1,0:T(8,128)S(1)}, u32[]{:S(2)}, u32[]{:S(2)}) async-start(f32[64,8,128]{2,1,0:T(8,128)} %get-tuple-element.65), calls=%async_computation.1 | async-start | bytes 524288 | tf_op jit(solution)/shard_map/all_to_all | solution.py:620
  46.6 4.8 %shard_map.108 = (f32[2,2,16,8,128]{4,3,2,1,0:T(8,128)S(1)}, f32[2,2,256,128]{3,2,1,0:T(8,128)S(1)}, bf16[2,2,512,512]{3,2,1,0:T(8,128)(2,1)}, bf16[2,2,1536,256]{3,2,1,0:T(8,128)(2,1)}) custom-call(f32[2,16,8,128]{3,2,1,0:T(8,128)S(1)} %copy-done.6, f32[2,16,8,128]{3,2,1,0:T(8,128)S(1)} %collective-permute-done.2.other_u_ref.other_u_hbm, ...), custom_call_target="tpu_custom_call" | custom-call | flops 10000000 | bytes 12000000 | tf_op jit(solution)/shard_map/pallas_call | solution.py:723
  51.5 3.8 %all-to-all-done.1.refs_7_ = f32[64,8,128]{2,1,0:T(8,128)S(1)} async-done(((f32[64,8,128]{2,1,0:T(8,128)}), f32[64,8,128]{2,1,0:T(8,128)S(1)}, u32[]{:S(2)}, u32[]{:S(2)}) %all-to-all-start.1) | async-done | bytes 262176 | tf_op jit(solution)/shard_map/all_to_all | solution.py:620
  56.9 3.6 %shard_map.109 = (f32[256,128]{1,0:T(8,128)S(1)}, f32[64,8,128]{2,1,0:T(8,128)S(1)}, f32[256,128]{1,0:T(8,128)S(1)}) custom-call(s32[1]{0:T(128)} %bitcast.place_ref.refs_0_, s32[16]{0:T(128)S(1)} %get-tuple-element.51.refs_1_.own_slots_ref, s32[16]{0:T(128)S(1)} %get-tuple-element.52.refs_2_.other_slots_ref, ...), custom_call_target="tpu_custom_call" | custom-call | flops 300000000 | bytes 3000000 | tf_op jit(solution)/shard_map/pallas_call | solution.py:771
  60.5 17.0 %all_to_all.80.arrived_ref = f32[64,8,128]{2,1,0:T(8,128)S(1)} all-to-all(f32[64,8,128]{2,1,0:T(8,128)S(1)} %get-tuple-element.68), channel_id=1, replica_groups=mesh['layer'=8,'front'=32] {'front'}, dimensions={0} | all-to-all | bytes 524288 | tf_op jit(solution)/shard_map/all_to_all | solution.py:620
  78.9 15.0 %all_to_all.81.returned_ref = f32[64,8,128]{2,1,0:T(8,128)S(1)} all-to-all(f32[64,8,128]{2,1,0:T(8,128)S(1)} %shard_map.110), channel_id=1, replica_groups=mesh['layer'=8,'front'=32] {'front'}, dimensions={0} | all-to-all | bytes 524288 | tf_op jit(solution)/shard_map/all_to_all | solution.py:620
  100.3 15.3 %all_to_all.82.arrived_ref = f32[64,8,128]{2,1,0:T(8,128)S(1)} all-to-all(f32[64,8,128]{2,1,0:T(8,128)S(1)} %get-tuple-element.72), channel_id=1, replica_groups=mesh['layer'=8,'front'=32] {'front'}, dimensions={0} | all-to-all | bytes 524288 | tf_op jit(solution)/shard_map/all_to_all | solution.py:620
  116.9 14.0 %all_to_all.83.refs_7_ = f32[64,8,128]{2,1,0:T(8,128)S(1)} all-to-all(f32[64,8,128]{2,1,0:T(8,128)S(1)} %shard_map.113), channel_id=1, replica_groups=mesh['layer'=8,'front'=32] {'front'}, dimensions={0} | all-to-all | bytes 524288 | tf_op jit(solution)/shard_map/all_to_all | solution.py:620
  134.4 13.9 %all_to_all.84.arrived_ref = f32[64,8,128]{2,1,0:T(8,128)S(1)} all-to-all(f32[64,8,128]{2,1,0:T(8,128)S(1)} %get-tuple-element.75), channel_id=1, replica_groups=mesh['layer'=8,'front'=32] {'front'}, dimensions={0} | all-to-all | bytes 524288 | tf_op jit(solution)/shard_map/all_to_all | solution.py:620
  149.6 13.9 %all_to_all.85.returned_ref = f32[64,8,128]{2,1,0:T(8,128)S(1)} all-to-all(f32[64,8,128]{2,1,0:T(8,128)S(1)} %shard_map.115), channel_id=1, replica_groups=mesh['layer'=8,'front'=32] {'front'}, dimensions={0} | all-to-all | bytes 524288 | tf_op jit(solution)/shard_map/all_to_all | solution.py:620
  166.5 13.8 %all_to_all.86.arrived_ref = f32[64,8,128]{2,1,0:T(8,128)S(1)} all-to-all(f32[64,8,128]{2,1,0:T(8,128)S(1)} %get-tuple-element.79), channel_id=1, replica_groups=mesh['layer'=8,'front'=32] {'front'}, dimensions={0} | all-to-all | bytes 524288 | tf_op jit(solution)/shard_map/all_to_all | solution.py:620
  181.5 13.8 %all_to_all.87.refs_7_ = f32[64,8,128]{2,1,0:T(8,128)S(1)} all-to-all(f32[64,8,128]{2,1,0:T(8,128)S(1)} %shard_map.118), channel_id=1, replica_groups=mesh['layer'=8,'front'=32] {'front'}, dimensions={0} | all-to-all | bytes 524288 | tf_op jit(solution)/shard_map/all_to_all | solution.py:620
  195.3 3.5 %shard_map.119 = (f32[256,128]{1,0:T(8,128)S(1)}, f32[64,8,128]{2,1,0:T(8,128)S(1)}, f32[256,128]{1,0:T(8,128)S(1)}) custom-call(s32[1]{0:T(128)} %bitcast.place_ref.refs_0_, s32[16]{0:T(128)S(1)} %get-tuple-element.51.refs_1_.own_slots_ref, s32[16]{0:T(128)S(1)} %get-tuple-element.52.refs_2_.other_slots_ref, ...), custom_call_target="tpu_custom_call" | custom-call | flops 300000000 | bytes 3000000 | tf_op jit(solution)/shard_map/pallas_call | solution.py:771
  198.8 13.8 %all_to_all.88.arrived_ref = f32[64,8,128]{2,1,0:T(8,128)S(1)} all-to-all(f32[64,8,128]{2,1,0:T(8,128)S(1)} %get-tuple-element.82), channel_id=1, replica_groups=mesh['layer'=8,'front'=32] {'front'}, dimensions={0} | all-to-all | bytes 524288 | tf_op jit(solution)/shard_map/all_to_all | solution.py:620
  213.8 13.8 %all_to_all.89.returned_ref = f32[64,8,128]{2,1,0:T(8,128)S(1)} all-to-all(f32[64,8,128]{2,1,0:T(8,128)S(1)} %shard_map.120), channel_id=1, replica_groups=mesh['layer'=8,'front'=32] {'front'}, dimensions={0} | all-to-all | bytes 524288 | tf_op jit(solution)/shard_map/all_to_all | solution.py:620
  230.1 7.7 %collective-permute-done.9.trace_ref = f32[4,8,128]{2,1,0:T(8,128)S(1)} collective-permute-done((f32[4,8,128]{2,1,0:T(8,128)S(1)}, f32[4,8,128]{2,1,0:T(8,128)S(1)}, u32[]{:S(2)}, u32[]{:S(2)}) %collective-permute-start.9) | collective-permute-done | bytes 16416 | tf_op jit(solution)/shard_map/ppermute | solution.py:626
  238.9 13.5 %all_to_all.90.arrived_ref = f32[64,8,128]{2,1,0:T(8,128)S(1)} all-to-all(f32[64,8,128]{2,1,0:T(8,128)S(1)} %get-tuple-element.86), channel_id=1, replica_groups=mesh['layer'=8,'front'=32] {'front'}, dimensions={0} | all-to-all | bytes 524288 | tf_op jit(solution)/shard_map/all_to_all | solution.py:620
  253.7 15.5 %all_to_all.91.refs_7_ = f32[64,8,128]{2,1,0:T(8,128)S(1)} all-to-all(f32[64,8,128]{2,1,0:T(8,128)S(1)} %shard_map.123), channel_id=1, replica_groups=mesh['layer'=8,'front'=32] {'front'}, dimensions={0} | all-to-all | bytes 524288 | tf_op jit(solution)/shard_map/all_to_all | solution.py:620
  272.7 16.6 %all_to_all.92.arrived_ref = f32[64,8,128]{2,1,0:T(8,128)S(1)} all-to-all(f32[64,8,128]{2,1,0:T(8,128)S(1)} %get-tuple-element.89), channel_id=1, replica_groups=mesh['layer'=8,'front'=32] {'front'}, dimensions={0} | all-to-all | bytes 524288 | tf_op jit(solution)/shard_map/all_to_all | solution.py:620
  290.6 14.1 %all_to_all.93.returned_ref = f32[64,8,128]{2,1,0:T(8,128)S(1)} all-to-all(f32[64,8,128]{2,1,0:T(8,128)S(1)} %shard_map.125), channel_id=1, replica_groups=mesh['layer'=8,'front'=32] {'front'}, dimensions={0} | all-to-all | bytes 524288 | tf_op jit(solution)/shard_map/all_to_all | solution.py:620
  307.4 20.3 %collective-permute-start.10 = (f32[2,2,16,256]{3,2,1,0:T(8,128)S(1)}, f32[2,2,16,256]{3,2,1,0:T(8,128)S(1)}, u32[]{:S(2)}, u32[]{:S(2)}) collective-permute-start(f32[2,2,16,256]{3,2,1,0:T(8,128)S(1)} %get-tuple-element.93), channel_id=1, source_target_pairs={{0,32},{32,0},{64,96},{96,64},{128,160},{160,128},{192,224},{224,1... | collective-permute-start | bytes 196616 | tf_op jit(solution)/shard_map/ppermute | solution.py:616
  (77 shorter events, 58.4 us)
Async XLA Ops:
  0.6 6.9 %copy-start.8 = (s32[1,1,16,1]{2,3,1,0:T(1,128)S(1)}, s32[1,1,16,1]{2,3,1,0:T(1,128)}, u32[]{:S(2)}) copy-start(s32[1,1,16,1]{2,3,1,0:T(1,128)} %param.16) | copy-start | bytes 196
  0.6 7.4 %copy-start.9 = (s32[1,1,16]{2,1,0:T(1,128)S(1)}, s32[1,1,16]{2,1,0:T(1,128)}, u32[]{:S(2)}) copy-start(s32[1,1,16]{2,1,0:T(1,128)} %param.17) | copy-start | bytes 196
  0.7 20.5 %collective-permute-start.4 = (f32[2,256,256]{2,1,0:T(8,128)}, f32[2,256,256]{2,1,0:T(8,128)S(1)}, u32[]{:S(2)}, u32[]{:S(2)}) collective-permute-start(f32[2,256,256]{2,1,0:T(8,128)} %bitcast.20), channel_id=1, source_target_pairs={{0,32},{32,0},{64,96},{96,64},{128,160},{160,128},{192,224},{224,1... | collective-permute-start | bytes 1572872 | tf_op jit(solution)/shard_map/ppermute | solution.py:616
  4.0 18.0 %copy-start.15 = (f32[1,1,2,128,256]{4,3,2,1,0:T(8,128)S(1)}, f32[1,1,2,128,256]{4,3,2,1,0:T(8,128)}, u32[]{:S(2)}) copy-start(f32[1,1,2,128,256]{4,3,2,1,0:T(8,128)} %param.14) | copy-start | bytes 786436
  4.0 18.0 %copy-start.16 = (f32[1,1,2,128,256]{4,3,2,1,0:T(8,128)S(1)}, f32[1,1,2,128,256]{4,3,2,1,0:T(8,128)}, u32[]{:S(2)}) copy-start(f32[1,1,2,128,256]{4,3,2,1,0:T(8,128)} %param.15) | copy-start | bytes 786436
  7.4 1.7 collective-permute-start.2
  7.6 1.3 collective-permute-start
  8.0 1.1 collective-permute-start.1
  11.9 23.6 %all-to-all-start = ((f32[32,24,128]{2,1,0:T(8,128)}), f32[32,24,128]{2,1,0:T(8,128)S(1)}, u32[]{:S(2)}, u32[]{:S(2)}) async-start(f32[32,24,128]{2,1,0:T(8,128)} %get-tuple-element.55.after_ref), calls=%async_computation | async-start | bytes 786432 | tf_op jit(solution)/shard_map/all_to_all | solution.py:620
  35.5 8.2 %copy-start.17 = (f32[2,256,128]{2,1,0:T(8,128)S(1)}, f32[2,256,128]{2,1,0:T(8,128)}, u32[]{:S(2)}) copy-start(f32[2,256,128]{2,1,0:T(8,128)} %get-tuple-element.54) | copy-start | bytes 786436
  35.5 10.2 %copy-start.6 = (f32[2,16,8,128]{3,2,1,0:T(8,128)S(1)}, f32[2,16,8,128]{3,2,1,0:T(8,128)}, u32[]{:S(2)}) copy-start(f32[2,16,8,128]{3,2,1,0:T(8,128)} %get-tuple-element.49.own_u_ref.own_u_hbm) | copy-start | bytes 393220
  37.6 8.1 %collective-permute-start.6 = (f32[2,768,256]{2,1,0:T(8,128)}, f32[2,768,256]{2,1,0:T(8,128)}, u32[]{:S(2)}, u32[]{:S(2)}) collective-permute-start(f32[2,768,256]{2,1,0:T(8,128)} %get-tuple-element.60.own_forward_hbm), channel_id=1, source_target_pairs={{0,32},{32,0},{64,96},{96,64},{128,160},{160,128},{192,224},{224,1... | collective-permute-start | bytes 4718600 | tf_op jit(solution)/shard_map/ppermute | solution.py:616
  39.7 6.0 %collective-permute-start.5 = (f32[2,256,512]{2,1,0:T(8,128)S(1)}, f32[2,256,512]{2,1,0:T(8,128)}, u32[]{:S(2)}, u32[]{:S(2)}) collective-permute-start(f32[2,256,512]{2,1,0:T(8,128)S(1)} %get-tuple-element.59.own_back_hbm), channel_id=1, source_target_pairs={{0,32},{32,0},{64,96},{96,64},{128,160},{160,128},{192,224},{224,1... | collective-permute-start | bytes 3145736 | tf_op jit(solution)/shard_map/ppermute | solution.py:616
  39.8 15.5 %all-to-all-start.1 = ((f32[64,8,128]{2,1,0:T(8,128)}), f32[64,8,128]{2,1,0:T(8,128)S(1)}, u32[]{:S(2)}, u32[]{:S(2)}) async-start(f32[64,8,128]{2,1,0:T(8,128)} %get-tuple-element.65), calls=%async_computation.1 | async-start | bytes 524288 | tf_op jit(solution)/shard_map/all_to_all | solution.py:620
  43.7 1.9 collective-permute-start.3
  55.3 1.6 copy-start.3
  56.9 37.0 %copy-start.4 = (bf16[2,2,512,512]{3,2,1,0:T(8,128)(2,1)S(1)}, bf16[2,2,512,512]{3,2,1,0:T(8,128)(2,1)}, u32[]{:S(2)}) copy-start(bf16[2,2,512,512]{3,2,1,0:T(8,128)(2,1)} %get-tuple-element.64.refs_6_.backs_ref) | copy-start | bytes 6291460
  77.6 21.6 %copy-start = (bf16[2,2,1536,256]{3,2,1,0:T(8,128)(2,1)S(1)}, bf16[2,2,1536,256]{3,2,1,0:T(8,128)(2,1)}, u32[]{:S(2)}) copy-start(bf16[2,2,1536,256]{3,2,1,0:T(8,128)(2,1)} %get-tuple-element.63.refs_5_.forwards_ref) | copy-start | bytes 9437188
  95.1 4.1 %collective-permute-start.7 = (f32[4,8,128]{2,1,0:T(8,128)S(1)}, f32[4,8,128]{2,1,0:T(8,128)S(1)}, u32[]{:S(2)}, u32[]{:S(2)}) collective-permute-start(f32[4,8,128]{2,1,0:T(8,128)S(1)} %get-tuple-element.71), channel_id=1, source_target_pairs={{0,64},{32,96},{192,128},{224,160},{1,65},{33,97},{193,129},{225,1... | collective-permute-start | bytes 49160 | tf_op jit(solution)/shard_map/ppermute | solution.py:626
  148.3 17.1 %copy-start.1 = (bf16[2,2,1536,256]{3,2,1,0:T(8,128)(2,1)S(1)}, bf16[2,2,1536,256]{3,2,1,0:T(8,128)(2,1)}, u32[]{:S(2)}) copy-start(bf16[2,2,1536,256]{3,2,1,0:T(8,128)(2,1)} %get-tuple-element.63.refs_5_.forwards_ref) | copy-start | bytes 9437188
  164.7 0.7 collective-permute-start.8
  212.5 25.3 %copy-start.2 = (bf16[2,2,1536,256]{3,2,1,0:T(8,128)(2,1)S(1)}, bf16[2,2,1536,256]{3,2,1,0:T(8,128)(2,1)}, u32[]{:S(2)}) copy-start(bf16[2,2,1536,256]{3,2,1,0:T(8,128)(2,1)} %get-tuple-element.63.refs_5_.forwards_ref) | copy-start | bytes 9437188
  228.8 9.0 %collective-permute-start.9 = (f32[4,8,128]{2,1,0:T(8,128)S(1)}, f32[4,8,128]{2,1,0:T(8,128)S(1)}, u32[]{:S(2)}, u32[]{:S(2)}) collective-permute-start(f32[4,8,128]{2,1,0:T(8,128)S(1)} %get-tuple-element.85), channel_id=1, source_target_pairs={{128,192},{160,224},{64,0},{96,32},{129,193},{161,225},{65,1},{97,... | collective-permute-start | bytes 49160 | tf_op jit(solution)/shard_map/ppermute | solution.py:626
  307.4 21.2 %collective-permute-start.10 = (f32[2,2,16,256]{3,2,1,0:T(8,128)S(1)}, f32[2,2,16,256]{3,2,1,0:T(8,128)S(1)}, u32[]{:S(2)}, u32[]{:S(2)}) collective-permute-start(f32[2,2,16,256]{3,2,1,0:T(8,128)S(1)} %get-tuple-element.93), channel_id=1, source_target_pairs={{0,32},{32,0},{64,96},{96,64},{128,160},{160,128},{192,224},{224,1... | collective-permute-start | bytes 196616 | tf_op jit(solution)/shard_map/ppermute | solution.py:616
  (7 other events, 7.0 us)

commit v6 on v3

--- a/solution.py
+++ b/solution.py
@@ -441,13 +441,11 @@
     other_slots_ref,
     u_ref,
     y_ref,
-    forwards_ref,
+    forward,
     send_ref,
     base_ref,
 ):
-    driven = stacked_product(
-        forwards_ref[choice, sweep], jnp.concatenate([trace, trace_turned], axis=0)
-    )
+    driven = stacked_product(forward, jnp.concatenate([trace, trace_turned], axis=0))
     packed = pack(driven[: NB * RB]) + u_ref[choice, sweep]
     send_blocks(choice, own_slots_ref, other_slots_ref, packed, send_ref)
     base_ref[...] = driven[NB * RB :] + y_ref[choice, sweep]
@@ -464,20 +462,25 @@
     other_slots_ref,
     u_ref,
     y_ref,
-    forwards_ref,
+    forwards_hbm,
     backs_ref,
     returned_ref,
     base_refs,
     field_ref,
     send_ref,
     next_base_ref,
+    forward_ref,
+    semaphore,
 ):
     sweep, first = stage_place(place_ref, stage)
+    copy = pltpu.make_async_copy(forwards_hbm.at[1 - first, sweep], forward_ref, semaphore)
+    copy.start()
     base = base_refs[0][...] if base_refs else y_ref[first, sweep]
     field_ref[...] = leaf_finish(
         first, own_slots_ref, other_slots_ref, returned_ref, backs_ref, base
     )
     trace = trace_rows(sweep, field_ref)
+    copy.wait()
     leaf_begin(
         sweep,
         1 - first,
@@ -487,7 +490,7 @@
         other_slots_ref,
         u_ref,
         y_ref,
-        forwards_ref,
+        forward_ref[...],
         send_ref,
         next_base_ref,
     )
@@ -534,7 +537,7 @@
         other_slots_ref,
         u_ref,
         y_ref,
-        forwards_ref,
+        forwards_ref[first, sweep],
         send_ref,
         next_base_ref,
     )
@@ -760,9 +763,13 @@
         field, send, base = call(
             middle,
             (field_shape, slot_shape, field_shape),
-            [smem] * 3 + [vmem] * (5 + len(bases)),
+            [smem] * 3 + [vmem] * 2 + [hbm] + [vmem] * (2 + len(bases)),
             (vmem,) * 3,
-            cost=cost_of(300_000_000, 3_000_000),
+            [
+                pltpu.VMEM((2 * (NB * RB + P_SIZE), 2 * TR), bf16),
+                pltpu.SemaphoreType.DMA,
+            ],
+            cost_of(300_000_000, 3_000_000),
         )(place, own_slots, other_slots, u, y, forwards, backs, returned, *bases)
         fields.append(field)
         returned = exchange(separator(stage, 1, exchange(send)))

time: 328 us -> 326 us (level)
  no operation moved by 1% of the time
where the time goes in v6:
time: 326 us; the launch traced here: 324 us
  blocking collectives  203 us (62%)
  starting transfers between devices  45.7 us (14%)
  Pallas kernels  45.5 us (14%)
  waiting for transfers between devices  20.1 us (6%)
  local copies, waits for them, and re-layouts  8.62 us (3%)
    all_to_all x14, blocking collectives, exchange(): lax.all_to_all(value, 'front', split_axis=0, concat_axis=0, tiled=True)  203 us
    ppermute x8, starting transfers between devices, across_cores(): lax.ppermute(value, 'layer', [(index, index ^ 1) for index in range(layer...  27.3 us
    all_to_all x2, starting transfers between devices, exchange(): lax.all_to_all(value, 'front', split_axis=0, concat_axis=0, tiled=True)  13.2 us
    pallas_call x4, Pallas kernels, body(): call(middle, (field_shape, slot_shape, field_shape), [smem] * 3 + [vmem]...  9.89 us
    pallas_call x7, Pallas kernels, separator(): call(functools.partial(separator_kernel, stage, step), slot_shape, [smem]...  9.23 us
    unnamed x36, local copies, waits for them, and re-layouts  8.62 us
    ppermute x3, waiting for transfers between devices, to_next_stage(): return lax.ppermute(value, 'layer', pairs)  8.53 us
    all_to_all x2, waiting for transfers between devices, exchange(): lax.all_to_all(value, 'front', split_axis=0, concat_axis=0, tiled=True)  8.53 us
  transfers between devices with their start and end apart: 13, of which 8 were waited for; matrix products, arithmetic and copies ran while one was open for 0% of the time, Pallas kernels for 4%

profile of v6, /device:TPU:1, one launch (start us, length us, event | category | flops | bytes accessed | tf_op | source)
XLA Modules:
  0.0 324.4 jit_solution(15871318119883372754)
XLA Ops:
  0.7 3.3 %collective-permute-start.4 = (f32[2,256,256]{2,1,0:T(8,128)}, f32[2,256,256]{2,1,0:T(8,128)S(1)}, u32[]{:S(2)}, u32[]{:S(2)}) collective-permute-start(f32[2,256,256]{2,1,0:T(8,128)} %bitcast.20), channel_id=1, source_target_pairs={{0,32},{32,0},{64,96},{96,64},{128,160},{160,128},{192,224},{224,1... | collective-permute-start | bytes 1572872 | tf_op jit(solution)/shard_map/ppermute | solution.py:608
  4.0 3.4 %shard_map.104 = (f32[2,16,8,128]{3,2,1,0:T(8,128)}, f32[2,16,8,128]{3,2,1,0:T(8,128)}, f32[2,256,128]{2,1,0:T(8,128)}, f32[2,256,128]{2,1,0:T(8,128)}) custom-call(s32[1]{0:T(128)} %bitcast.place_ref.refs_0_, f32[2,32,256]{2,1,0:T(8,128)} %bitcast.24, f32[2,32,256]{2,1,0:T(8,128)} %bitcast.25, f32[2,256,256]{2,1,0:T(8,128)} %bitcast.18, f32[2,512,256]{2,1,0:T(8,128)} %bitcast.16), custom_call_target="tpu_custom_call" | custom-call | flops 600000000 | bytes 2500000 | tf_op jit(solution)/shard_map/pallas_call | solution.py:649
  11.9 9.3 %all-to-all-start = ((f32[32,24,128]{2,1,0:T(8,128)}), f32[32,24,128]{2,1,0:T(8,128)S(1)}, u32[]{:S(2)}, u32[]{:S(2)}) async-start(f32[32,24,128]{2,1,0:T(8,128)} %get-tuple-element.55.after_ref), calls=%async_computation | async-start | bytes 786432 | tf_op jit(solution)/shard_map/all_to_all | solution.py:612
  26.4 4.5 %shard_map.106 = (f32[2,768,256]{2,1,0:T(8,128)}, f32[2,256,512]{2,1,0:T(8,128)S(1)}, bf16[2,2,512,256]{3,2,1,0:T(8,128)(2,1)S(1)}) custom-call(f32[32,24,128]{2,1,0:T(8,128)} %get-tuple-element.55.after_ref, f32[2,256,256]{2,1,0:T(8,128)S(1)} %bitcast.19, f32[2,512,256]{2,1,0:T(8,128)S(1)} %bitcast.17, f32[2,128,256]{2,1,0:T(8,128)S(1)} %bitcast.22, ...), custom_call_target="tpu_custom_call" | custom-call | flops 4000000000 | bytes 5000000 | tf_op jit(solution)/shard_map/pallas_call | solution.py:677
  30.8 4.7 %all-to-all-done.arrived_ref = f32[32,24,128]{2,1,0:T(8,128)S(1)} async-done(((f32[32,24,128]{2,1,0:T(8,128)}), f32[32,24,128]{2,1,0:T(8,128)S(1)}, u32[]{:S(2)}, u32[]{:S(2)}) %all-to-all-start) | async-done | bytes 393248 | tf_op jit(solution)/shard_map/all_to_all | solution.py:612
  39.8 3.9 %all-to-all-start.1 = ((f32[64,8,128]{2,1,0:T(8,128)}), f32[64,8,128]{2,1,0:T(8,128)S(1)}, u32[]{:S(2)}, u32[]{:S(2)}) async-start(f32[64,8,128]{2,1,0:T(8,128)} %get-tuple-element.65), calls=%async_computation.1 | async-start | bytes 524288 | tf_op jit(solution)/shard_map/all_to_all | solution.py:612
  46.7 4.8 %shard_map.108 = (f32[2,2,16,8,128]{4,3,2,1,0:T(8,128)S(1)}, f32[2,2,256,128]{3,2,1,0:T(8,128)S(1)}, bf16[2,2,512,512]{3,2,1,0:T(8,128)(2,1)}, bf16[2,2,1536,256]{3,2,1,0:T(8,128)(2,1)}) custom-call(f32[2,16,8,128]{3,2,1,0:T(8,128)S(1)} %copy-done.6, f32[2,16,8,128]{3,2,1,0:T(8,128)S(1)} %collective-permute-done.2.other_u_ref.other_u_hbm, ...), custom_call_target="tpu_custom_call" | custom-call | flops 10000000 | bytes 12000000 | tf_op jit(solution)/shard_map/pallas_call | solution.py:715
  51.5 3.8 %all-to-all-done.1.refs_7_ = f32[64,8,128]{2,1,0:T(8,128)S(1)} async-done(((f32[64,8,128]{2,1,0:T(8,128)}), f32[64,8,128]{2,1,0:T(8,128)S(1)}, u32[]{:S(2)}, u32[]{:S(2)}) %all-to-all-start.1) | async-done | bytes 262176 | tf_op jit(solution)/shard_map/all_to_all | solution.py:612
  59.5 17.1 %all_to_all.80.arrived_ref = f32[64,8,128]{2,1,0:T(8,128)S(1)} all-to-all(f32[64,8,128]{2,1,0:T(8,128)S(1)} %get-tuple-element.68), channel_id=1, replica_groups=mesh['layer'=8,'front'=32] {'front'}, dimensions={0} | all-to-all | bytes 524288 | tf_op jit(solution)/shard_map/all_to_all | solution.py:612
  77.9 15.0 %all_to_all.81.returned_ref = f32[64,8,128]{2,1,0:T(8,128)S(1)} all-to-all(f32[64,8,128]{2,1,0:T(8,128)S(1)} %shard_map.110), channel_id=1, replica_groups=mesh['layer'=8,'front'=32] {'front'}, dimensions={0} | all-to-all | bytes 524288 | tf_op jit(solution)/shard_map/all_to_all | solution.py:612
  99.2 15.3 %all_to_all.82.arrived_ref = f32[64,8,128]{2,1,0:T(8,128)S(1)} all-to-all(f32[64,8,128]{2,1,0:T(8,128)S(1)} %get-tuple-element.72), channel_id=1, replica_groups=mesh['layer'=8,'front'=32] {'front'}, dimensions={0} | all-to-all | bytes 524288 | tf_op jit(solution)/shard_map/all_to_all | solution.py:612
  115.8 14.0 %all_to_all.83.refs_7_ = f32[64,8,128]{2,1,0:T(8,128)S(1)} all-to-all(f32[64,8,128]{2,1,0:T(8,128)S(1)} %shard_map.113), channel_id=1, replica_groups=mesh['layer'=8,'front'=32] {'front'}, dimensions={0} | all-to-all | bytes 524288 | tf_op jit(solution)/shard_map/all_to_all | solution.py:612
  132.3 13.9 %all_to_all.84.arrived_ref = f32[64,8,128]{2,1,0:T(8,128)S(1)} all-to-all(f32[64,8,128]{2,1,0:T(8,128)S(1)} %get-tuple-element.75), channel_id=1, replica_groups=mesh['layer'=8,'front'=32] {'front'}, dimensions={0} | all-to-all | bytes 524288 | tf_op jit(solution)/shard_map/all_to_all | solution.py:612
  147.5 13.9 %all_to_all.85.returned_ref = f32[64,8,128]{2,1,0:T(8,128)S(1)} all-to-all(f32[64,8,128]{2,1,0:T(8,128)S(1)} %shard_map.115), channel_id=1, replica_groups=mesh['layer'=8,'front'=32] {'front'}, dimensions={0} | all-to-all | bytes 524288 | tf_op jit(solution)/shard_map/all_to_all | solution.py:612
  164.2 13.8 %all_to_all.86.arrived_ref = f32[64,8,128]{2,1,0:T(8,128)S(1)} all-to-all(f32[64,8,128]{2,1,0:T(8,128)S(1)} %get-tuple-element.79), channel_id=1, replica_groups=mesh['layer'=8,'front'=32] {'front'}, dimensions={0} | all-to-all | bytes 524288 | tf_op jit(solution)/shard_map/all_to_all | solution.py:612
  179.3 13.8 %all_to_all.87.refs_7_ = f32[64,8,128]{2,1,0:T(8,128)S(1)} all-to-all(f32[64,8,128]{2,1,0:T(8,128)S(1)} %shard_map.118), channel_id=1, replica_groups=mesh['layer'=8,'front'=32] {'front'}, dimensions={0} | all-to-all | bytes 524288 | tf_op jit(solution)/shard_map/all_to_all | solution.py:612
  195.5 13.8 %all_to_all.88.arrived_ref = f32[64,8,128]{2,1,0:T(8,128)S(1)} all-to-all(f32[64,8,128]{2,1,0:T(8,128)S(1)} %get-tuple-element.82), channel_id=1, replica_groups=mesh['layer'=8,'front'=32] {'front'}, dimensions={0} | all-to-all | bytes 524288 | tf_op jit(solution)/shard_map/all_to_all | solution.py:612
  210.6 13.8 %all_to_all.89.returned_ref = f32[64,8,128]{2,1,0:T(8,128)S(1)} all-to-all(f32[64,8,128]{2,1,0:T(8,128)S(1)} %shard_map.120), channel_id=1, replica_groups=mesh['layer'=8,'front'=32] {'front'}, dimensions={0} | all-to-all | bytes 524288 | tf_op jit(solution)/shard_map/all_to_all | solution.py:612
  226.8 7.7 %collective-permute-done.9.trace_ref = f32[4,8,128]{2,1,0:T(8,128)S(1)} collective-permute-done((f32[4,8,128]{2,1,0:T(8,128)S(1)}, f32[4,8,128]{2,1,0:T(8,128)S(1)}, u32[]{:S(2)}, u32[]{:S(2)}) %collective-permute-start.9) | collective-permute-done | bytes 16416 | tf_op jit(solution)/shard_map/ppermute | solution.py:618
  235.5 13.5 %all_to_all.90.arrived_ref = f32[64,8,128]{2,1,0:T(8,128)S(1)} all-to-all(f32[64,8,128]{2,1,0:T(8,128)S(1)} %get-tuple-element.86), channel_id=1, replica_groups=mesh['layer'=8,'front'=32] {'front'}, dimensions={0} | all-to-all | bytes 524288 | tf_op jit(solution)/shard_map/all_to_all | solution.py:612
  250.3 15.5 %all_to_all.91.refs_7_ = f32[64,8,128]{2,1,0:T(8,128)S(1)} all-to-all(f32[64,8,128]{2,1,0:T(8,128)S(1)} %shard_map.123), channel_id=1, replica_groups=mesh['layer'=8,'front'=32] {'front'}, dimensions={0} | all-to-all | bytes 524288 | tf_op jit(solution)/shard_map/all_to_all | solution.py:612
  268.3 15.7 %all_to_all.92.arrived_ref = f32[64,8,128]{2,1,0:T(8,128)S(1)} all-to-all(f32[64,8,128]{2,1,0:T(8,128)S(1)} %get-tuple-element.89), channel_id=1, replica_groups=mesh['layer'=8,'front'=32] {'front'}, dimensions={0} | all-to-all | bytes 524288 | tf_op jit(solution)/shard_map/all_to_all | solution.py:612
  285.3 14.6 %all_to_all.93.returned_ref = f32[64,8,128]{2,1,0:T(8,128)S(1)} all-to-all(f32[64,8,128]{2,1,0:T(8,128)S(1)} %shard_map.125), channel_id=1, replica_groups=mesh['layer'=8,'front'=32] {'front'}, dimensions={0} | all-to-all | bytes 524288 | tf_op jit(solution)/shard_map/all_to_all | solution.py:612
  302.5 20.2 %collective-permute-start.10 = (f32[2,2,16,256]{3,2,1,0:T(8,128)S(1)}, f32[2,2,16,256]{3,2,1,0:T(8,128)S(1)}, u32[]{:S(2)}, u32[]{:S(2)}) collective-permute-start(f32[2,2,16,256]{3,2,1,0:T(8,128)S(1)} %get-tuple-element.93), channel_id=1, source_target_pairs={{0,32},{32,0},{64,96},{96,64},{128,160},{160,128},{192,224},{224,1... | collective-permute-start | bytes 196616 | tf_op jit(solution)/shard_map/ppermute | solution.py:608
  (77 shorter events, 54.2 us)
Async XLA Ops:
  0.6 6.9 %copy-start.8 = (s32[1,1,16,1]{2,3,1,0:T(1,128)S(1)}, s32[1,1,16,1]{2,3,1,0:T(1,128)}, u32[]{:S(2)}) copy-start(s32[1,1,16,1]{2,3,1,0:T(1,128)} %param.16) | copy-start | bytes 196
  0.6 7.4 %copy-start.9 = (s32[1,1,16]{2,1,0:T(1,128)S(1)}, s32[1,1,16]{2,1,0:T(1,128)}, u32[]{:S(2)}) copy-start(s32[1,1,16]{2,1,0:T(1,128)} %param.17) | copy-start | bytes 196
  0.7 20.5 %collective-permute-start.4 = (f32[2,256,256]{2,1,0:T(8,128)}, f32[2,256,256]{2,1,0:T(8,128)S(1)}, u32[]{:S(2)}, u32[]{:S(2)}) collective-permute-start(f32[2,256,256]{2,1,0:T(8,128)} %bitcast.20), channel_id=1, source_target_pairs={{0,32},{32,0},{64,96},{96,64},{128,160},{160,128},{192,224},{224,1... | collective-permute-start | bytes 1572872 | tf_op jit(solution)/shard_map/ppermute | solution.py:608
  4.0 18.0 %copy-start.15 = (f32[1,1,2,128,256]{4,3,2,1,0:T(8,128)S(1)}, f32[1,1,2,128,256]{4,3,2,1,0:T(8,128)}, u32[]{:S(2)}) copy-start(f32[1,1,2,128,256]{4,3,2,1,0:T(8,128)} %param.14) | copy-start | bytes 786436
  4.0 18.0 %copy-start.16 = (f32[1,1,2,128,256]{4,3,2,1,0:T(8,128)S(1)}, f32[1,1,2,128,256]{4,3,2,1,0:T(8,128)}, u32[]{:S(2)}) copy-start(f32[1,1,2,128,256]{4,3,2,1,0:T(8,128)} %param.15) | copy-start | bytes 786436
  7.4 1.7 collective-permute-start.2
  7.6 1.3 collective-permute-start
  8.0 1.1 collective-permute-start.1
  11.9 23.6 %all-to-all-start = ((f32[32,24,128]{2,1,0:T(8,128)}), f32[32,24,128]{2,1,0:T(8,128)S(1)}, u32[]{:S(2)}, u32[]{:S(2)}) async-start(f32[32,24,128]{2,1,0:T(8,128)} %get-tuple-element.55.after_ref), calls=%async_computation | async-start | bytes 786432 | tf_op jit(solution)/shard_map/all_to_all | solution.py:612
  35.5 8.3 %copy-start.17 = (f32[2,256,128]{2,1,0:T(8,128)S(1)}, f32[2,256,128]{2,1,0:T(8,128)}, u32[]{:S(2)}) copy-start(f32[2,256,128]{2,1,0:T(8,128)} %get-tuple-element.54) | copy-start | bytes 786436
  35.5 10.2 %copy-start.6 = (f32[2,16,8,128]{3,2,1,0:T(8,128)S(1)}, f32[2,16,8,128]{3,2,1,0:T(8,128)}, u32[]{:S(2)}) copy-start(f32[2,16,8,128]{3,2,1,0:T(8,128)} %get-tuple-element.49.own_u_ref.own_u_hbm) | copy-start | bytes 393220
  37.6 8.1 %collective-permute-start.6 = (f32[2,768,256]{2,1,0:T(8,128)}, f32[2,768,256]{2,1,0:T(8,128)}, u32[]{:S(2)}, u32[]{:S(2)}) collective-permute-start(f32[2,768,256]{2,1,0:T(8,128)} %get-tuple-element.60.own_forward_hbm), channel_id=1, source_target_pairs={{0,32},{32,0},{64,96},{96,64},{128,160},{160,128},{192,224},{224,1... | collective-permute-start | bytes 4718600 | tf_op jit(solution)/shard_map/ppermute | solution.py:608
  39.7 6.0 %collective-permute-start.5 = (f32[2,256,512]{2,1,0:T(8,128)S(1)}, f32[2,256,512]{2,1,0:T(8,128)}, u32[]{:S(2)}, u32[]{:S(2)}) collective-permute-start(f32[2,256,512]{2,1,0:T(8,128)S(1)} %get-tuple-element.59.own_back_hbm), channel_id=1, source_target_pairs={{0,32},{32,0},{64,96},{96,64},{128,160},{160,128},{192,224},{224,1... | collective-permute-start | bytes 3145736 | tf_op jit(solution)/shard_map/ppermute | solution.py:608
  39.8 15.5 %all-to-all-start.1 = ((f32[64,8,128]{2,1,0:T(8,128)}), f32[64,8,128]{2,1,0:T(8,128)S(1)}, u32[]{:S(2)}, u32[]{:S(2)}) async-start(f32[64,8,128]{2,1,0:T(8,128)} %get-tuple-element.65), calls=%async_computation.1 | async-start | bytes 524288 | tf_op jit(solution)/shard_map/all_to_all | solution.py:612
  43.8 1.9 collective-permute-start.3
  55.3 1.6 copy-start.3
  56.9 36.0 %copy-start.4 = (bf16[2,2,512,512]{3,2,1,0:T(8,128)(2,1)S(1)}, bf16[2,2,512,512]{3,2,1,0:T(8,128)(2,1)}, u32[]{:S(2)}) copy-start(bf16[2,2,512,512]{3,2,1,0:T(8,128)(2,1)} %get-tuple-element.64.refs_6_.backs_ref) | copy-start | bytes 6291460
  76.6 21.6 %copy-start = (bf16[2,2,1536,256]{3,2,1,0:T(8,128)(2,1)S(1)}, bf16[2,2,1536,256]{3,2,1,0:T(8,128)(2,1)}, u32[]{:S(2)}) copy-start(bf16[2,2,1536,256]{3,2,1,0:T(8,128)(2,1)} %get-tuple-element.63.refs_5_.forwards_ref) | copy-start | bytes 9437188
  94.1 4.1 %collective-permute-start.7 = (f32[4,8,128]{2,1,0:T(8,128)S(1)}, f32[4,8,128]{2,1,0:T(8,128)S(1)}, u32[]{:S(2)}, u32[]{:S(2)}) collective-permute-start(f32[4,8,128]{2,1,0:T(8,128)S(1)} %get-tuple-element.71), channel_id=1, source_target_pairs={{0,64},{32,96},{192,128},{224,160},{1,65},{33,97},{193,129},{225,1... | collective-permute-start | bytes 49160 | tf_op jit(solution)/shard_map/ppermute | solution.py:618
  146.1 17.0 %copy-start.1 = (bf16[2,2,1536,256]{3,2,1,0:T(8,128)(2,1)S(1)}, bf16[2,2,1536,256]{3,2,1,0:T(8,128)(2,1)}, u32[]{:S(2)}) copy-start(bf16[2,2,1536,256]{3,2,1,0:T(8,128)(2,1)} %get-tuple-element.63.refs_5_.forwards_ref) | copy-start | bytes 9437188
  162.5 0.7 collective-permute-start.8
  209.3 25.2 %copy-start.2 = (bf16[2,2,1536,256]{3,2,1,0:T(8,128)(2,1)S(1)}, bf16[2,2,1536,256]{3,2,1,0:T(8,128)(2,1)}, u32[]{:S(2)}) copy-start(bf16[2,2,1536,256]{3,2,1,0:T(8,128)(2,1)} %get-tuple-element.63.refs_5_.forwards_ref) | copy-start | bytes 9437188
  225.5 9.0 %collective-permute-start.9 = (f32[4,8,128]{2,1,0:T(8,128)S(1)}, f32[4,8,128]{2,1,0:T(8,128)S(1)}, u32[]{:S(2)}, u32[]{:S(2)}) collective-permute-start(f32[4,8,128]{2,1,0:T(8,128)S(1)} %get-tuple-element.85), channel_id=1, source_target_pairs={{128,192},{160,224},{64,0},{96,32},{129,193},{161,225},{65,1},{97,... | collective-permute-start | bytes 49160 | tf_op jit(solution)/shard_map/ppermute | solution.py:618
  302.5 21.1 %collective-permute-start.10 = (f32[2,2,16,256]{3,2,1,0:T(8,128)S(1)}, f32[2,2,16,256]{3,2,1,0:T(8,128)S(1)}, u32[]{:S(2)}, u32[]{:S(2)}) collective-permute-start(f32[2,2,16,256]{3,2,1,0:T(8,128)S(1)} %get-tuple-element.93), channel_id=1, source_target_pairs={{0,32},{32,0},{64,96},{96,64},{128,160},{160,128},{192,224},{224,1... | collective-permute-start | bytes 196616 | tf_op jit(solution)/shard_map/ppermute | solution.py:608
  (7 other events, 7.0 us)

commit v7 on v6

--- a/solution.py
+++ b/solution.py
@@ -24,6 +24,7 @@
 bf16 = jnp.bfloat16
 VMEM_LIMIT = 48 * 1024 * 1024
 ALMOST_ALL_VMEM = 60 * 1024 * 1024
+FIRST_MIDDLE_VMEM = 58 * 1024 * 1024
 smem = pl.BlockSpec(memory_space=pltpu.SMEM)
 vmem = pl.BlockSpec(memory_space=pltpu.VMEM)
 hbm = pl.BlockSpec(memory_space=pl.ANY)
@@ -419,16 +420,17 @@
     )
 
 
-def leaf_finish(choice, own_slots_ref, other_slots_ref, returned_ref, backs_ref, base):
+def leaf_finish(choice, own_slots_ref, other_slots_ref, returned_ref, back, base):
     blocks = []
     for block in range(NB):
         slot = jnp.where(choice == 0, own_slots_ref[block], other_slots_ref[block])
         blocks.append(returned_ref[slot])
     mine, mine_turned = unpack_both(jnp.stack(blocks, axis=0))
+    real, imag = back()
     return (
         base
-        + stacked_product(backs_ref[choice, 0], mine)
-        + stacked_product(backs_ref[choice, 1], mine_turned)
+        + stacked_product(real, mine)
+        + stacked_product(imag, mine_turned)
     )
 
 
@@ -471,13 +473,25 @@
     next_base_ref,
     forward_ref,
     semaphore,
+    *back_scratch,
 ):
     sweep, first = stage_place(place_ref, stage)
     copy = pltpu.make_async_copy(forwards_hbm.at[1 - first, sweep], forward_ref, semaphore)
+    if back_scratch:
+        back_ref, back_semaphore = back_scratch
+        back_copy = pltpu.make_async_copy(backs_ref.at[first], back_ref, back_semaphore)
+        back_copy.start()
     copy.start()
+
+    def back():
+        if not back_scratch:
+            return backs_ref[first, 0], backs_ref[first, 1]
+        back_copy.wait()
+        return back_ref[0], back_ref[1]
+
     base = base_refs[0][...] if base_refs else y_ref[first, sweep]
     field_ref[...] = leaf_finish(
-        first, own_slots_ref, other_slots_ref, returned_ref, backs_ref, base
+        first, own_slots_ref, other_slots_ref, returned_ref, back, base
     )
     trace = trace_rows(sweep, field_ref)
     copy.wait()
@@ -509,7 +523,12 @@
 ):
     sweep, first = stage_place(place_ref, stage)
     field_ref[...] = leaf_finish(
-        1 - first, own_slots_ref, other_slots_ref, returned_ref, backs_ref, base_ref[...]
+        1 - first,
+        own_slots_ref,
+        other_slots_ref,
+        returned_ref,
+        lambda: (backs_ref[1 - first, 0], backs_ref[1 - first, 1]),
+        base_ref[...],
     )
     trace_ref[...] = pack(trace_rows(sweep, field_ref))
 
@@ -543,26 +562,61 @@
     )
 
 
-def collect_kernel(place_ref, field_refs, own_ref, other_ref, parts_ref, semaphores):
+def final_kernel(
+    place_ref,
+    own_slots_ref,
+    other_slots_ref,
+    backs_ref,
+    returned_ref,
+    base_ref,
+    field_refs,
+    own_ref,
+    other_ref,
+    parts_ref,
+    semaphores,
+):
     row = place_ref[0] // 2
     core = place_ref[0] % 2
+    sweep_now, first = stage_place(place_ref, 3)
+    spots, finals = [], []
     for sweep in range(2):
         for position in range(2):
             layer = position if sweep == 0 else 1 - position
-            side = jnp.where(core == layer, 0, 1)
+            spot = 2 * sweep + jnp.where(core == layer, 0, 1)
+            spots.append(spot)
             for stage in range(4):
                 active = row == stage if sweep == 0 else row == 3 - stage
+                if 2 * stage + position == len(field_refs):
+                    finals.append(active)
+                    continue
 
                 @pl.when(active)
                 def _():
                     pltpu.make_async_copy(
                         field_refs[2 * stage + position],
-                        parts_ref.at[2 * sweep + side],
+                        parts_ref.at[spot],
                         semaphores.at[2 * sweep + position],
                     ).start()
 
-    for index in range(4):
-        wait_for(field_refs[0], parts_ref.at[0], semaphores.at[index])
+    field = leaf_finish(
+        1 - first,
+        own_slots_ref,
+        other_slots_ref,
+        returned_ref,
+        lambda: (backs_ref[1 - first, 0], backs_ref[1 - first, 1]),
+        base_ref[...],
+    )
+    for sweep in range(2):
+
+        @pl.when(finals[sweep])
+        def _():
+            parts_ref[spots[2 * sweep + 1]] = field
+
+        @pl.when(jnp.logical_not(finals[sweep]))
+        def _():
+            wait_for(field_refs[0], parts_ref.at[0], semaphores.at[2 * sweep + 1])
+
+        wait_for(field_refs[0], parts_ref.at[0], semaphores.at[2 * sweep])
     group = lane_ids(P_SIZE) // GROUP
     joined = pick(group, [parts_ref[index] for index in range(4)])
     rows = joined.T.reshape(2, 2, 2, HALF, P_SIZE)
@@ -763,16 +817,28 @@
         field, send, base = call(
             middle,
             (field_shape, slot_shape, field_shape),
-            [smem] * 3 + [vmem] * 2 + [hbm] + [vmem] * (2 + len(bases)),
+            [smem] * 3
+            + [vmem] * 2
+            + [hbm]
+            + ([vmem] if bases else [hbm])
+            + [vmem] * (1 + len(bases)),
             (vmem,) * 3,
             [
                 pltpu.VMEM((2 * (NB * RB + P_SIZE), 2 * TR), bf16),
                 pltpu.SemaphoreType.DMA,
-            ],
+            ]
+            + (
+                []
+                if bases
+                else [pltpu.VMEM((2, 2 * P_SIZE, NB * RB), bf16), pltpu.SemaphoreType.DMA]
+            ),
             cost_of(300_000_000, 3_000_000),
+            VMEM_LIMIT if bases else FIRST_MIDDLE_VMEM,
         )(place, own_slots, other_slots, u, y, forwards, backs, returned, *bases)
         fields.append(field)
         returned = exchange(separator(stage, 1, exchange(send)))
+        if stage == 3:
+            break
         field, trace = call(
             functools.partial(last_kernel, stage),
             (field_shape, shape(TR // RB, 8, LANES)),
@@ -781,21 +847,20 @@
             cost=cost_of(200_000_000, 2_000_000),
         )(place, own_slots, other_slots, backs, returned, base)
         fields.append(field)
-        if stage < 3:
-            trace = to_next_stage(trace, stage)
+        trace = to_next_stage(trace, stage)
 
     half_shape = shape(2, 2, HALF, P_SIZE)
 
-    def collect(place_ref, *refs):
-        collect_kernel(place_ref, refs[:8], *refs[8:])
+    def final(*refs):
+        final_kernel(*refs[:6], refs[6 : 6 + len(fields)], *refs[6 + len(fields) :])
 
     own, to_other = call(
-        collect,
+        final,
         (half_shape, half_shape),
-        [smem] + [hbm] * 8,
+        [smem] * 3 + [vmem] * 3 + [hbm] * len(fields),
         (vmem, vmem),
         [pltpu.VMEM((4, P_SIZE, LANES), f32), pltpu.SemaphoreType.DMA((4,))],
-    )(place, *fields)
+    )(place, own_slots, other_slots, backs, returned, base, *fields)
     down, up = call(
         output_kernel,
         (shape(2, S, P_SIZE), shape(2, S, P_SIZE)),

time: 326 us -> 328 us (level)
    unnamed x36 -> x54, local copies, waits for them, and re-layouts: 8.62 us -> 9.18 us
where the time goes in v7:
time: 328 us; the launch traced here: 326 us
  blocking collectives  205 us (62%)
  starting transfers between devices  46.2 us (14%)
  Pallas kernels  45.6 us (14%)
  waiting for transfers between devices  19.4 us (6%)
  local copies, waits for them, and re-layouts  9.18 us (3%)
    all_to_all x14, blocking collectives, exchange(): lax.all_to_all(value, 'front', split_axis=0, concat_axis=0, tiled=True)  205 us
    ppermute x8, starting transfers between devices, across_cores(): lax.ppermute(value, 'layer', [(index, index ^ 1) for index in range(layer...  27.1 us
    all_to_all x2, starting transfers between devices, exchange(): lax.all_to_all(value, 'front', split_axis=0, concat_axis=0, tiled=True)  13.9 us
    pallas_call x4, Pallas kernels, body(): call(middle, (field_shape, slot_shape, field_shape), [smem] * 3 + [vmem]...  11.5 us
    pallas_call x7, Pallas kernels, separator(): call(functools.partial(separator_kernel, stage, step), slot_shape, [smem]...  9.24 us
    unnamed x54, local copies, waits for them, and re-layouts  9.18 us
    ppermute x3, waiting for transfers between devices, to_next_stage(): return lax.ppermute(value, 'layer', pairs)  8.55 us
    all_to_all x2, waiting for transfers between devices, exchange(): lax.all_to_all(value, 'front', split_axis=0, concat_axis=0, tiled=True)  7.58 us
  transfers between devices with their start and end apart: 13, of which 8 were waited for; matrix products, arithmetic and copies ran while one was open for 0% of the time, Pallas kernels for 4%

profile of v7, /device:TPU:1, one launch (start us, length us, event | category | flops | bytes accessed | tf_op | source)
XLA Modules:
  0.0 326.4 jit_solution(6927764843926319729)
XLA Ops:
  0.7 3.3 %collective-permute-start.4 = (f32[2,256,256]{2,1,0:T(8,128)}, f32[2,256,256]{2,1,0:T(8,128)S(1)}, u32[]{:S(2)}, u32[]{:S(2)}) collective-permute-start(f32[2,256,256]{2,1,0:T(8,128)} %bitcast.20), channel_id=1, source_target_pairs={{0,32},{32,0},{64,96},{96,64},{128,160},{160,128},{192,224},{224,1... | collective-permute-start | bytes 1572872 | tf_op jit(solution)/shard_map/ppermute | solution.py:662
  4.0 3.5 %shard_map.104 = (f32[2,16,8,128]{3,2,1,0:T(8,128)}, f32[2,16,8,128]{3,2,1,0:T(8,128)}, f32[2,256,128]{2,1,0:T(8,128)}, f32[2,256,128]{2,1,0:T(8,128)}) custom-call(s32[1]{0:T(128)} %bitcast.place_ref.refs_0_, f32[2,32,256]{2,1,0:T(8,128)} %bitcast.24, f32[2,32,256]{2,1,0:T(8,128)} %bitcast.25, f32[2,256,256]{2,1,0:T(8,128)} %bitcast.18, f32[2,512,256]{2,1,0:T(8,128)} %bitcast.16), custom_call_target="tpu_custom_call" | custom-call | flops 600000000 | bytes 2500000 | tf_op jit(solution)/shard_map/pallas_call | solution.py:703
  11.9 9.3 %all-to-all-start = ((f32[32,24,128]{2,1,0:T(8,128)}), f32[32,24,128]{2,1,0:T(8,128)S(1)}, u32[]{:S(2)}, u32[]{:S(2)}) async-start(f32[32,24,128]{2,1,0:T(8,128)} %get-tuple-element.54.after_ref), calls=%async_computation | async-start | bytes 786432 | tf_op jit(solution)/shard_map/all_to_all | solution.py:666
  26.3 4.4 %shard_map.106 = (f32[2,768,256]{2,1,0:T(8,128)}, f32[2,256,512]{2,1,0:T(8,128)S(1)}, bf16[2,2,512,256]{3,2,1,0:T(8,128)(2,1)S(1)}) custom-call(f32[32,24,128]{2,1,0:T(8,128)} %get-tuple-element.54.after_ref, f32[2,256,256]{2,1,0:T(8,128)S(1)} %bitcast.19, f32[2,512,256]{2,1,0:T(8,128)S(1)} %bitcast.17, f32[2,128,256]{2,1,0:T(8,128)S(1)} %bitcast.22, ...), custom_call_target="tpu_custom_call" | custom-call | flops 4000000000 | bytes 5000000 | tf_op jit(solution)/shard_map/pallas_call | solution.py:731
  30.7 4.8 %all-to-all-done.arrived_ref = f32[32,24,128]{2,1,0:T(8,128)S(1)} async-done(((f32[32,24,128]{2,1,0:T(8,128)}), f32[32,24,128]{2,1,0:T(8,128)S(1)}, u32[]{:S(2)}, u32[]{:S(2)}) %all-to-all-start) | async-done | bytes 393248 | tf_op jit(solution)/shard_map/all_to_all | solution.py:666
  39.8 4.6 %all-to-all-start.1 = ((f32[64,8,128]{2,1,0:T(8,128)}), f32[64,8,128]{2,1,0:T(8,128)}, u32[]{:S(2)}, u32[]{:S(2)}) async-start(f32[64,8,128]{2,1,0:T(8,128)} %copy-done.11), calls=%async_computation.1 | async-start | bytes 524288 | tf_op jit(solution)/shard_map/all_to_all | solution.py:666
  47.4 4.5 %shard_map.108 = (f32[2,2,16,8,128]{4,3,2,1,0:T(8,128)S(1)}, f32[2,2,256,128]{3,2,1,0:T(8,128)S(1)}, bf16[2,2,512,512]{3,2,1,0:T(8,128)(2,1)}, bf16[2,2,1536,256]{3,2,1,0:T(8,128)(2,1)}) custom-call(f32[2,16,8,128]{3,2,1,0:T(8,128)S(1)} %copy-done.9, f32[2,16,8,128]{3,2,1,0:T(8,128)S(1)} %collective-permute-done.2.other_u_ref.other_u_hbm, ...), custom_call_target="tpu_custom_call" | custom-call | flops 10000000 | bytes 12000000 | tf_op jit(solution)/shard_map/pallas_call | solution.py:769
  56.2 4.2 %shard_map.109 = (f32[256,128]{1,0:T(8,128)}, f32[64,8,128]{2,1,0:T(8,128)}, f32[256,128]{1,0:T(8,128)}) custom-call(s32[1]{0:T(128)} %bitcast.place_ref.refs_0_, s32[16]{0:T(128)} %copy-done.14, s32[16]{0:T(128)} %copy-done.16, f32[2,2,16,8,128]{4,3,2,1,0:T(8,128)} %copy-done.6, f32[2,2,256,128]{3,2,1,0:T(8,128)} %copy-done.4, ...), custom_call_target="tpu_custom_call" | custom-call | flops 300000000 | bytes 3000000 | tf_op jit(solution)/shard_map/pallas_call | solution.py:817
  60.4 18.4 %all_to_all.80.arrived_ref = f32[64,8,128]{2,1,0:T(8,128)S(1)} all-to-all(f32[64,8,128]{2,1,0:T(8,128)} %get-tuple-element.66), channel_id=1, replica_groups=mesh['layer'=8,'front'=32] {'front'}, dimensions={0} | all-to-all | bytes 524288 | tf_op jit(solution)/shard_map/all_to_all | solution.py:666
  80.1 15.1 %all_to_all.81.returned_ref = f32[64,8,128]{2,1,0:T(8,128)S(1)} all-to-all(f32[64,8,128]{2,1,0:T(8,128)S(1)} %shard_map.110), channel_id=1, replica_groups=mesh['layer'=8,'front'=32] {'front'}, dimensions={0} | all-to-all | bytes 524288 | tf_op jit(solution)/shard_map/all_to_all | solution.py:666
  101.5 15.3 %all_to_all.82.arrived_ref = f32[64,8,128]{2,1,0:T(8,128)S(1)} all-to-all(f32[64,8,128]{2,1,0:T(8,128)S(1)} %get-tuple-element.69), channel_id=1, replica_groups=mesh['layer'=8,'front'=32] {'front'}, dimensions={0} | all-to-all | bytes 524288 | tf_op jit(solution)/shard_map/all_to_all | solution.py:666
  118.2 14.0 %all_to_all.83.refs_7_ = f32[64,8,128]{2,1,0:T(8,128)S(1)} all-to-all(f32[64,8,128]{2,1,0:T(8,128)S(1)} %shard_map.113), channel_id=1, replica_groups=mesh['layer'=8,'front'=32] {'front'}, dimensions={0} | all-to-all | bytes 524288 | tf_op jit(solution)/shard_map/all_to_all | solution.py:666
  134.6 13.9 %all_to_all.84.arrived_ref = f32[64,8,128]{2,1,0:T(8,128)S(1)} all-to-all(f32[64,8,128]{2,1,0:T(8,128)S(1)} %get-tuple-element.71), channel_id=1, replica_groups=mesh['layer'=8,'front'=32] {'front'}, dimensions={0} | all-to-all | bytes 524288 | tf_op jit(solution)/shard_map/all_to_all | solution.py:666
  149.8 13.9 %all_to_all.85.returned_ref = f32[64,8,128]{2,1,0:T(8,128)S(1)} all-to-all(f32[64,8,128]{2,1,0:T(8,128)S(1)} %shard_map.115), channel_id=1, replica_groups=mesh['layer'=8,'front'=32] {'front'}, dimensions={0} | all-to-all | bytes 524288 | tf_op jit(solution)/shard_map/all_to_all | solution.py:666
  166.6 13.8 %all_to_all.86.arrived_ref = f32[64,8,128]{2,1,0:T(8,128)S(1)} all-to-all(f32[64,8,128]{2,1,0:T(8,128)S(1)} %get-tuple-element.74), channel_id=1, replica_groups=mesh['layer'=8,'front'=32] {'front'}, dimensions={0} | all-to-all | bytes 524288 | tf_op jit(solution)/shard_map/all_to_all | solution.py:666
  181.7 13.8 %all_to_all.87.refs_7_ = f32[64,8,128]{2,1,0:T(8,128)S(1)} all-to-all(f32[64,8,128]{2,1,0:T(8,128)S(1)} %shard_map.118), channel_id=1, replica_groups=mesh['layer'=8,'front'=32] {'front'}, dimensions={0} | all-to-all | bytes 524288 | tf_op jit(solution)/shard_map/all_to_all | solution.py:666
  197.9 13.7 %all_to_all.88.arrived_ref = f32[64,8,128]{2,1,0:T(8,128)S(1)} all-to-all(f32[64,8,128]{2,1,0:T(8,128)S(1)} %get-tuple-element.76), channel_id=1, replica_groups=mesh['layer'=8,'front'=32] {'front'}, dimensions={0} | all-to-all | bytes 524288 | tf_op jit(solution)/shard_map/all_to_all | solution.py:666
  212.9 13.8 %all_to_all.89.returned_ref = f32[64,8,128]{2,1,0:T(8,128)S(1)} all-to-all(f32[64,8,128]{2,1,0:T(8,128)S(1)} %shard_map.120), channel_id=1, replica_groups=mesh['layer'=8,'front'=32] {'front'}, dimensions={0} | all-to-all | bytes 524288 | tf_op jit(solution)/shard_map/all_to_all | solution.py:666
  229.2 7.7 %collective-permute-done.9.trace_ref = f32[4,8,128]{2,1,0:T(8,128)S(1)} collective-permute-done((f32[4,8,128]{2,1,0:T(8,128)S(1)}, f32[4,8,128]{2,1,0:T(8,128)S(1)}, u32[]{:S(2)}, u32[]{:S(2)}) %collective-permute-start.9) | collective-permute-done | bytes 16416 | tf_op jit(solution)/shard_map/ppermute | solution.py:672
  237.9 13.5 %all_to_all.90.arrived_ref = f32[64,8,128]{2,1,0:T(8,128)S(1)} all-to-all(f32[64,8,128]{2,1,0:T(8,128)S(1)} %get-tuple-element.79), channel_id=1, replica_groups=mesh['layer'=8,'front'=32] {'front'}, dimensions={0} | all-to-all | bytes 524288 | tf_op jit(solution)/shard_map/all_to_all | solution.py:666
  252.7 15.5 %all_to_all.91.refs_7_ = f32[64,8,128]{2,1,0:T(8,128)S(1)} all-to-all(f32[64,8,128]{2,1,0:T(8,128)S(1)} %shard_map.123), channel_id=1, replica_groups=mesh['layer'=8,'front'=32] {'front'}, dimensions={0} | all-to-all | bytes 524288 | tf_op jit(solution)/shard_map/all_to_all | solution.py:666
  270.7 16.0 %all_to_all.92.arrived_ref = f32[64,8,128]{2,1,0:T(8,128)S(1)} all-to-all(f32[64,8,128]{2,1,0:T(8,128)S(1)} %get-tuple-element.81), channel_id=1, replica_groups=mesh['layer'=8,'front'=32] {'front'}, dimensions={0} | all-to-all | bytes 524288 | tf_op jit(solution)/shard_map/all_to_all | solution.py:666
  288.0 14.5 %all_to_all.93.refs_4_ = f32[64,8,128]{2,1,0:T(8,128)S(1)} all-to-all(f32[64,8,128]{2,1,0:T(8,128)S(1)} %shard_map.125), channel_id=1, replica_groups=mesh['layer'=8,'front'=32] {'front'}, dimensions={0} | all-to-all | bytes 524288 | tf_op jit(solution)/shard_map/all_to_all | solution.py:666
  304.3 20.5 %collective-permute-start.10 = (f32[2,2,16,256]{3,2,1,0:T(8,128)S(1)}, f32[2,2,16,256]{3,2,1,0:T(8,128)S(1)}, u32[]{:S(2)}, u32[]{:S(2)}) collective-permute-start(f32[2,2,16,256]{3,2,1,0:T(8,128)S(1)} %get-tuple-element.91), channel_id=1, source_target_pairs={{0,32},{32,0},{64,96},{96,64},{128,160},{160,128},{192,224},{224,1... | collective-permute-start | bytes 196616 | tf_op jit(solution)/shard_map/ppermute | solution.py:662
  (94 shorter events, 53.5 us)
Async XLA Ops:
  0.7 20.5 %collective-permute-start.4 = (f32[2,256,256]{2,1,0:T(8,128)}, f32[2,256,256]{2,1,0:T(8,128)S(1)}, u32[]{:S(2)}, u32[]{:S(2)}) collective-permute-start(f32[2,256,256]{2,1,0:T(8,128)} %bitcast.20), channel_id=1, source_target_pairs={{0,32},{32,0},{64,96},{96,64},{128,160},{160,128},{192,224},{224,1... | collective-permute-start | bytes 1572872 | tf_op jit(solution)/shard_map/ppermute | solution.py:662
  4.0 18.0 %copy-start.21 = (f32[1,1,2,256,256]{4,3,2,1,0:T(8,128)S(1)}, f32[1,1,2,256,256]{4,3,2,1,0:T(8,128)}, u32[]{:S(2)}) copy-start(f32[1,1,2,256,256]{4,3,2,1,0:T(8,128)} %param.11) | copy-start | bytes 1572868
  4.0 18.0 %copy-start.25 = (f32[1,1,2,128,256]{4,3,2,1,0:T(8,128)S(1)}, f32[1,1,2,128,256]{4,3,2,1,0:T(8,128)}, u32[]{:S(2)}) copy-start(f32[1,1,2,128,256]{4,3,2,1,0:T(8,128)} %param.14) | copy-start | bytes 786436
  7.5 1.7 collective-permute-start.2
  7.6 1.3 collective-permute-start
  8.1 1.1 collective-permute-start.1
  11.9 23.6 %all-to-all-start = ((f32[32,24,128]{2,1,0:T(8,128)}), f32[32,24,128]{2,1,0:T(8,128)S(1)}, u32[]{:S(2)}, u32[]{:S(2)}) async-start(f32[32,24,128]{2,1,0:T(8,128)} %get-tuple-element.54.after_ref), calls=%async_computation | async-start | bytes 786432 | tf_op jit(solution)/shard_map/all_to_all | solution.py:666
  37.8 8.6 %collective-permute-start.6 = (f32[2,768,256]{2,1,0:T(8,128)}, f32[2,768,256]{2,1,0:T(8,128)}, u32[]{:S(2)}, u32[]{:S(2)}) collective-permute-start(f32[2,768,256]{2,1,0:T(8,128)} %get-tuple-element.59.own_forward_hbm), channel_id=1, source_target_pairs={{0,32},{32,0},{64,96},{96,64},{128,160},{160,128},{192,224},{224,1... | collective-permute-start | bytes 4718600 | tf_op jit(solution)/shard_map/ppermute | solution.py:662
  39.8 6.6 %collective-permute-start.5 = (f32[2,256,512]{2,1,0:T(8,128)S(1)}, f32[2,256,512]{2,1,0:T(8,128)S(1)}, u32[]{:S(2)}, u32[]{:S(2)}) collective-permute-start(f32[2,256,512]{2,1,0:T(8,128)S(1)} %get-tuple-element.58.own_back_hbm), channel_id=1, source_target_pairs={{0,32},{32,0},{64,96},{96,64},{128,160},{160,128},{192,224},{224,1... | collective-permute-start | bytes 3145736 | tf_op jit(solution)/shard_map/ppermute | solution.py:662
  39.8 16.4 %all-to-all-start.1 = ((f32[64,8,128]{2,1,0:T(8,128)}), f32[64,8,128]{2,1,0:T(8,128)}, u32[]{:S(2)}, u32[]{:S(2)}) async-start(f32[64,8,128]{2,1,0:T(8,128)} %copy-done.11), calls=%async_computation.1 | async-start | bytes 524288 | tf_op jit(solution)/shard_map/all_to_all | solution.py:666
  44.4 2.0 collective-permute-start.3
  56.2 39.1 %copy-start.3 = (bf16[2,2,512,512]{3,2,1,0:T(8,128)(2,1)S(1)}, bf16[2,2,512,512]{3,2,1,0:T(8,128)(2,1)}, u32[]{:S(2)}) copy-start(bf16[2,2,512,512]{3,2,1,0:T(8,128)(2,1)} %get-tuple-element.60.refs_6_.backs_ref.refs_3_) | copy-start | bytes 6291460
  60.4 34.9 %copy-start.12 = (f32[256,128]{1,0:T(8,128)S(1)}, f32[256,128]{1,0:T(8,128)}, u32[]{:S(2)}) copy-start(f32[256,128]{1,0:T(8,128)} %get-tuple-element.67.base_ref) | copy-start | bytes 393220
  60.4 34.9 %copy-start.15 = (s32[16]{0:T(128)S(1)}, s32[16]{0:T(128)}, u32[]{:S(2)}) copy-start(s32[16]{0:T(128)} %copy-done.14) | copy-start | bytes 196
  60.4 34.9 %copy-start.17 = (s32[16]{0:T(128)S(1)}, s32[16]{0:T(128)}, u32[]{:S(2)}) copy-start(s32[16]{0:T(128)} %copy-done.16) | copy-start | bytes 196
  78.8 21.7 %copy-start = (bf16[2,2,1536,256]{3,2,1,0:T(8,128)(2,1)S(1)}, bf16[2,2,1536,256]{3,2,1,0:T(8,128)(2,1)}, u32[]{:S(2)}) copy-start(bf16[2,2,1536,256]{3,2,1,0:T(8,128)(2,1)} %get-tuple-element.64.refs_5_.forwards_ref) | copy-start | bytes 9437188
  80.1 20.4 %copy-start.5 = (f32[2,2,256,128]{3,2,1,0:T(8,128)S(1)}, f32[2,2,256,128]{3,2,1,0:T(8,128)}, u32[]{:S(2)}) copy-start(f32[2,2,256,128]{3,2,1,0:T(8,128)} %copy-done.4) | copy-start | bytes 1572868
  80.1 20.4 %copy-start.7 = (f32[2,2,16,8,128]{4,3,2,1,0:T(8,128)S(1)}, f32[2,2,16,8,128]{4,3,2,1,0:T(8,128)}, u32[]{:S(2)}) copy-start(f32[2,2,16,8,128]{4,3,2,1,0:T(8,128)} %copy-done.6) | copy-start | bytes 786436
  96.5 4.0 %collective-permute-start.7 = (f32[4,8,128]{2,1,0:T(8,128)S(1)}, f32[4,8,128]{2,1,0:T(8,128)S(1)}, u32[]{:S(2)}, u32[]{:S(2)}) collective-permute-start(f32[4,8,128]{2,1,0:T(8,128)S(1)} %get-tuple-element.68), channel_id=1, source_target_pairs={{0,64},{32,96},{192,128},{224,160},{1,65},{33,97},{193,129},{225,1... | collective-permute-start | bytes 49160 | tf_op jit(solution)/shard_map/ppermute | solution.py:672
  164.9 0.7 collective-permute-start.8
  211.6 25.3 %copy-start.2 = (bf16[2,2,1536,256]{3,2,1,0:T(8,128)(2,1)S(1)}, bf16[2,2,1536,256]{3,2,1,0:T(8,128)(2,1)}, u32[]{:S(2)}) copy-start(bf16[2,2,1536,256]{3,2,1,0:T(8,128)(2,1)} %get-tuple-element.64.refs_5_.forwards_ref) | copy-start | bytes 9437188
  227.9 9.0 %collective-permute-start.9 = (f32[4,8,128]{2,1,0:T(8,128)S(1)}, f32[4,8,128]{2,1,0:T(8,128)S(1)}, u32[]{:S(2)}, u32[]{:S(2)}) collective-permute-start(f32[4,8,128]{2,1,0:T(8,128)S(1)} %get-tuple-element.78), channel_id=1, source_target_pairs={{128,192},{160,224},{64,0},{96,32},{129,193},{161,225},{65,1},{97,... | collective-permute-start | bytes 49160 | tf_op jit(solution)/shard_map/ppermute | solution.py:672
  270.6 31.8 %copy-start.13 = (f32[256,128]{1,0:T(8,128)S(1)}, f32[256,128]{1,0:T(8,128)}, u32[]{:S(2)}) copy-start(f32[256,128]{1,0:T(8,128)} %get-tuple-element.83.refs_6_) | copy-start | bytes 393220
  304.3 21.4 %collective-permute-start.10 = (f32[2,2,16,256]{3,2,1,0:T(8,128)S(1)}, f32[2,2,16,256]{3,2,1,0:T(8,128)S(1)}, u32[]{:S(2)}, u32[]{:S(2)}) collective-permute-start(f32[2,2,16,256]{3,2,1,0:T(8,128)S(1)} %get-tuple-element.91), channel_id=1, source_target_pairs={{0,32},{32,0},{64,96},{96,64},{128,160},{160,128},{192,224},{224,1... | collective-permute-start | bytes 196616 | tf_op jit(solution)/shard_map/ppermute | solution.py:662
  (16 other events, 71.7 us)

commit v8 on v7

--- a/solution.py
+++ b/solution.py
@@ -24,7 +24,6 @@
 bf16 = jnp.bfloat16
 VMEM_LIMIT = 48 * 1024 * 1024
 ALMOST_ALL_VMEM = 60 * 1024 * 1024
-FIRST_MIDDLE_VMEM = 58 * 1024 * 1024
 smem = pl.BlockSpec(memory_space=pltpu.SMEM)
 vmem = pl.BlockSpec(memory_space=pltpu.VMEM)
 hbm = pl.BlockSpec(memory_space=pl.ANY)
@@ -420,17 +419,16 @@
     )
 
 
-def leaf_finish(choice, own_slots_ref, other_slots_ref, returned_ref, back, base):
+def leaf_finish(choice, own_slots_ref, other_slots_ref, returned_ref, backs_ref, base):
     blocks = []
     for block in range(NB):
         slot = jnp.where(choice == 0, own_slots_ref[block], other_slots_ref[block])
         blocks.append(returned_ref[slot])
     mine, mine_turned = unpack_both(jnp.stack(blocks, axis=0))
-    real, imag = back()
     return (
         base
-        + stacked_product(real, mine)
-        + stacked_product(imag, mine_turned)
+        + stacked_product(backs_ref[choice, 0], mine)
+        + stacked_product(backs_ref[choice, 1], mine_turned)
     )
 
 
@@ -473,25 +471,13 @@
     next_base_ref,
     forward_ref,
     semaphore,
-    *back_scratch,
 ):
     sweep, first = stage_place(place_ref, stage)
     copy = pltpu.make_async_copy(forwards_hbm.at[1 - first, sweep], forward_ref, semaphore)
-    if back_scratch:
-        back_ref, back_semaphore = back_scratch
-        back_copy = pltpu.make_async_copy(backs_ref.at[first], back_ref, back_semaphore)
-        back_copy.start()
     copy.start()
-
-    def back():
-        if not back_scratch:
-            return backs_ref[first, 0], backs_ref[first, 1]
-        back_copy.wait()
-        return back_ref[0], back_ref[1]
-
     base = base_refs[0][...] if base_refs else y_ref[first, sweep]
     field_ref[...] = leaf_finish(
-        first, own_slots_ref, other_slots_ref, returned_ref, back, base
+        first, own_slots_ref, other_slots_ref, returned_ref, backs_ref, base
     )
     trace = trace_rows(sweep, field_ref)
     copy.wait()
@@ -523,12 +509,7 @@
 ):
     sweep, first = stage_place(place_ref, stage)
     field_ref[...] = leaf_finish(
-        1 - first,
-        own_slots_ref,
-        other_slots_ref,
-        returned_ref,
-        lambda: (backs_ref[1 - first, 0], backs_ref[1 - first, 1]),
-        base_ref[...],
+        1 - first, own_slots_ref, other_slots_ref, returned_ref, backs_ref, base_ref[...]
     )
     trace_ref[...] = pack(trace_rows(sweep, field_ref))
 
@@ -599,12 +580,7 @@
                     ).start()
 
     field = leaf_finish(
-        1 - first,
-        own_slots_ref,
-        other_slots_ref,
-        returned_ref,
-        lambda: (backs_ref[1 - first, 0], backs_ref[1 - first, 1]),
-        base_ref[...],
+        1 - first, own_slots_ref, other_slots_ref, returned_ref, backs_ref, base_ref[...]
     )
     for sweep in range(2):
 
@@ -817,23 +793,13 @@
         field, send, base = call(
             middle,
             (field_shape, slot_shape, field_shape),
-            [smem] * 3
-            + [vmem] * 2
-            + [hbm]
-            + ([vmem] if bases else [hbm])
-            + [vmem] * (1 + len(bases)),
+            [smem] * 3 + [vmem] * 2 + [hbm] + [vmem] * (2 + len(bases)),
             (vmem,) * 3,
             [
                 pltpu.VMEM((2 * (NB * RB + P_SIZE), 2 * TR), bf16),
                 pltpu.SemaphoreType.DMA,
-            ]
-            + (
-                []
-                if bases
-                else [pltpu.VMEM((2, 2 * P_SIZE, NB * RB), bf16), pltpu.SemaphoreType.DMA]
-            ),
+            ],
             cost_of(300_000_000, 3_000_000),
-            VMEM_LIMIT if bases else FIRST_MIDDLE_VMEM,
         )(place, own_slots, other_slots, u, y, forwards, backs, returned, *bases)
         fields.append(field)
         returned = exchange(separator(stage, 1, exchange(send)))

time: 328 us -> 325 us (level)
    unnamed x54 -> x36, local copies, waits for them, and re-layouts: 9.18 us -> 8.63 us
where the time goes in v8:
time: 325 us; the launch traced here: 324 us
  blocking collectives  203 us (62%)
  starting transfers between devices  45.7 us (14%)
  Pallas kernels  44.8 us (14%)
  waiting for transfers between devices  20.1 us (6%)
  local copies, waits for them, and re-layouts  8.63 us (3%)
    all_to_all x14, blocking collectives, exchange(): lax.all_to_all(value, 'front', split_axis=0, concat_axis=0, tiled=True)  203 us
    ppermute x8, starting transfers between devices, across_cores(): lax.ppermute(value, 'layer', [(index, index ^ 1) for index in range(layer...  27.3 us
    all_to_all x2, starting transfers between devices, exchange(): lax.all_to_all(value, 'front', split_axis=0, concat_axis=0, tiled=True)  13.2 us
    pallas_call x4, Pallas kernels, body(): call(middle, (field_shape, slot_shape, field_shape), [smem] * 3 + [vmem]...  9.9 us
    pallas_call x7, Pallas kernels, separator(): call(functools.partial(separator_kernel, stage, step), slot_shape, [smem]...  9.24 us
    unnamed x36, local copies, waits for them, and re-layouts  8.63 us
    ppermute x3, waiting for transfers between devices, to_next_stage(): return lax.ppermute(value, 'layer', pairs)  8.53 us
    all_to_all x2, waiting for transfers between devices, exchange(): lax.all_to_all(value, 'front', split_axis=0, concat_axis=0, tiled=True)  8.51 us
  transfers between devices with their start and end apart: 13, of which 8 were waited for; matrix products, arithmetic and copies ran while one was open for 0% of the time, Pallas kernels for 4%

profile of v8, /device:TPU:1, one launch (start us, length us, event | category | flops | bytes accessed | tf_op | source)
XLA Modules:
  0.0 323.6 jit_solution(833231381600016361)
XLA Ops:
  0.7 3.3 %collective-permute-start.4 = (f32[2,256,256]{2,1,0:T(8,128)}, f32[2,256,256]{2,1,0:T(8,128)S(1)}, u32[]{:S(2)}, u32[]{:S(2)}) collective-permute-start(f32[2,256,256]{2,1,0:T(8,128)} %bitcast.20), channel_id=1, source_target_pairs={{0,32},{32,0},{64,96},{96,64},{128,160},{160,128},{192,224},{224,1... | collective-permute-start | bytes 1572872 | tf_op jit(solution)/shard_map/ppermute | solution.py:638
  4.0 3.5 %shard_map.104 = (f32[2,16,8,128]{3,2,1,0:T(8,128)}, f32[2,16,8,128]{3,2,1,0:T(8,128)}, f32[2,256,128]{2,1,0:T(8,128)}, f32[2,256,128]{2,1,0:T(8,128)}) custom-call(s32[1]{0:T(128)} %bitcast.place_ref.refs_0_, f32[2,32,256]{2,1,0:T(8,128)} %bitcast.24, f32[2,32,256]{2,1,0:T(8,128)} %bitcast.25, f32[2,256,256]{2,1,0:T(8,128)} %bitcast.18, f32[2,512,256]{2,1,0:T(8,128)} %bitcast.16), custom_call_target="tpu_custom_call" | custom-call | flops 600000000 | bytes 2500000 | tf_op jit(solution)/shard_map/pallas_call | solution.py:679
  11.9 9.3 %all-to-all-start = ((f32[32,24,128]{2,1,0:T(8,128)}), f32[32,24,128]{2,1,0:T(8,128)S(1)}, u32[]{:S(2)}, u32[]{:S(2)}) async-start(f32[32,24,128]{2,1,0:T(8,128)} %get-tuple-element.54.after_ref), calls=%async_computation | async-start | bytes 786432 | tf_op jit(solution)/shard_map/all_to_all | solution.py:642
  26.3 4.5 %shard_map.106 = (f32[2,768,256]{2,1,0:T(8,128)}, f32[2,256,512]{2,1,0:T(8,128)S(1)}, bf16[2,2,512,256]{3,2,1,0:T(8,128)(2,1)S(1)}) custom-call(f32[32,24,128]{2,1,0:T(8,128)} %get-tuple-element.54.after_ref, f32[2,256,256]{2,1,0:T(8,128)S(1)} %bitcast.19, f32[2,512,256]{2,1,0:T(8,128)S(1)} %bitcast.17, f32[2,128,256]{2,1,0:T(8,128)S(1)} %bitcast.22, ...), custom_call_target="tpu_custom_call" | custom-call | flops 4000000000 | bytes 5000000 | tf_op jit(solution)/shard_map/pallas_call | solution.py:707
  30.8 4.7 %all-to-all-done.arrived_ref = f32[32,24,128]{2,1,0:T(8,128)S(1)} async-done(((f32[32,24,128]{2,1,0:T(8,128)}), f32[32,24,128]{2,1,0:T(8,128)S(1)}, u32[]{:S(2)}, u32[]{:S(2)}) %all-to-all-start) | async-done | bytes 393248 | tf_op jit(solution)/shard_map/all_to_all | solution.py:642
  39.8 3.9 %all-to-all-start.1 = ((f32[64,8,128]{2,1,0:T(8,128)}), f32[64,8,128]{2,1,0:T(8,128)S(1)}, u32[]{:S(2)}, u32[]{:S(2)}) async-start(f32[64,8,128]{2,1,0:T(8,128)} %get-tuple-element.65), calls=%async_computation.1 | async-start | bytes 524288 | tf_op jit(solution)/shard_map/all_to_all | solution.py:642
  46.7 4.8 %shard_map.108 = (f32[2,2,16,8,128]{4,3,2,1,0:T(8,128)S(1)}, f32[2,2,256,128]{3,2,1,0:T(8,128)S(1)}, bf16[2,2,512,512]{3,2,1,0:T(8,128)(2,1)}, bf16[2,2,1536,256]{3,2,1,0:T(8,128)(2,1)}) custom-call(f32[2,16,8,128]{3,2,1,0:T(8,128)S(1)} %copy-done.6, f32[2,16,8,128]{3,2,1,0:T(8,128)S(1)} %collective-permute-done.2.other_u_ref.other_u_hbm, ...), custom_call_target="tpu_custom_call" | custom-call | flops 10000000 | bytes 12000000 | tf_op jit(solution)/shard_map/pallas_call | solution.py:745
  51.5 3.8 %all-to-all-done.1.refs_7_ = f32[64,8,128]{2,1,0:T(8,128)S(1)} async-done(((f32[64,8,128]{2,1,0:T(8,128)}), f32[64,8,128]{2,1,0:T(8,128)S(1)}, u32[]{:S(2)}, u32[]{:S(2)}) %all-to-all-start.1) | async-done | bytes 262176 | tf_op jit(solution)/shard_map/all_to_all | solution.py:642
  59.5 17.0 %all_to_all.80.arrived_ref = f32[64,8,128]{2,1,0:T(8,128)S(1)} all-to-all(f32[64,8,128]{2,1,0:T(8,128)S(1)} %get-tuple-element.66), channel_id=1, replica_groups=mesh['layer'=8,'front'=32] {'front'}, dimensions={0} | all-to-all | bytes 524288 | tf_op jit(solution)/shard_map/all_to_all | solution.py:642
  77.9 14.9 %all_to_all.81.returned_ref = f32[64,8,128]{2,1,0:T(8,128)S(1)} all-to-all(f32[64,8,128]{2,1,0:T(8,128)S(1)} %shard_map.110), channel_id=1, replica_groups=mesh['layer'=8,'front'=32] {'front'}, dimensions={0} | all-to-all | bytes 524288 | tf_op jit(solution)/shard_map/all_to_all | solution.py:642
  99.2 15.3 %all_to_all.82.arrived_ref = f32[64,8,128]{2,1,0:T(8,128)S(1)} all-to-all(f32[64,8,128]{2,1,0:T(8,128)S(1)} %get-tuple-element.69), channel_id=1, replica_groups=mesh['layer'=8,'front'=32] {'front'}, dimensions={0} | all-to-all | bytes 524288 | tf_op jit(solution)/shard_map/all_to_all | solution.py:642
  115.8 14.0 %all_to_all.83.refs_7_ = f32[64,8,128]{2,1,0:T(8,128)S(1)} all-to-all(f32[64,8,128]{2,1,0:T(8,128)S(1)} %shard_map.113), channel_id=1, replica_groups=mesh['layer'=8,'front'=32] {'front'}, dimensions={0} | all-to-all | bytes 524288 | tf_op jit(solution)/shard_map/all_to_all | solution.py:642
  132.3 13.9 %all_to_all.84.arrived_ref = f32[64,8,128]{2,1,0:T(8,128)S(1)} all-to-all(f32[64,8,128]{2,1,0:T(8,128)S(1)} %get-tuple-element.71), channel_id=1, replica_groups=mesh['layer'=8,'front'=32] {'front'}, dimensions={0} | all-to-all | bytes 524288 | tf_op jit(solution)/shard_map/all_to_all | solution.py:642
  147.4 13.9 %all_to_all.85.returned_ref = f32[64,8,128]{2,1,0:T(8,128)S(1)} all-to-all(f32[64,8,128]{2,1,0:T(8,128)S(1)} %shard_map.115), channel_id=1, replica_groups=mesh['layer'=8,'front'=32] {'front'}, dimensions={0} | all-to-all | bytes 524288 | tf_op jit(solution)/shard_map/all_to_all | solution.py:642
  164.2 13.8 %all_to_all.86.arrived_ref = f32[64,8,128]{2,1,0:T(8,128)S(1)} all-to-all(f32[64,8,128]{2,1,0:T(8,128)S(1)} %get-tuple-element.74), channel_id=1, replica_groups=mesh['layer'=8,'front'=32] {'front'}, dimensions={0} | all-to-all | bytes 524288 | tf_op jit(solution)/shard_map/all_to_all | solution.py:642
  179.3 13.8 %all_to_all.87.refs_7_ = f32[64,8,128]{2,1,0:T(8,128)S(1)} all-to-all(f32[64,8,128]{2,1,0:T(8,128)S(1)} %shard_map.118), channel_id=1, replica_groups=mesh['layer'=8,'front'=32] {'front'}, dimensions={0} | all-to-all | bytes 524288 | tf_op jit(solution)/shard_map/all_to_all | solution.py:642
  195.5 13.8 %all_to_all.88.arrived_ref = f32[64,8,128]{2,1,0:T(8,128)S(1)} all-to-all(f32[64,8,128]{2,1,0:T(8,128)S(1)} %get-tuple-element.76), channel_id=1, replica_groups=mesh['layer'=8,'front'=32] {'front'}, dimensions={0} | all-to-all | bytes 524288 | tf_op jit(solution)/shard_map/all_to_all | solution.py:642
  210.6 13.8 %all_to_all.89.returned_ref = f32[64,8,128]{2,1,0:T(8,128)S(1)} all-to-all(f32[64,8,128]{2,1,0:T(8,128)S(1)} %shard_map.120), channel_id=1, replica_groups=mesh['layer'=8,'front'=32] {'front'}, dimensions={0} | all-to-all | bytes 524288 | tf_op jit(solution)/shard_map/all_to_all | solution.py:642
  226.8 7.7 %collective-permute-done.9.trace_ref = f32[4,8,128]{2,1,0:T(8,128)S(1)} collective-permute-done((f32[4,8,128]{2,1,0:T(8,128)S(1)}, f32[4,8,128]{2,1,0:T(8,128)S(1)}, u32[]{:S(2)}, u32[]{:S(2)}) %collective-permute-start.9) | collective-permute-done | bytes 16416 | tf_op jit(solution)/shard_map/ppermute | solution.py:648
  235.5 13.5 %all_to_all.90.arrived_ref = f32[64,8,128]{2,1,0:T(8,128)S(1)} all-to-all(f32[64,8,128]{2,1,0:T(8,128)S(1)} %get-tuple-element.79), channel_id=1, replica_groups=mesh['layer'=8,'front'=32] {'front'}, dimensions={0} | all-to-all | bytes 524288 | tf_op jit(solution)/shard_map/all_to_all | solution.py:642
  250.3 15.5 %all_to_all.91.refs_7_ = f32[64,8,128]{2,1,0:T(8,128)S(1)} all-to-all(f32[64,8,128]{2,1,0:T(8,128)S(1)} %shard_map.123), channel_id=1, replica_groups=mesh['layer'=8,'front'=32] {'front'}, dimensions={0} | all-to-all | bytes 524288 | tf_op jit(solution)/shard_map/all_to_all | solution.py:642
  268.3 15.7 %all_to_all.92.arrived_ref = f32[64,8,128]{2,1,0:T(8,128)S(1)} all-to-all(f32[64,8,128]{2,1,0:T(8,128)S(1)} %get-tuple-element.81), channel_id=1, replica_groups=mesh['layer'=8,'front'=32] {'front'}, dimensions={0} | all-to-all | bytes 524288 | tf_op jit(solution)/shard_map/all_to_all | solution.py:642
  285.3 14.7 %all_to_all.93.refs_4_ = f32[64,8,128]{2,1,0:T(8,128)S(1)} all-to-all(f32[64,8,128]{2,1,0:T(8,128)S(1)} %shard_map.125), channel_id=1, replica_groups=mesh['layer'=8,'front'=32] {'front'}, dimensions={0} | all-to-all | bytes 524288 | tf_op jit(solution)/shard_map/all_to_all | solution.py:642
  301.8 20.2 %collective-permute-start.10 = (f32[2,2,16,256]{3,2,1,0:T(8,128)S(1)}, f32[2,2,16,256]{3,2,1,0:T(8,128)S(1)}, u32[]{:S(2)}, u32[]{:S(2)}) collective-permute-start(f32[2,2,16,256]{3,2,1,0:T(8,128)S(1)} %get-tuple-element.91), channel_id=1, source_target_pairs={{0,32},{32,0},{64,96},{96,64},{128,160},{160,128},{192,224},{224,1... | collective-permute-start | bytes 196616 | tf_op jit(solution)/shard_map/ppermute | solution.py:638
  (76 shorter events, 53.6 us)
Async XLA Ops:
  0.6 6.9 %copy-start.8 = (s32[1,1,16,1]{2,3,1,0:T(1,128)S(1)}, s32[1,1,16,1]{2,3,1,0:T(1,128)}, u32[]{:S(2)}) copy-start(s32[1,1,16,1]{2,3,1,0:T(1,128)} %param.16) | copy-start | bytes 196
  0.6 7.4 %copy-start.9 = (s32[1,1,16]{2,1,0:T(1,128)S(1)}, s32[1,1,16]{2,1,0:T(1,128)}, u32[]{:S(2)}) copy-start(s32[1,1,16]{2,1,0:T(1,128)} %param.17) | copy-start | bytes 196
  0.7 20.5 %collective-permute-start.4 = (f32[2,256,256]{2,1,0:T(8,128)}, f32[2,256,256]{2,1,0:T(8,128)S(1)}, u32[]{:S(2)}, u32[]{:S(2)}) collective-permute-start(f32[2,256,256]{2,1,0:T(8,128)} %bitcast.20), channel_id=1, source_target_pairs={{0,32},{32,0},{64,96},{96,64},{128,160},{160,128},{192,224},{224,1... | collective-permute-start | bytes 1572872 | tf_op jit(solution)/shard_map/ppermute | solution.py:638
  4.0 18.0 %copy-start.15 = (f32[1,1,2,128,256]{4,3,2,1,0:T(8,128)S(1)}, f32[1,1,2,128,256]{4,3,2,1,0:T(8,128)}, u32[]{:S(2)}) copy-start(f32[1,1,2,128,256]{4,3,2,1,0:T(8,128)} %param.14) | copy-start | bytes 786436
  4.0 18.0 %copy-start.16 = (f32[1,1,2,128,256]{4,3,2,1,0:T(8,128)S(1)}, f32[1,1,2,128,256]{4,3,2,1,0:T(8,128)}, u32[]{:S(2)}) copy-start(f32[1,1,2,128,256]{4,3,2,1,0:T(8,128)} %param.15) | copy-start | bytes 786436
  7.4 1.7 collective-permute-start.2
  7.6 1.3 collective-permute-start
  8.0 1.1 collective-permute-start.1
  11.9 23.6 %all-to-all-start = ((f32[32,24,128]{2,1,0:T(8,128)}), f32[32,24,128]{2,1,0:T(8,128)S(1)}, u32[]{:S(2)}, u32[]{:S(2)}) async-start(f32[32,24,128]{2,1,0:T(8,128)} %get-tuple-element.54.after_ref), calls=%async_computation | async-start | bytes 786432 | tf_op jit(solution)/shard_map/all_to_all | solution.py:642
  35.5 8.3 %copy-start.17 = (f32[2,256,128]{2,1,0:T(8,128)S(1)}, f32[2,256,128]{2,1,0:T(8,128)}, u32[]{:S(2)}) copy-start(f32[2,256,128]{2,1,0:T(8,128)} %get-tuple-element.53) | copy-start | bytes 786436
  35.5 10.2 %copy-start.6 = (f32[2,16,8,128]{3,2,1,0:T(8,128)S(1)}, f32[2,16,8,128]{3,2,1,0:T(8,128)}, u32[]{:S(2)}) copy-start(f32[2,16,8,128]{3,2,1,0:T(8,128)} %get-tuple-element.48.own_u_ref.own_u_hbm) | copy-start | bytes 393220
  37.6 8.1 %collective-permute-start.6 = (f32[2,768,256]{2,1,0:T(8,128)}, f32[2,768,256]{2,1,0:T(8,128)}, u32[]{:S(2)}, u32[]{:S(2)}) collective-permute-start(f32[2,768,256]{2,1,0:T(8,128)} %get-tuple-element.59.own_forward_hbm), channel_id=1, source_target_pairs={{0,32},{32,0},{64,96},{96,64},{128,160},{160,128},{192,224},{224,1... | collective-permute-start | bytes 4718600 | tf_op jit(solution)/shard_map/ppermute | solution.py:638
  39.7 6.0 %collective-permute-start.5 = (f32[2,256,512]{2,1,0:T(8,128)S(1)}, f32[2,256,512]{2,1,0:T(8,128)}, u32[]{:S(2)}, u32[]{:S(2)}) collective-permute-start(f32[2,256,512]{2,1,0:T(8,128)S(1)} %get-tuple-element.58.own_back_hbm), channel_id=1, source_target_pairs={{0,32},{32,0},{64,96},{96,64},{128,160},{160,128},{192,224},{224,1... | collective-permute-start | bytes 3145736 | tf_op jit(solution)/shard_map/ppermute | solution.py:638
  39.8 15.5 %all-to-all-start.1 = ((f32[64,8,128]{2,1,0:T(8,128)}), f32[64,8,128]{2,1,0:T(8,128)S(1)}, u32[]{:S(2)}, u32[]{:S(2)}) async-start(f32[64,8,128]{2,1,0:T(8,128)} %get-tuple-element.65), calls=%async_computation.1 | async-start | bytes 524288 | tf_op jit(solution)/shard_map/all_to_all | solution.py:642
  43.8 1.9 collective-permute-start.3
  55.3 1.6 copy-start.3
  56.9 35.9 %copy-start.4 = (bf16[2,2,512,512]{3,2,1,0:T(8,128)(2,1)S(1)}, bf16[2,2,512,512]{3,2,1,0:T(8,128)(2,1)}, u32[]{:S(2)}) copy-start(bf16[2,2,512,512]{3,2,1,0:T(8,128)(2,1)} %get-tuple-element.60.refs_6_.backs_ref.refs_3_) | copy-start | bytes 6291460
  76.5 21.6 %copy-start = (bf16[2,2,1536,256]{3,2,1,0:T(8,128)(2,1)S(1)}, bf16[2,2,1536,256]{3,2,1,0:T(8,128)(2,1)}, u32[]{:S(2)}) copy-start(bf16[2,2,1536,256]{3,2,1,0:T(8,128)(2,1)} %get-tuple-element.64.refs_5_.forwards_ref) | copy-start | bytes 9437188
  94.0 4.1 %collective-permute-start.7 = (f32[4,8,128]{2,1,0:T(8,128)S(1)}, f32[4,8,128]{2,1,0:T(8,128)S(1)}, u32[]{:S(2)}, u32[]{:S(2)}) collective-permute-start(f32[4,8,128]{2,1,0:T(8,128)S(1)} %get-tuple-element.68), channel_id=1, source_target_pairs={{0,64},{32,96},{192,128},{224,160},{1,65},{33,97},{193,129},{225,1... | collective-permute-start | bytes 49160 | tf_op jit(solution)/shard_map/ppermute | solution.py:648
  146.1 17.0 %copy-start.1 = (bf16[2,2,1536,256]{3,2,1,0:T(8,128)(2,1)S(1)}, bf16[2,2,1536,256]{3,2,1,0:T(8,128)(2,1)}, u32[]{:S(2)}) copy-start(bf16[2,2,1536,256]{3,2,1,0:T(8,128)(2,1)} %get-tuple-element.64.refs_5_.forwards_ref) | copy-start | bytes 9437188
  162.5 0.7 collective-permute-start.8
  209.3 25.2 %copy-start.2 = (bf16[2,2,1536,256]{3,2,1,0:T(8,128)(2,1)S(1)}, bf16[2,2,1536,256]{3,2,1,0:T(8,128)(2,1)}, u32[]{:S(2)}) copy-start(bf16[2,2,1536,256]{3,2,1,0:T(8,128)(2,1)} %get-tuple-element.64.refs_5_.forwards_ref) | copy-start | bytes 9437188
  225.5 9.0 %collective-permute-start.9 = (f32[4,8,128]{2,1,0:T(8,128)S(1)}, f32[4,8,128]{2,1,0:T(8,128)S(1)}, u32[]{:S(2)}, u32[]{:S(2)}) collective-permute-start(f32[4,8,128]{2,1,0:T(8,128)S(1)} %get-tuple-element.78), channel_id=1, source_target_pairs={{128,192},{160,224},{64,0},{96,32},{129,193},{161,225},{65,1},{97,... | collective-permute-start | bytes 49160 | tf_op jit(solution)/shard_map/ppermute | solution.py:648
  301.8 21.1 %collective-permute-start.10 = (f32[2,2,16,256]{3,2,1,0:T(8,128)S(1)}, f32[2,2,16,256]{3,2,1,0:T(8,128)S(1)}, u32[]{:S(2)}, u32[]{:S(2)}) collective-permute-start(f32[2,2,16,256]{3,2,1,0:T(8,128)S(1)} %get-tuple-element.91), channel_id=1, source_target_pairs={{0,32},{32,0},{64,96},{96,64},{128,160},{160,128},{192,224},{224,1... | collective-permute-start | bytes 196616 | tf_op jit(solution)/shard_map/ppermute | solution.py:638
  (7 other events, 7.0 us)

commit v9 on v8

--- a/solution.py
+++ b/solution.py
@@ -22,7 +22,7 @@
 
 f32 = jnp.float32
 bf16 = jnp.bfloat16
-VMEM_LIMIT = 48 * 1024 * 1024
+VMEM_LIMIT = 40 * 1024 * 1024
 ALMOST_ALL_VMEM = 60 * 1024 * 1024
 smem = pl.BlockSpec(memory_space=pltpu.SMEM)
 vmem = pl.BlockSpec(memory_space=pltpu.VMEM)

time: 325 us -> 328 us (level)
  local copies, waits for them, and re-layouts: 8.63 us -> 18.4 us
  Pallas kernels: 44.8 us -> 39.2 us
  waiting for transfers between devices: 20.1 us -> 15.9 us
  blocking collectives: 203 us -> 207 us
    unnamed x36 -> x52, local copies, waits for them, and re-layouts: 8.63 us -> 18.4 us
    all_to_all x2, waiting for transfers between devices: 8.51 us -> 4.27 us  [exchange(): lax.all_to_all(value, 'front', split_axis=0, concat_axis=0, tiled=True)]
    all_to_all x14, blocking collectives: 203 us -> 207 us  [exchange(): lax.all_to_all(value, 'front', split_axis=0, concat_axis=0, tiled=True)]
where the time goes in v9:
time: 328 us; the launch traced here: 327 us
  blocking collectives  207 us (63%)
  starting transfers between devices  45.9 us (14%)
  Pallas kernels  39.2 us (12%)
  local copies, waits for them, and re-layouts  18.4 us (6%)
  waiting for transfers between devices  15.9 us (5%)
    all_to_all x14, blocking collectives, exchange(): lax.all_to_all(value, 'front', split_axis=0, concat_axis=0, tiled=True)  207 us
    ppermute x8, starting transfers between devices, across_cores(): lax.ppermute(value, 'layer', [(index, index ^ 1) for index in range(layer...  26.8 us
    unnamed x52, local copies, waits for them, and re-layouts  18.4 us
    all_to_all x2, starting transfers between devices, exchange(): lax.all_to_all(value, 'front', split_axis=0, concat_axis=0, tiled=True)  13.9 us
    pallas_call x7, Pallas kernels, separator(): call(functools.partial(separator_kernel, stage, step), slot_shape, [smem]...  9.25 us
    ppermute x3, waiting for transfers between devices, to_next_stage(): return lax.ppermute(value, 'layer', pairs)  8.56 us
    pallas_call x4, Pallas kernels, body(): call(middle, (field_shape, slot_shape, field_shape), [smem] * 3 + [vmem]...  7.21 us
  transfers between devices with their start and end apart: 13, of which 8 were waited for; matrix products, arithmetic and copies ran while one was open for 0% of the time, Pallas kernels for 4%

profile of v9, /device:TPU:1, one launch (start us, length us, event | category | flops | bytes accessed | tf_op | source)
XLA Modules:
  0.0 327.0 jit_solution(2428571669973097489)
XLA Ops:
  0.7 3.3 %collective-permute-start.4 = (f32[2,256,256]{2,1,0:T(8,128)}, f32[2,256,256]{2,1,0:T(8,128)S(1)}, u32[]{:S(2)}, u32[]{:S(2)}) collective-permute-start(f32[2,256,256]{2,1,0:T(8,128)} %bitcast.20), channel_id=1, source_target_pairs={{0,32},{32,0},{64,96},{96,64},{128,160},{160,128},{192,224},{224,1... | collective-permute-start | bytes 1572872 | tf_op jit(solution)/shard_map/ppermute | solution.py:638
  4.0 3.4 %shard_map.104 = (f32[2,16,8,128]{3,2,1,0:T(8,128)}, f32[2,16,8,128]{3,2,1,0:T(8,128)}, f32[2,256,128]{2,1,0:T(8,128)}, f32[2,256,128]{2,1,0:T(8,128)}) custom-call(s32[1]{0:T(128)} %bitcast.place_ref.refs_0_, f32[2,32,256]{2,1,0:T(8,128)} %bitcast.24, f32[2,32,256]{2,1,0:T(8,128)} %bitcast.25, f32[2,256,256]{2,1,0:T(8,128)} %bitcast.18, f32[2,512,256]{2,1,0:T(8,128)} %bitcast.16), custom_call_target="tpu_custom_call" | custom-call | flops 600000000 | bytes 2500000 | tf_op jit(solution)/shard_map/pallas_call | solution.py:679
  11.9 9.3 %all-to-all-start = ((f32[32,24,128]{2,1,0:T(8,128)}), f32[32,24,128]{2,1,0:T(8,128)S(1)}, u32[]{:S(2)}, u32[]{:S(2)}) async-start(f32[32,24,128]{2,1,0:T(8,128)} %get-tuple-element.54.after_ref), calls=%async_computation | async-start | bytes 786432 | tf_op jit(solution)/shard_map/all_to_all | solution.py:642
  27.2 4.2 %shard_map.106 = (f32[2,768,256]{2,1,0:T(8,128)S(1)}, f32[2,256,512]{2,1,0:T(8,128)}, bf16[2,2,512,256]{3,2,1,0:T(8,128)(2,1)S(1)}) custom-call(f32[32,24,128]{2,1,0:T(8,128)} %get-tuple-element.54.after_ref, f32[2,256,256]{2,1,0:T(8,128)S(1)} %bitcast.19, f32[2,512,256]{2,1,0:T(8,128)S(1)} %bitcast.17, f32[2,128,256]{2,1,0:T(8,128)S(1)} %bitcast.22, ...), custom_call_target="tpu_custom_call" | custom-call | flops 4000000000 | bytes 5000000 | tf_op jit(solution)/shard_map/pallas_call | solution.py:707
  31.5 4.1 %all-to-all-done.arrived_ref = f32[32,24,128]{2,1,0:T(8,128)S(1)} async-done(((f32[32,24,128]{2,1,0:T(8,128)}), f32[32,24,128]{2,1,0:T(8,128)S(1)}, u32[]{:S(2)}, u32[]{:S(2)}) %all-to-all-start) | async-done | bytes 393248 | tf_op jit(solution)/shard_map/all_to_all | solution.py:642
  40.9 4.6 %all-to-all-start.1 = ((f32[64,8,128]{2,1,0:T(8,128)}), f32[64,8,128]{2,1,0:T(8,128)}, u32[]{:S(2)}, u32[]{:S(2)}) async-start(f32[64,8,128]{2,1,0:T(8,128)} %get-tuple-element.65), calls=%async_computation.1 | async-start | bytes 524288 | tf_op jit(solution)/shard_map/all_to_all | solution.py:642
  59.9 2.2 shard_map.109
  62.1 20.7 %all_to_all.80.arrived_ref = f32[64,8,128]{2,1,0:T(8,128)S(1)} all-to-all(f32[64,8,128]{2,1,0:T(8,128)S(1)} %get-tuple-element.66), channel_id=1, replica_groups=mesh['layer'=8,'front'=32] {'front'}, dimensions={0} | all-to-all | bytes 524288 | tf_op jit(solution)/shard_map/all_to_all | solution.py:642
  84.2 15.0 %all_to_all.81.returned_ref = f32[64,8,128]{2,1,0:T(8,128)S(1)} all-to-all(f32[64,8,128]{2,1,0:T(8,128)S(1)} %shard_map.110), channel_id=1, replica_groups=mesh['layer'=8,'front'=32] {'front'}, dimensions={0} | all-to-all | bytes 524288 | tf_op jit(solution)/shard_map/all_to_all | solution.py:642
  100.3 3.2 collective-permute-start.7
  105.4 15.3 %all_to_all.82.arrived_ref = f32[64,8,128]{2,1,0:T(8,128)S(1)} all-to-all(f32[64,8,128]{2,1,0:T(8,128)S(1)} %get-tuple-element.69), channel_id=1, replica_groups=mesh['layer'=8,'front'=32] {'front'}, dimensions={0} | all-to-all | bytes 524288 | tf_op jit(solution)/shard_map/all_to_all | solution.py:642
  122.1 14.0 %all_to_all.83.refs_7_ = f32[64,8,128]{2,1,0:T(8,128)S(1)} all-to-all(f32[64,8,128]{2,1,0:T(8,128)S(1)} %shard_map.113), channel_id=1, replica_groups=mesh['layer'=8,'front'=32] {'front'}, dimensions={0} | all-to-all | bytes 524288 | tf_op jit(solution)/shard_map/all_to_all | solution.py:642
  137.8 13.9 %all_to_all.84.arrived_ref = f32[64,8,128]{2,1,0:T(8,128)S(1)} all-to-all(f32[64,8,128]{2,1,0:T(8,128)S(1)} %get-tuple-element.71), channel_id=1, replica_groups=mesh['layer'=8,'front'=32] {'front'}, dimensions={0} | all-to-all | bytes 524288 | tf_op jit(solution)/shard_map/all_to_all | solution.py:642
  153.0 13.9 %all_to_all.85.returned_ref = f32[64,8,128]{2,1,0:T(8,128)S(1)} all-to-all(f32[64,8,128]{2,1,0:T(8,128)S(1)} %shard_map.115), channel_id=1, replica_groups=mesh['layer'=8,'front'=32] {'front'}, dimensions={0} | all-to-all | bytes 524288 | tf_op jit(solution)/shard_map/all_to_all | solution.py:642
  169.7 13.8 %all_to_all.86.arrived_ref = f32[64,8,128]{2,1,0:T(8,128)S(1)} all-to-all(f32[64,8,128]{2,1,0:T(8,128)S(1)} %get-tuple-element.74), channel_id=1, replica_groups=mesh['layer'=8,'front'=32] {'front'}, dimensions={0} | all-to-all | bytes 524288 | tf_op jit(solution)/shard_map/all_to_all | solution.py:642
  184.8 13.7 %all_to_all.87.refs_7_ = f32[64,8,128]{2,1,0:T(8,128)S(1)} all-to-all(f32[64,8,128]{2,1,0:T(8,128)S(1)} %shard_map.118), channel_id=1, replica_groups=mesh['layer'=8,'front'=32] {'front'}, dimensions={0} | all-to-all | bytes 524288 | tf_op jit(solution)/shard_map/all_to_all | solution.py:642
  200.2 13.7 %all_to_all.88.arrived_ref = f32[64,8,128]{2,1,0:T(8,128)S(1)} all-to-all(f32[64,8,128]{2,1,0:T(8,128)S(1)} %get-tuple-element.76), channel_id=1, replica_groups=mesh['layer'=8,'front'=32] {'front'}, dimensions={0} | all-to-all | bytes 524288 | tf_op jit(solution)/shard_map/all_to_all | solution.py:642
  215.3 13.8 %all_to_all.89.returned_ref = f32[64,8,128]{2,1,0:T(8,128)S(1)} all-to-all(f32[64,8,128]{2,1,0:T(8,128)S(1)} %shard_map.120), channel_id=1, replica_groups=mesh['layer'=8,'front'=32] {'front'}, dimensions={0} | all-to-all | bytes 524288 | tf_op jit(solution)/shard_map/all_to_all | solution.py:642
  231.5 7.7 %collective-permute-done.9.trace_ref = f32[4,8,128]{2,1,0:T(8,128)S(1)} collective-permute-done((f32[4,8,128]{2,1,0:T(8,128)S(1)}, f32[4,8,128]{2,1,0:T(8,128)S(1)}, u32[]{:S(2)}, u32[]{:S(2)}) %collective-permute-start.9) | collective-permute-done | bytes 16416 | tf_op jit(solution)/shard_map/ppermute | solution.py:648
  240.3 13.5 %all_to_all.90.arrived_ref = f32[64,8,128]{2,1,0:T(8,128)S(1)} all-to-all(f32[64,8,128]{2,1,0:T(8,128)S(1)} %get-tuple-element.79), channel_id=1, replica_groups=mesh['layer'=8,'front'=32] {'front'}, dimensions={0} | all-to-all | bytes 524288 | tf_op jit(solution)/shard_map/all_to_all | solution.py:642
  255.1 15.5 %all_to_all.91.refs_7_ = f32[64,8,128]{2,1,0:T(8,128)S(1)} all-to-all(f32[64,8,128]{2,1,0:T(8,128)S(1)} %shard_map.123), channel_id=1, replica_groups=mesh['layer'=8,'front'=32] {'front'}, dimensions={0} | all-to-all | bytes 524288 | tf_op jit(solution)/shard_map/all_to_all | solution.py:642
  272.3 14.8 %all_to_all.92.arrived_ref = f32[64,8,128]{2,1,0:T(8,128)S(1)} all-to-all(f32[64,8,128]{2,1,0:T(8,128)S(1)} %get-tuple-element.81), channel_id=1, replica_groups=mesh['layer'=8,'front'=32] {'front'}, dimensions={0} | all-to-all | bytes 524288 | tf_op jit(solution)/shard_map/all_to_all | solution.py:642
  288.4 15.1 %all_to_all.93.refs_4_ = f32[64,8,128]{2,1,0:T(8,128)S(1)} all-to-all(f32[64,8,128]{2,1,0:T(8,128)S(1)} %shard_map.125), channel_id=1, replica_groups=mesh['layer'=8,'front'=32] {'front'}, dimensions={0} | all-to-all | bytes 524288 | tf_op jit(solution)/shard_map/all_to_all | solution.py:642
  305.4 20.1 %collective-permute-start.10 = (f32[2,2,16,256]{3,2,1,0:T(8,128)S(1)}, f32[2,2,16,256]{3,2,1,0:T(8,128)S(1)}, u32[]{:S(2)}, u32[]{:S(2)}) collective-permute-start(f32[2,2,16,256]{3,2,1,0:T(8,128)S(1)} %get-tuple-element.91), channel_id=1, source_target_pairs={{0,32},{32,0},{64,96},{96,64},{128,160},{160,128},{192,224},{224,1... | collective-permute-start | bytes 196616 | tf_op jit(solution)/shard_map/ppermute | solution.py:638
  (92 shorter events, 57.3 us)
Async XLA Ops:
  0.6 6.9 %copy-start.16 = (s32[1,1,16,1]{2,3,1,0:T(1,128)S(1)}, s32[1,1,16,1]{2,3,1,0:T(1,128)}, u32[]{:S(2)}) copy-start(s32[1,1,16,1]{2,3,1,0:T(1,128)} %param.16) | copy-start | bytes 196
  0.6 7.4 %copy-start.17 = (s32[1,1,16]{2,1,0:T(1,128)S(1)}, s32[1,1,16]{2,1,0:T(1,128)}, u32[]{:S(2)}) copy-start(s32[1,1,16]{2,1,0:T(1,128)} %param.17) | copy-start | bytes 196
  0.7 20.6 %collective-permute-start.4 = (f32[2,256,256]{2,1,0:T(8,128)}, f32[2,256,256]{2,1,0:T(8,128)S(1)}, u32[]{:S(2)}, u32[]{:S(2)}) collective-permute-start(f32[2,256,256]{2,1,0:T(8,128)} %bitcast.20), channel_id=1, source_target_pairs={{0,32},{32,0},{64,96},{96,64},{128,160},{160,128},{192,224},{224,1... | collective-permute-start | bytes 1572872 | tf_op jit(solution)/shard_map/ppermute | solution.py:638
  4.0 18.0 %copy-start.19 = (f32[1,1,2,256,256]{4,3,2,1,0:T(8,128)S(1)}, f32[1,1,2,256,256]{4,3,2,1,0:T(8,128)}, u32[]{:S(2)}) copy-start(f32[1,1,2,256,256]{4,3,2,1,0:T(8,128)} %param.11) | copy-start | bytes 1572868
  7.4 1.7 collective-permute-start.2
  7.6 1.3 collective-permute-start
  8.0 1.1 collective-permute-start.1
  9.2 2.7 copy-start.13
  11.9 23.6 %all-to-all-start = ((f32[32,24,128]{2,1,0:T(8,128)}), f32[32,24,128]{2,1,0:T(8,128)S(1)}, u32[]{:S(2)}, u32[]{:S(2)}) async-start(f32[32,24,128]{2,1,0:T(8,128)} %get-tuple-element.54.after_ref), calls=%async_computation | async-start | bytes 786432 | tf_op jit(solution)/shard_map/all_to_all | solution.py:642
  31.4 6.2 %copy-start.3 = (bf16[2,2,512,256]{3,2,1,0:T(8,128)(2,1)}, bf16[2,2,512,256]{3,2,1,0:T(8,128)(2,1)S(1)}, u32[]{:S(2)}) copy-start(bf16[2,2,512,256]{3,2,1,0:T(8,128)(2,1)S(1)} %get-tuple-element.55.seps_ref) | copy-start | bytes 3145732
  35.5 10.0 %copy-start.25 = (f32[2,256,128]{2,1,0:T(8,128)S(1)}, f32[2,256,128]{2,1,0:T(8,128)}, u32[]{:S(2)}) copy-start(f32[2,256,128]{2,1,0:T(8,128)} %get-tuple-element.53) | copy-start | bytes 786436
  35.5 12.7 %copy-start.12 = (f32[2,16,8,128]{3,2,1,0:T(8,128)S(1)}, f32[2,16,8,128]{3,2,1,0:T(8,128)}, u32[]{:S(2)}) copy-start(f32[2,16,8,128]{3,2,1,0:T(8,128)} %get-tuple-element.48.own_u_ref.own_u_hbm) | copy-start | bytes 393220
  37.7 10.6 %collective-permute-start.6 = (f32[2,768,256]{2,1,0:T(8,128)S(1)}, f32[2,768,256]{2,1,0:T(8,128)}, u32[]{:S(2)}, u32[]{:S(2)}) collective-permute-start(f32[2,768,256]{2,1,0:T(8,128)S(1)} %get-tuple-element.59.own_forward_hbm), channel_id=1, source_target_pairs={{0,32},{32,0},{64,96},{96,64},{128,160},{160,128},{192,224},{224,1... | collective-permute-start | bytes 4718600 | tf_op jit(solution)/shard_map/ppermute | solution.py:638
  40.9 6.4 %collective-permute-start.5 = (f32[2,256,512]{2,1,0:T(8,128)}, f32[2,256,512]{2,1,0:T(8,128)S(1)}, u32[]{:S(2)}, u32[]{:S(2)}) collective-permute-start(f32[2,256,512]{2,1,0:T(8,128)} %get-tuple-element.58.own_back_hbm), channel_id=1, source_target_pairs={{0,32},{32,0},{64,96},{96,64},{128,160},{160,128},{192,224},{224,1... | collective-permute-start | bytes 3145736 | tf_op jit(solution)/shard_map/ppermute | solution.py:638
  40.9 16.4 %all-to-all-start.1 = ((f32[64,8,128]{2,1,0:T(8,128)}), f32[64,8,128]{2,1,0:T(8,128)}, u32[]{:S(2)}, u32[]{:S(2)}) async-start(f32[64,8,128]{2,1,0:T(8,128)} %get-tuple-element.65), calls=%async_computation.1 | async-start | bytes 524288 | tf_op jit(solution)/shard_map/all_to_all | solution.py:642
  45.5 1.7 collective-permute-start.3
  48.3 1.4 copy-start.8
  57.3 1.6 copy-start.1
  59.9 23.0 %copy-start.4 = (bf16[2,2,512,256]{3,2,1,0:T(8,128)(2,1)S(1)}, bf16[2,2,512,256]{3,2,1,0:T(8,128)(2,1)}, u32[]{:S(2)}) copy-start(bf16[2,2,512,256]{3,2,1,0:T(8,128)(2,1)} %copy-done.3) | copy-start | bytes 3145732
  62.1 37.1 %copy-start.2 = (bf16[2,2,512,512]{3,2,1,0:T(8,128)(2,1)S(1)}, bf16[2,2,512,512]{3,2,1,0:T(8,128)(2,1)}, u32[]{:S(2)}) copy-start(bf16[2,2,512,512]{3,2,1,0:T(8,128)(2,1)} %copy-done) | copy-start | bytes 6291460
  100.3 4.1 %collective-permute-start.7 = (f32[4,8,128]{2,1,0:T(8,128)S(1)}, f32[4,8,128]{2,1,0:T(8,128)S(1)}, u32[]{:S(2)}, u32[]{:S(2)}) collective-permute-start(f32[4,8,128]{2,1,0:T(8,128)S(1)} %get-tuple-element.68), channel_id=1, source_target_pairs={{0,64},{32,96},{192,128},{224,160},{1,65},{33,97},{193,129},{225,1... | collective-permute-start | bytes 49160 | tf_op jit(solution)/shard_map/ppermute | solution.py:648
  168.0 0.7 collective-permute-start.8
  230.2 9.0 %collective-permute-start.9 = (f32[4,8,128]{2,1,0:T(8,128)S(1)}, f32[4,8,128]{2,1,0:T(8,128)S(1)}, u32[]{:S(2)}, u32[]{:S(2)}) collective-permute-start(f32[4,8,128]{2,1,0:T(8,128)S(1)} %get-tuple-element.78), channel_id=1, source_target_pairs={{128,192},{160,224},{64,0},{96,32},{129,193},{161,225},{65,1},{97,... | collective-permute-start | bytes 49160 | tf_op jit(solution)/shard_map/ppermute | solution.py:648
  305.4 21.0 %collective-permute-start.10 = (f32[2,2,16,256]{3,2,1,0:T(8,128)S(1)}, f32[2,2,16,256]{3,2,1,0:T(8,128)S(1)}, u32[]{:S(2)}, u32[]{:S(2)}) collective-permute-start(f32[2,2,16,256]{3,2,1,0:T(8,128)S(1)} %get-tuple-element.91), channel_id=1, source_target_pairs={{0,32},{32,0},{64,96},{96,64},{128,160},{160,128},{192,224},{224,1... | collective-permute-start | bytes 196616 | tf_op jit(solution)/shard_map/ppermute | solution.py:638
  (15 other events, 15.4 us)
